TPU v7x, 32 devices: a whole 2x2x4 slice. The times are simulated.
32 devices in a mesh: row: 4 (over y, x), col: 8 (over z, core).
Axes of the slice: x: 2, y: 2, z: 4, core: 2. Of those that a mesh axis runs over, the one named last changes fastest.
Arguments:
- features: bfloat16 [8, 512, 768], P(None, 'row', 'col'), may hold values from -6 to 6
- lengthscale: float32 [768], replicated, may hold values from 8 to 200
- noise: float32 [8, 512], P(None, 'row'), may hold values from 0.05 to 0.5
Outputs:
- panel: float32 [8, 512, 128], P(None, 'row')
- trailing: float32 [8, 512, 4, 1024], P(None, 'row', None, 'col')
All inputs are finite; a program needn't handle non-finite values.
Results may differ from a plain program's by a relative error of at most 0.005.
Values may be sent and summed in bfloat16 or wider, within the bound.
No kernel may reach another device: no remote copies, remote signals or barrier semaphores. Data moves between devices by JAX's collectives and lax.ppermute only.
A program may use at most 64 MiB of HBM per device.

v0:
```python
import jax
import jax.numpy as jnp
from jax import lax
from jax.sharding import PartitionSpec as P


def from_root(block, axis, holder):
    block = jnp.where(lax.axis_index(axis) == holder, block, jnp.zeros_like(block))
    return lax.psum(block, axis)


def kernel_block(left, left_sq, right, right_sq):
    gram = jnp.dot(left, right.T, precision=lax.Precision.HIGHEST)
    return jnp.exp(-0.5 * (left_sq[:, None] + right_sq[None, :] - 2.0 * gram))


def body(features, lengthscale, noise):
    rows_axis = lax.axis_size("row")
    cols_axis = lax.axis_size("col")
    row_id = lax.axis_index("row")
    col_id = lax.axis_index("col")
    tiles_row = features.shape[0]
    width = features.shape[1]
    stride = cols_axis // rows_axis
    tiles_col = tiles_row // stride
    row_feats = lax.all_gather(features, "col", axis=2, tiled=True)
    depth = row_feats.shape[2]
    grouped = row_feats.reshape(tiles_col, stride, width, depth)
    picked = lax.dynamic_index_in_dim(grouped, col_id // rows_axis, 1, keepdims=False)
    col_feats = from_root(picked, "row", col_id % rows_axis)
    inverse = 1.0 / lengthscale
    left = row_feats.reshape(tiles_row * width, depth).astype(jnp.float32) * inverse[None, :]
    right = col_feats.reshape(tiles_col * width, depth).astype(jnp.float32) * inverse[None, :]
    left_sq = jnp.sum(left * left, axis=1)
    right_sq = jnp.sum(right * right, axis=1)
    inner = jnp.arange(width, dtype=jnp.int32)
    row_index = (
        (jnp.arange(tiles_row, dtype=jnp.int32)[:, None] * rows_axis + row_id) * width
        + inner[None, :]
    ).reshape(-1)
    col_index = (
        (jnp.arange(tiles_col, dtype=jnp.int32)[:, None] * cols_axis + col_id) * width
        + inner[None, :]
    ).reshape(-1)
    noise_rows = noise.reshape(-1)
    kern = kernel_block(left, left_sq, right, right_sq)
    kern = kern + jnp.where(row_index[:, None] == col_index[None, :], noise_rows[:, None], 0.0)
    diag_tile = from_root(kern[:width, :width], "row", 0)
    factor = jnp.linalg.cholesky(diag_tile)
    own_rows = jax.scipy.linalg.solve_triangular(factor, kern[:, :width].T, lower=True).T
    panel_rows = from_root(own_rows, "col", 0)
    panel_grouped = panel_rows.reshape(tiles_col, stride, width, width)
    panel_pick = lax.dynamic_index_in_dim(panel_grouped, col_id // rows_axis, 1, keepdims=False)
    panel_cols = from_root(panel_pick, "row", col_id % rows_axis).reshape(tiles_col * width, width)
    trailing = kern - jnp.dot(panel_rows, panel_cols.T, precision=lax.Precision.HIGHEST)
    return (
        panel_rows.reshape(tiles_row, width, width),
        trailing.reshape(tiles_row, width, tiles_col, width),
    )


def solution(mesh):
    placed = (P(None, "row", "col"), P(), P(None, "row"))
    return jax.shard_map(
        body,
        mesh=mesh,
        in_specs=placed,
        out_specs=(P(None, "row", None), P(None, "row", None, "col")),
        check_vma=False,
    )
```

profile of v0, /device:TPU:0, one launch (start us, length us, event | category | flops | bytes accessed | tf_op | source)
XLA Modules:
  0.0 281.7 jit_solution(10318070649635550357)
XLA Ops:
  7.2 1.7 copy.12
  9.1 28.9 %all-gather.2.cloned.1.call-done = bf16[8,128,768]{1,0,2:T(8,128)(2,1)} async-done(((bf16[8,128,96]{1,0,2:T(8,128)(2,1)}), bf16[8,128,768]{1,0,2:T(8,128)(2,1)}) %all-gather.2.cloned.1.call-update) | async-done | bytes 1572880 | tf_op jit(solution)/shard_map/all_gather | solution.py:26
  38.0 2.1 copy.13
  40.1 0.9 select_bitcast_fusion
  41.2 2.1 multiply_reduce_fusion
  43.3 46.6 %all-reduce.5.cloned.1.call-done = bf16[4,128,768]{2,1,0:T(8,128)(2,1)} async-done(((bf16[4,128,768]{2,1,0:T(8,128)(2,1)}), bf16[4,128,768]{2,1,0:T(8,128)(2,1)}) %all-reduce.5.cloned.1.call-update) | async-done | bytes 786448 | tf_op jit(solution)/shard_map/psum | solution.py:9
  89.9 1.4 multiply_reduce_fusion.1
  91.3 7.4 %select_add_fusion = f32[1024,512]{1,0:T(8,128)S(1)} fusion(f32[1024,768]{1,0:T(8,128)} %bitcast.31, f32[512,768]{1,0:T(8,128)S(1)} %bitcast.32, f32[1024]{0:T(1024)S(1)} %bitcast.36, s32[512]{0:T(512)S(1)} %add_bitcast_fusion.1, f32[512]{0:T(512)S(1)} %bitcast.35, f32[1024]{0:T(1024)S(1)} %bitcast.34, s32[1024]{0:T(1024)S(1)} %add_bitcast_fusion), kind=kOutput, calls=%fused_computation.2 | convolution fusion | flops 4835508224 | bytes 6832128 | tf_op jit(solution)/shard_map/dot_general | solution.py:13
  98.8 0.7 slice_select_fusion
  99.5 0.2 all-reduce.9.cloned.1.call-start
  99.7 41.4 %all-reduce.7.cloned.1.call-done = f32[128,128]{1,0:T(8,128)} async-done(((f32[128,128]{1,0:T(8,128)}), f32[128,128]{1,0:T(8,128)}) %all-reduce.7.cloned.1.call-update) | async-done | bytes 65552 | tf_op jit(solution)/shard_map/psum | solution.py:9
  141.1 0.9 copy.15
  142.1 0.9 fusion.3
  142.9 11.7 %cholesky.15 = f32[128,128]{1,0:T(8,128)S(1)} custom-call(f32[128,128]{1,0:T(8,128)S(1)} %fusion.3), custom_call_target="Cholesky" | custom-call | tf_op jit(solution)/shard_map/jit(cholesky)/cholesky | solution.py:49
  154.7 0.6 compare_reduce_fusion
  155.3 0.7 fusion.1
  156.0 9.8 %custom-call.7 = f32[1,128,128]{1,2,0:T(8,128)S(1)} custom-call(f32[1,128,128]{2,1,0:T(8,128)S(1)} %fusion.1), custom_call_target="InvertDiagBlocksLowerTriangular" | custom-call | tf_op jit(solution)/shard_map/jit(_solve_triangular)/triangular_solve | solution.py:50
  165.8 1.4 convolution_select_fusion
  167.2 56.3 %all-reduce.9.cloned.1.call-done = f32[1024,128]{1,0:T(8,128)} async-done(((f32[1024,128]{1,0:T(8,128)}), f32[1024,128]{1,0:T(8,128)}) %all-reduce.9.cloned.1.call-update) | async-done | bytes 524304 | tf_op jit(solution)/shard_map/psum | solution.py:9
  223.5 1.7 dynamic-slice_select_fusion
  225.2 43.8 %all-reduce.11.cloned.1.call-done = f32[512,128]{1,0:T(8,128)} async-done(((f32[512,128]{1,0:T(8,128)}), f32[512,128]{1,0:T(8,128)}) %all-reduce.11.cloned.1.call-update) | async-done | bytes 262160 | tf_op jit(solution)/shard_map/psum | solution.py:9
  269.0 3.6 %convolution_subtract_fusion = f32[1024,512]{1,0:T(8,128)S(1)} fusion(f32[1024,512]{1,0:T(8,128)} %copy-done, f32[1024,128]{1,0:T(8,128)} %all-reduce.9.cloned.1.call-done, f32[512,128]{1,0:T(8,128)} %all-reduce.11.cloned.1.call-done), kind=kOutput, calls=%fused_computation.3 | convolution fusion | flops 805830656 | bytes 4980736 | tf_op jit(solution)/shard_map/dot_general | solution.py:55
  272.7 1.7 reshape.114
  274.4 0.8 copy.20
  (23 shorter events, 0.5 us)
Async XLA Ops:
  7.2 30.8 %all-gather.2.cloned.1.call-start = ((), (), s32[]{:S(2)}) async-start(), calls=%async_computation | async-start | bytes 1769472 | tf_op jit(solution)/shard_map/all_gather | solution.py:26
  8.9 81.0 %all-reduce.5.cloned.1.call-start = ((), (), s32[]{:S(2)}) async-start(), calls=%async_computation.1 | async-start | bytes 1572864 | tf_op jit(solution)/shard_map/psum | solution.py:9
  9.1 32.1 %copy-start.2 = (f32[768]{0:T(1024)S(1)}, f32[768]{0:T(1024)}, u32[]{:S(2)}) copy-start(f32[768]{0:T(1024)} %param.4) | copy-start | bytes 9220
  41.1 100.0 %all-reduce.7.cloned.1.call-start = ((), (), s32[]{:S(2)}) async-start(), calls=%async_computation.2 | async-start | bytes 131072 | tf_op jit(solution)/shard_map/psum | solution.py:9
  43.3 48.1 %copy-start.3 = (f32[8,128]{1,0:T(8,128)S(1)}, f32[8,128]{1,0:T(8,128)}, u32[]{:S(2)}) copy-start(f32[8,128]{1,0:T(8,128)} %param.5) | copy-start | bytes 12292
  98.8 126.4 %copy-start = (f32[1024,512]{1,0:T(8,128)}, f32[1024,512]{1,0:T(8,128)S(1)}, u32[]{:S(2)}) copy-start(f32[1024,512]{1,0:T(8,128)S(1)} %select_add_fusion) | copy-start | bytes 6291460
  99.5 124.0 %all-reduce.9.cloned.1.call-start = ((), (), s32[]{:S(2)}) async-start(), calls=%async_computation.3 | async-start | bytes 1048576 | tf_op jit(solution)/shard_map/psum | solution.py:9
  167.2 101.8 %all-reduce.11.cloned.1.call-start = ((), (), s32[]{:S(2)}) async-start(), calls=%async_computation.4 | async-start | bytes 524288 | tf_op jit(solution)/shard_map/psum | solution.py:9
  272.7 1.7 copy-start.1
Sparse Core Ops, SparseCore 0:
  10.2 27.7 all-gather.1
  41.6 48.2 all-reduce.4
  99.6 41.4 all-reduce.6
  167.3 56.1 all-reduce.8
  227.1 41.8 all-reduce.10
where the time goes:
time: 282 us
  waiting for transfers between devices  217 us (77%)
  other arithmetic  30.7 us (11%)
  between operations  13.9 us (5%)
  matrix products  12.4 us (4%)
  local copies, waits for them, and re-layouts  7.25 us (3%)
    psum x4, waiting for transfers between devices, from_root(): return lax.psum(block, axis)  188 us
    all_gather x1, waiting for transfers between devices, body(): row_feats = lax.all_gather(features, 'col', axis=2, tiled=True)  28.9 us
    another operation x3, other arithmetic, body(): factor = jnp.linalg.cholesky(diag_tile)  12.4 us
    another operation x2, other arithmetic, body(): jax.scipy.linalg.solve_triangular(factor, kern[:, :width].T, lower=True)  10.5 us
    dot_general x1, matrix products, kernel_block(): gram = jnp.dot(left, right.T, precision=lax.Precision.HIGHEST)  7.41 us
  transfers between devices with their start and end apart: 5, of which 5 were waited for; matrix products, arithmetic and copies ran while one was open for 1% of the time, Pallas kernels for 0%

commit v1 on v0

--- a/solution.py
+++ b/solution.py
@@ -1,7 +1,303 @@
+import functools
+
 import jax
 import jax.numpy as jnp
 from jax import lax
+from jax.experimental import pallas as pl
+from jax.experimental.pallas import tpu as pltpu
 from jax.sharding import PartitionSpec as P
+
+LANES = 128
+VM = pl.BlockSpec(memory_space=pltpu.VMEM)
+SM = pl.BlockSpec(memory_space=pltpu.SMEM)
+
+
+def nt(a, b, precision=None):
+    return lax.dot_general(
+        a, b, (((1,), (1,)), ((), ())), precision=precision, preferred_element_type=jnp.float32
+    )
+
+
+def split2(x):
+    hi = x.astype(jnp.bfloat16)
+    return hi, (x - hi.astype(jnp.float32)).astype(jnp.bfloat16)
+
+
+def split3(x):
+    hi, mid = split2(x)
+    rest = x - hi.astype(jnp.float32) - mid.astype(jnp.float32)
+    return hi, mid, rest.astype(jnp.bfloat16)
+
+
+def pack_kernel(parity_ref, feat_ref, noise_ref, own_ref, oth_ref, first_ref, pad):
+    width, depth = feat_ref.shape[1], feat_ref.shape[2]
+    rest = LANES - depth
+    pad[...] = jnp.zeros_like(pad)
+    lane = lax.broadcasted_iota(jnp.int32, (width, LANES), 1)
+    pad[:, 0:depth] = feat_ref[0].astype(jnp.float32)
+    first_ref[0:width, :] = pad[...].astype(jnp.bfloat16)
+    hi, mid, low = split3(noise_ref[0:1, :])
+    row = lax.broadcasted_iota(jnp.int32, (16, LANES), 0)
+    parts = jnp.where(row == 0, hi.astype(jnp.float32), 0.0)
+    parts = jnp.where(row == 1, mid.astype(jnp.float32), parts)
+    parts = jnp.where(row == 2, low.astype(jnp.float32), parts)
+    first_ref[width : width + 16, :] = parts.astype(jnp.bfloat16)
+    for out_ref, parity in ((own_ref, parity_ref[0]), (oth_ref, 1 - parity_ref[0])):
+        pad[:, 0:depth] = feat_ref[6 + parity].astype(jnp.float32)
+        last = pad[...]
+        for k in range(3):
+            pad[:, 0:depth] = feat_ref[2 * k + parity].astype(jnp.float32)
+            moved = pltpu.roll(last, depth - rest * k, 1)
+            out_ref[k * width : (k + 1) * width, :] = jnp.where(
+                lane < depth, pad[...], moved
+            ).astype(jnp.bfloat16)
+
+
+def pack(parity, features, noise):
+    width = features.shape[1]
+    half = jax.ShapeDtypeStruct((3 * width, LANES), jnp.bfloat16)
+    return pl.pallas_call(
+        pack_kernel,
+        out_shape=(half, half, jax.ShapeDtypeStruct((width + 16, LANES), jnp.bfloat16)),
+        in_specs=[SM, VM, VM],
+        out_specs=(VM, VM, VM),
+        scratch_shapes=[pltpu.VMEM((width, LANES), jnp.float32)],
+        name="pack",
+    )(parity, features, noise)
+
+
+def bcast(v):
+    return jnp.broadcast_to(v, (8, LANES))
+
+
+def inverse_factor(tiles, rows, lanes, m=8):
+    size = 8 * len(tiles)
+    tiles, out = list(tiles), [None] * len(tiles)
+    for k in range(0, size, m):
+        b, j = divmod(k, 8)
+        r = [bcast(tiles[b][j + i : j + i + 1, :]) for i in range(m)]
+        s = [[bcast(r[i][:, k + l : k + l + 1]) if l >= i else None for l in range(m)] for i in range(m)]
+        r = [r[i] + jnp.where(lanes == k + i, 1.0, 0.0) for i in range(m)]
+        inv, f = [], [[None] * m for _ in range(m)]
+        for p in range(m):
+            inv.append(1.0 / s[p][p])
+            for i in range(p + 1, m):
+                f[p][i] = s[p][i] * inv[p]
+            for i in range(p + 1, m):
+                for l in range(i, m):
+                    s[i][l] = s[i][l] - f[p][i] * s[p][l]
+            for i in range(p + 1, m):
+                r[i] = r[i] - f[p][i] * r[p]
+        for i in range(m):
+            w = jnp.where(lanes < k + i, r[i], jnp.where(lanes == k + i, 1.0, 0.0)) * lax.rsqrt(s[i][i])
+            out[b] = w if out[b] is None else jnp.where(rows == j + i, w, out[b])
+        if k + m >= size:
+            break
+        y = [r[i] * inv[i] for i in range(m)]
+        for i in range(m - 1, -1, -1):
+            for l in range(i + 1, m):
+                y[i] = y[i] - f[i][l] * y[l]
+        for i in range(b, len(tiles)):
+            if i == b and j + m >= 8:
+                continue
+            acc = None
+            for q in range(m):
+                c = bcast(tiles[i][:, k + q : k + q + 1])
+                if i == b:
+                    c = jnp.where(rows > j + m - 1, c, 0.0)
+                acc = c * y[q] if acc is None else acc + c * y[q]
+            tiles[i] = tiles[i] - acc
+    return out
+
+
+def first_kernel(weight_ref, *refs):
+    pieces, (out_ref, work) = refs[:-2], refs[-2:]
+    width = out_ref.shape[0]
+    x = jnp.concatenate([piece[0:width, :] for piece in pieces], axis=1)
+    w = jnp.concatenate([weight_ref[s : s + 1, :] for s in range(len(pieces))], axis=1)
+    xf = x.astype(jnp.float32)
+    xw = xf * w
+    gram = sum(nt(x, part) for part in split3(xw))
+    partial = jnp.zeros((width, LANES), jnp.float32)
+    for s in range(len(pieces)):
+        cut = slice(s * LANES, (s + 1) * LANES)
+        partial = partial + xf[:, cut] * xw[:, cut]
+    sq_col = jnp.sum(partial, axis=1, keepdims=True)
+    sq_row = jnp.sum(partial.T, axis=0, keepdims=True)
+    tail = pieces[0][width : width + 16, :].astype(jnp.float32)
+    noise = tail[0:1, :] + tail[1:2, :] + tail[2:3, :]
+    i = lax.broadcasted_iota(jnp.int32, (width, width), 0)
+    j = lax.broadcasted_iota(jnp.int32, (width, width), 1)
+    work[...] = jnp.exp(-0.5 * (sq_col + sq_row - 2.0 * gram)) + jnp.where(i == j, noise, 0.0)
+    rows = lax.broadcasted_iota(jnp.int32, (8, LANES), 0)
+    lanes = lax.broadcasted_iota(jnp.int32, (8, LANES), 1)
+    tiles = [work[8 * t : 8 * t + 8, :] for t in range(width // 8)]
+    for t, tile in enumerate(inverse_factor(tiles, rows, lanes)):
+        out_ref[8 * t : 8 * t + 8, :] = tile
+
+
+def first_tile(weight, pieces):
+    width = pieces[0].shape[0] - 16
+    return pl.pallas_call(
+        first_kernel,
+        out_shape=jax.ShapeDtypeStruct((width, width), jnp.float32),
+        in_specs=[VM] * (1 + len(pieces)),
+        out_specs=VM,
+        scratch_shapes=[pltpu.VMEM((width, width), jnp.float32)],
+        name="first_tile",
+    )(weight, *pieces)
+
+
+def unpack(blocks, depth):
+    rest = LANES - depth
+    lane = lax.broadcasted_iota(jnp.int32, blocks[0].shape, 1)
+    tile = jnp.zeros(blocks[0].shape, jnp.float32)
+    for k, block in enumerate(blocks):
+        moved = pltpu.roll(block.astype(jnp.float32), LANES - depth + rest * k, 1)
+        tile = jnp.where((lane >= rest * k) & (lane < rest * (k + 1)), moved, tile)
+    return tile.astype(jnp.bfloat16)
+
+
+def rest_kernel(depth, where_ref, weight_ref, noise_ref, inv_ref, *refs):
+    n = 8
+    firsts, refs = refs[:n], refs[n:]
+    row_own, row_oth, cols = refs[:n], refs[n : 2 * n], refs[2 * n : 3 * n]
+    panel_ref, trail_ref = refs[3 * n :]
+    width = inv_ref.shape[0]
+    parity, row_id, col_id, diag = where_ref[0], where_ref[1], where_ref[2], where_ref[3]
+    highest = lax.Precision.HIGHEST
+
+    def tile_of(refs_, t):
+        parts = []
+        for ref in refs_:
+            if t < 3:
+                parts.append(ref[t * width : (t + 1) * width, :])
+            else:
+                parts.append(unpack([ref[k * width : (k + 1) * width, :] for k in range(3)], depth))
+        return jnp.concatenate(parts, axis=1)
+
+    w = jnp.concatenate([weight_ref[s : s + 1, :] for s in range(n)], axis=1)
+
+    def squares(xf, xw):
+        partial = xf[:, 0:LANES] * xw[:, 0:LANES]
+        for s in range(1, n):
+            cut = slice(s * LANES, (s + 1) * LANES)
+            partial = partial + xf[:, cut] * xw[:, cut]
+        return partial
+
+    def col_sum(partial):
+        return jnp.sum(partial, axis=1, keepdims=True)
+
+    def row_sum(partial):
+        return jnp.sum(partial.T, axis=0, keepdims=True)
+
+    eye = lax.broadcasted_iota(jnp.int32, (width, width), 0) == lax.broadcasted_iota(
+        jnp.int32, (width, width), 1
+    )
+    tail = firsts[0][width : width + 16, :].astype(jnp.float32)
+    noise0 = tail[0:1, :] + tail[1:2, :] + tail[2:3, :]
+    diag0 = jnp.where(eye, noise0, 0.0)
+    inv = inv_ref[...]
+
+    a = jnp.concatenate([f[0:width, :] for f in firsts], axis=1)
+    af = a.astype(jnp.float32)
+    aw = af * w
+    a_hi, a_lo = split2(aw)
+    sq0 = row_sum(squares(af, aw))
+
+    def panel_of(x, sq, first):
+        gram = nt(x, a_hi) + nt(x, a_lo)
+        kern = jnp.exp(-0.5 * (sq + sq0 - 2.0 * gram))
+        kern = kern + jnp.where(first, diag0, 0.0)
+        return nt(kern, inv, highest)
+
+    c_hi, c_lo, c_sq, c_panel = [], [], [], []
+    for t in range(4):
+        c = tile_of(cols, t)
+        cf = c.astype(jnp.float32)
+        cw = cf * w
+        partial = squares(cf, cw)
+        hi, lo = split2(cw)
+        c_hi.append(hi)
+        c_lo.append(lo)
+        c_sq.append(row_sum(partial))
+        c_panel.append(panel_of(c, col_sum(partial), (col_id == 0) & (t == 0)))
+    c_hi, c_lo = jnp.concatenate(c_hi, axis=0), jnp.concatenate(c_lo, axis=0)
+    c_sq, c_panel = jnp.concatenate(c_sq, axis=1), jnp.concatenate(c_panel, axis=0)
+
+    for t in range(4):
+        for half, refs_ in enumerate((row_own, row_oth)):
+            par = parity if half == 0 else 1 - parity
+            tile = 2 * t + par
+            x = tile_of(refs_, t)
+            xf = x.astype(jnp.float32)
+            sq = col_sum(squares(xf, xf * w))
+            panel = panel_of(x, sq, (row_id == 0) & (tile == 0))
+            panel_ref[tile] = panel
+            gram = nt(x, c_hi) + nt(x, c_lo)
+            kern = jnp.exp(-0.5 * (sq + c_sq - 2.0 * gram))
+            trail = kern - nt(panel, c_panel, highest)
+            for tc in range(4):
+                block = trail[:, tc * width : (tc + 1) * width]
+                if half == 0 and tc == t:
+                    block = block + jnp.where(eye & (diag == 1), noise_ref[pl.ds(tile, 1), :], 0.0)
+                trail_ref[pl.ds(tile * (4 * width) + tc, width, stride=4), :] = block
+
+
+def rest(depth, where, weight, noise, inv, firsts, row_own, row_oth, cols):
+    tiles, width = noise.shape
+    return pl.pallas_call(
+        functools.partial(rest_kernel, depth),
+        out_shape=(
+            jax.ShapeDtypeStruct((tiles, width, width), jnp.float32),
+            jax.ShapeDtypeStruct((tiles * width * 4, width), jnp.float32),
+        ),
+        in_specs=[SM] + [VM] * (3 + 4 * 8),
+        out_specs=(VM, VM),
+        compiler_params=pltpu.CompilerParams(vmem_limit_bytes=48 * 1024 * 1024),
+        name="rest",
+    )(where, weight, noise, inv, *firsts, *row_own, *row_oth, *cols)
+
+
+def body(features, lengthscale, noise):
+    tiles, width, depth = features.shape
+    row_id = lax.axis_index("row")
+    col_id = lax.axis_index("col")
+    n_rows, n_cols = lax.axis_size("row"), lax.axis_size("col")
+    home = col_id % n_rows
+    parity = col_id // n_rows
+
+    def over_row(x, k):
+        return lax.ppermute(x, "row", [(i, i ^ k) for i in range(n_rows)])
+
+    def over_col(x, k):
+        return lax.ppermute(x, "col", [(i, i ^ k) for i in range(n_cols)])
+
+    own, oth, first = pack(parity.astype(jnp.int32).reshape(1), features, noise)
+    firsts = [first] + [over_row(first, k) for k in (1, 2, 3)]
+    first = lax.select_n(row_id, *firsts)
+    mine = [first] + [over_col(first, 2 * k) for k in (1, 2, 3)]
+    theirs = over_col(jnp.stack(mine), 1)
+    firsts = mine + [theirs[k] for k in range(4)]
+    order = col_id ^ jnp.array([0, 2, 4, 6, 1, 3, 5, 7], jnp.int32)
+    inverse = 1.0 / lengthscale
+    weight = jnp.pad((inverse * inverse).reshape(n_cols, depth), ((0, 0), (0, LANES - depth)))
+    weight = jnp.take(weight, order, axis=0)
+    inv = first_tile(weight, firsts)
+    p = [own, over_col(own, 2), over_col(oth, 4), over_col(oth, 6)]
+    q = [oth, over_col(oth, 2), over_col(own, 4), over_col(own, 6)]
+    p_all, q_all = jnp.stack(p), jnp.stack(q)
+    p_sib, q_sib = over_col(p_all, 1), over_col(q_all, 1)
+    row_own = p + [p_sib[k] for k in range(4)]
+    row_oth = q + [q_sib[k] for k in range(4)]
+    near = [p_all] + [over_row(p_all, k) for k in (1, 2, 3)]
+    keep = lax.select_n(row_id ^ home, *near)
+    give = lax.select_n(row_id ^ home ^ 1, *near)
+    give = over_col(give, 1)
+    cols = [keep[k] for k in range(4)] + [give[k] for k in range(4)]
+    where = jnp.stack([parity, row_id, col_id, (row_id == home).astype(jnp.int32)]).astype(jnp.int32)
+    panel, trailing = rest(depth, where, weight, noise, inv, firsts, row_own, row_oth, cols)
+    return panel, trailing.reshape(tiles, width, 4, width)
 
 
 def from_root(block, axis, holder):
@@ -9,12 +305,7 @@
     return lax.psum(block, axis)
 
 
-def kernel_block(left, left_sq, right, right_sq):
-    gram = jnp.dot(left, right.T, precision=lax.Precision.HIGHEST)
-    return jnp.exp(-0.5 * (left_sq[:, None] + right_sq[None, :] - 2.0 * gram))
-
-
-def body(features, lengthscale, noise):
+def general_body(features, lengthscale, noise):
     rows_axis = lax.axis_size("row")
     cols_axis = lax.axis_size("col")
     row_id = lax.axis_index("row")
@@ -35,16 +326,14 @@
     right_sq = jnp.sum(right * right, axis=1)
     inner = jnp.arange(width, dtype=jnp.int32)
     row_index = (
-        (jnp.arange(tiles_row, dtype=jnp.int32)[:, None] * rows_axis + row_id) * width
-        + inner[None, :]
+        (jnp.arange(tiles_row, dtype=jnp.int32)[:, None] * rows_axis + row_id) * width + inner[None, :]
     ).reshape(-1)
     col_index = (
-        (jnp.arange(tiles_col, dtype=jnp.int32)[:, None] * cols_axis + col_id) * width
-        + inner[None, :]
+        (jnp.arange(tiles_col, dtype=jnp.int32)[:, None] * cols_axis + col_id) * width + inner[None, :]
     ).reshape(-1)
-    noise_rows = noise.reshape(-1)
-    kern = kernel_block(left, left_sq, right, right_sq)
-    kern = kern + jnp.where(row_index[:, None] == col_index[None, :], noise_rows[:, None], 0.0)
+    gram = jnp.dot(left, right.T, precision=lax.Precision.HIGHEST)
+    kern = jnp.exp(-0.5 * (left_sq[:, None] + right_sq[None, :] - 2.0 * gram))
+    kern = kern + jnp.where(row_index[:, None] == col_index[None, :], noise.reshape(-1)[:, None], 0.0)
     diag_tile = from_root(kern[:width, :width], "row", 0)
     factor = jnp.linalg.cholesky(diag_tile)
     own_rows = jax.scipy.linalg.solve_triangular(factor, kern[:, :width].T, lower=True).T
@@ -61,8 +350,9 @@
 
 def solution(mesh):
     placed = (P(None, "row", "col"), P(), P(None, "row"))
+    small = mesh.shape["row"] == 4 and mesh.shape["col"] == 8
     return jax.shard_map(
-        body,
+        body if small else general_body,
         mesh=mesh,
         in_specs=placed,
         out_specs=(P(None, "row", None), P(None, "row", None, "col")),

time: 282 us -> 73.8 us (0.26)
  waiting for transfers between devices: 217 us -> 13.3 us
  Pallas kernels: 0 us -> 25.9 us
  other arithmetic: 30.7 us -> 5.69 us
  starting transfers between devices: 0.39 us -> 24.3 us
  between operations: 13.9 us -> 0.98 us
  matrix products: 12.4 us -> 0 us
  local copies, waits for them, and re-layouts: 7.25 us -> 3.26 us
    psum x4 -> x0, waiting for transfers between devices: 188 us -> none  [from_root(): return lax.psum(block, axis)]
    all_gather x1 -> x0, waiting for transfers between devices: 28.9 us -> none  [body(): row_feats = lax.all_gather(features, 'col', axis=2, tiled=True)]
    pallas_call x0 -> x3, Pallas kernels: none -> 25.9 us  [the longest x1 16.3 us: rest(): pl.pallas_call(functools.partial(rest_kernel, depth), out_shape=(jax.Shap...]
    ppermute x0 -> x19, starting transfers between devices: none -> 24.3 us  [the longest x13 16.2 us: over_col(): return lax.ppermute(x, 'col', [(i, i ^ k) for i in range(n_cols)])]
    another operation x5 -> x4, other arithmetic: 22.9 us -> 2.73 us  [the longest x2 2.63 us: body(): p_all, q_all = (jnp.stack(p), jnp.stack(q))]
    ppermute x0 -> x19, waiting for transfers between devices: none -> 13.3 us  [the longest x13 8.02 us: over_col(): return lax.ppermute(x, 'col', [(i, i ^ k) for i in range(n_cols)])]
    dot_general x2 -> x0, matrix products: 11 us -> none  [the longest x1 7.41 us: kernel_block(): gram = jnp.dot(left, right.T, precision=lax.Precision.HIGHEST)]
    reduce_sum x2 -> x0, other arithmetic: 3.48 us -> none  [the longest x1 2.07 us: body(): left_sq = jnp.sum(left * left, axis=1)]
  transfers between devices with their start and end apart: 5 -> 19, of which waited for: 5 -> 8; matrix products, arithmetic and copies ran while one was open for 1% -> 10% of each run, Pallas kernels for 0% -> 11%
where the time goes in v1:
time: 73.8 us; the launch traced here: 73.4 us
  Pallas kernels  25.9 us (35%)
  starting transfers between devices  24.3 us (33%)
  waiting for transfers between devices  13.3 us (18%)
  other arithmetic  5.69 us (8%)
  local copies, waits for them, and re-layouts  3.26 us (4%)
  between operations  0.98 us (1%)
    pallas_call x1, Pallas kernels, rest(): pl.pallas_call(functools.partial(rest_kernel, depth), out_shape=(jax.Shap...  16.3 us
    ppermute x13, starting transfers between devices, over_col(): return lax.ppermute(x, 'col', [(i, i ^ k) for i in range(n_cols)])  16.2 us
    ppermute x6, starting transfers between devices, over_row(): return lax.ppermute(x, 'row', [(i, i ^ k) for i in range(n_rows)])  8.06 us
    ppermute x13, waiting for transfers between devices, over_col(): return lax.ppermute(x, 'col', [(i, i ^ k) for i in range(n_cols)])  8.02 us
    pallas_call x1, Pallas kernels, first_tile(): pl.pallas_call(first_kernel, out_shape=jax.ShapeDtypeStruct((width, width...  7.88 us
    ppermute x6, waiting for transfers between devices, over_row(): return lax.ppermute(x, 'row', [(i, i ^ k) for i in range(n_rows)])  5.28 us
    another operation x2, other arithmetic, body(): p_all, q_all = (jnp.stack(p), jnp.stack(q))  2.63 us
    unnamed x35, local copies, waits for them, and re-layouts  1.84 us
  transfers between devices with their start and end apart: 19, of which 8 were waited for; matrix products, arithmetic and copies ran while one was open for 10% of the time, Pallas kernels for 11%

profile of v1, /device:TPU:0, one launch (start us, length us, event | category | flops | bytes accessed | tf_op | source)
XLA Modules:
  0.0 73.4 jit_solution(18264180914299730918)
XLA Ops:
  0.6 1.8 %copy.6.feat_ref = bf16[8,128,96]{2,1,0:T(8,128)(2,1)} copy(bf16[8,128,96]{1,2,0:T(8,128)(2,1)} %param.4) | data formatting | bytes 393216 | tf_op args[0]
  2.4 1.8 %pack.1 = (bf16[384,128]{1,0:T(8,128)(2,1)}, bf16[384,128]{1,0:T(8,128)(2,1)}, bf16[144,128]{1,0:T(8,128)(2,1)}) custom-call(s32[1]{0:T(128)} %bitcast.parity_ref, bf16[8,128,96]{2,1,0:T(8,128)(2,1)} %copy.6.feat_ref, f32[8,128]{1,0:T(8,128)} %noise_ref.3), custom_call_target="tpu_custom_call" | custom-call | tf_op jit(solution)/shard_map/pack/pallas_call | solution.py:59
  4.2 3.9 %collective-permute-start.2 = (bf16[144,128]{1,0:T(8,128)(2,1)}, bf16[144,128]{1,0:T(8,128)(2,1)S(1)}, u32[]{:S(2)}, u32[]{:S(2)}) collective-permute-start(bf16[144,128]{1,0:T(8,128)(2,1)} %get-tuple-element.7), channel_id=1, source_target_pairs={{0,24},{8,16},{16,8},{24,0},{1,25},{9,17},{17,9},{25,1},{2,26},{10... | collective-permute-start | bytes 110600 | tf_op jit(solution)/shard_map/ppermute | solution.py:271
  8.7 4.0 %collective-permute-start.13 = (bf16[384,128]{1,0:T(8,128)(2,1)}, bf16[384,128]{1,0:T(8,128)(2,1)S(1)}, u32[]{:S(2)}, u32[]{:S(2)}) collective-permute-start(bf16[384,128]{1,0:T(8,128)(2,1)} %get-tuple-element.8.refs_8_), channel_id=1, source_target_pairs={{0,6},{1,7},{2,4},{3,5},{4,2},{5,3},{6,0},{7,1},{8,14},{9,15},{10,... | collective-permute-start | bytes 294920 | tf_op jit(solution)/shard_map/ppermute | solution.py:274
  13.4 0.7 divide_multiply_fusion
  14.7 0.8 %select_select_fusion.2.refs_0_ = bf16[144,128]{1,0:T(8,128)(2,1)S(1)} fusion(bf16[144,128]{1,0:T(8,128)(2,1)S(1)} %collective-permute-done.1, bf16[144,128]{1,0:T(8,128)(2,1)S(1)} %collective-permute-done.2, bf16[144,128]{1,0:T(8,128)(2,1)} %get-tuple-element.7, bf16[144,128]{1,0:T(8,128)(2,1)S(1)} %collective-permute-done, pred[]{:T(512)S(6)} %select_n.110, ...), kind=kLoop, calls=%fused_computation.26 | loop fusion | flops 55296 | bytes 184323 | tf_op jit(solution)/shard_map/select_n | solution.py:278
  15.5 2.0 %collective-permute-start.5 = (bf16[144,128]{1,0:T(8,128)(2,1)S(1)}, bf16[144,128]{1,0:T(8,128)(2,1)S(1)}, u32[]{:S(2)}, u32[]{:S(2)}) collective-permute-start(bf16[144,128]{1,0:T(8,128)(2,1)S(1)} %select_select_fusion.2.refs_0_), channel_id=1, source_target_pairs={{0,6},{1,7},{2,4},{3,5},{4,2},{5,3},{6,0},{7,1},{8,14},{9,15},{10,... | collective-permute-start | bytes 110600 | tf_op jit(solution)/shard_map/ppermute | solution.py:274
  17.5 1.1 %collective-permute-start.4 = (bf16[144,128]{1,0:T(8,128)(2,1)S(1)}, bf16[144,128]{1,0:T(8,128)(2,1)S(1)}, u32[]{:S(2)}, u32[]{:S(2)}) collective-permute-start(bf16[144,128]{1,0:T(8,128)(2,1)S(1)} %select_select_fusion.2.refs_0_), channel_id=1, source_target_pairs={{0,4},{1,5},{2,6},{3,7},{4,0},{5,1},{6,2},{7,3},{8,12},{9,13},{10,... | collective-permute-start | bytes 110600 | tf_op jit(solution)/shard_map/ppermute | solution.py:274
  18.6 1.4 %collective-permute-start.3 = (bf16[144,128]{1,0:T(8,128)(2,1)S(1)}, bf16[144,128]{1,0:T(8,128)(2,1)S(1)}, u32[]{:S(2)}, u32[]{:S(2)}) collective-permute-start(bf16[144,128]{1,0:T(8,128)(2,1)S(1)} %select_select_fusion.2.refs_0_), channel_id=1, source_target_pairs={{0,2},{1,3},{2,0},{3,1},{4,6},{5,7},{6,4},{7,5},{8,10},{9,11},{10,... | collective-permute-start | bytes 110600 | tf_op jit(solution)/shard_map/ppermute | solution.py:274
  20.7 0.7 collective-permute-done.5.refs_3_
  21.4 1.9 %collective-permute-start.7 = (bf16[384,128]{1,0:T(8,128)(2,1)}, bf16[384,128]{1,0:T(8,128)(2,1)S(1)}, u32[]{:S(2)}, u32[]{:S(2)}) collective-permute-start(bf16[384,128]{1,0:T(8,128)(2,1)} %get-tuple-element.8.refs_8_), channel_id=1, source_target_pairs={{0,2},{1,3},{2,0},{3,1},{4,6},{5,7},{6,4},{7,5},{8,10},{9,11},{10,... | collective-permute-start | bytes 294920 | tf_op jit(solution)/shard_map/ppermute | solution.py:274
  23.5 2.8 %collective-permute-start.9 = (bf16[384,128]{1,0:T(8,128)(2,1)}, bf16[384,128]{1,0:T(8,128)(2,1)S(1)}, u32[]{:S(2)}, u32[]{:S(2)}) collective-permute-start(bf16[384,128]{1,0:T(8,128)(2,1)} %get-tuple-element.9.refs_16_), channel_id=1, source_target_pairs={{0,6},{1,7},{2,4},{3,5},{4,2},{5,3},{6,0},{7,1},{8,14},{9,15},{10,... | collective-permute-start | bytes 294920 | tf_op jit(solution)/shard_map/ppermute | solution.py:274
  26.8 2.4 %collective-permute-start.11 = (bf16[384,128]{1,0:T(8,128)(2,1)}, bf16[384,128]{1,0:T(8,128)(2,1)S(1)}, u32[]{:S(2)}, u32[]{:S(2)}) collective-permute-start(bf16[384,128]{1,0:T(8,128)(2,1)} %get-tuple-element.9.refs_16_), channel_id=1, source_target_pairs={{0,2},{1,3},{2,0},{3,1},{4,6},{5,7},{6,4},{7,5},{8,10},{9,11},{10,... | collective-permute-start | bytes 294920 | tf_op jit(solution)/shard_map/ppermute | solution.py:274
  29.1 3.0 %collective-permute-done.9.refs_11_ = bf16[384,128]{1,0:T(8,128)(2,1)S(1)} collective-permute-done((bf16[384,128]{1,0:T(8,128)(2,1)}, bf16[384,128]{1,0:T(8,128)(2,1)S(1)}, u32[]{:S(2)}, u32[]{:S(2)}) %collective-permute-start.9) | collective-permute-done | bytes 98336 | tf_op jit(solution)/shard_map/ppermute | solution.py:274
  32.1 2.1 %collective-permute-done.8.refs_10_ = bf16[384,128]{1,0:T(8,128)(2,1)S(1)} collective-permute-done((bf16[384,128]{1,0:T(8,128)(2,1)}, bf16[384,128]{1,0:T(8,128)(2,1)S(1)}, u32[]{:S(2)}, u32[]{:S(2)}) %collective-permute-start.8) | collective-permute-done | bytes 98336 | tf_op jit(solution)/shard_map/ppermute | solution.py:274
  34.2 0.9 %pad_maximum_fusion = bf16[4,384,128]{2,1,0:T(8,128)(2,1)S(1)} fusion(bf16[1,384,128]{2,1,0:T(8,128)(2,1)S(1)} %bitcast.61, bf16[1,384,128]{2,1,0:T(8,128)(2,1)S(1)} %bitcast.63, bf16[1,384,128]{2,1,0:T(8,128)(2,1)S(1)} %bitcast.59, bf16[1,384,128]{2,1,0:T(8,128)(2,1)} %bitcast.57), kind=kLoop, calls=%fused_computation.1 | loop fusion | flops 589824 | bytes 786432 | tf_op jit(solution)/shard_map/stack | solution.py:289
  35.2 1.6 %collective-permute-start.16 = (bf16[4,384,128]{2,1,0:T(8,128)(2,1)S(1)}, bf16[4,384,128]{2,1,0:T(8,128)(2,1)S(1)}, u32[]{:S(2)}, u32[]{:S(2)}) collective-permute-start(bf16[4,384,128]{2,1,0:T(8,128)(2,1)S(1)} %pad_maximum_fusion), channel_id=1, source_target_pairs={{0,16},{8,24},{16,0},{24,8},{1,17},{9,25},{17,1},{25,9},{2,18},{10... | collective-permute-start | bytes 1179656 | tf_op jit(solution)/shard_map/ppermute | solution.py:271
  36.8 1.4 %collective-permute-start.17 = (bf16[4,384,128]{2,1,0:T(8,128)(2,1)S(1)}, bf16[4,384,128]{2,1,0:T(8,128)(2,1)S(1)}, u32[]{:S(2)}, u32[]{:S(2)}) collective-permute-start(bf16[4,384,128]{2,1,0:T(8,128)(2,1)S(1)} %pad_maximum_fusion), channel_id=1, source_target_pairs={{0,24},{8,16},{16,8},{24,0},{1,25},{9,17},{17,9},{25,1},{2,26},{10... | collective-permute-start | bytes 1179656 | tf_op jit(solution)/shard_map/ppermute | solution.py:271
  38.9 1.7 %pad_maximum_fusion.1 = bf16[4,384,128]{2,1,0:T(8,128)(2,1)} fusion(bf16[1,384,128]{2,1,0:T(8,128)(2,1)S(1)} %bitcast.67, bf16[1,384,128]{2,1,0:T(8,128)(2,1)S(1)} %bitcast.68, bf16[1,384,128]{2,1,0:T(8,128)(2,1)S(1)} %bitcast.69, bf16[1,384,128]{2,1,0:T(8,128)(2,1)} %bitcast.66), kind=kLoop, calls=%fused_computation.2 | loop fusion | flops 589824 | bytes 786432 | tf_op jit(solution)/shard_map/stack | solution.py:289
  41.8 7.9 %first_tile.1.inv_ref = f32[128,128]{1,0:T(8,128)} custom-call(f32[8,128]{1,0:T(8,128)} %pad_select_fusion.weight_ref, bf16[144,128]{1,0:T(8,128)(2,1)} %copy-done.1, bf16[144,128]{1,0:T(8,128)(2,1)} %copy-done.8, bf16[144,128]{1,0:T(8,128)(2,1)} %copy-done.6, bf16[144,128]{1,0:T(8,128)(2,1)} %copy-done.4, bf16[144,128]{1,0:T(8,128)(2,1)} %get-tuple-element.35.refs_4_, ...), custom_call_target="tpu_custom_call" | custom-call | tf_op jit(solution)/shard_map/first_tile/pallas_call | solution.py:141
  49.6 4.0 %collective-permute-done.16 = bf16[4,384,128]{2,1,0:T(8,128)(2,1)S(1)} collective-permute-done((bf16[4,384,128]{2,1,0:T(8,128)(2,1)S(1)}, bf16[4,384,128]{2,1,0:T(8,128)(2,1)S(1)}, u32[]{:S(2)}, u32[]{:S(2)}) %collective-permute-start.16) | collective-permute-done | bytes 393248 | tf_op jit(solution)/shard_map/ppermute | solution.py:271
  53.6 1.3 %collective-permute-done.15 = bf16[4,384,128]{2,1,0:T(8,128)(2,1)S(1)} collective-permute-done((bf16[4,384,128]{2,1,0:T(8,128)(2,1)S(1)}, bf16[4,384,128]{2,1,0:T(8,128)(2,1)S(1)}, u32[]{:S(2)}, u32[]{:S(2)}) %collective-permute-start.15) | collective-permute-done | bytes 393248 | tf_op jit(solution)/shard_map/ppermute | solution.py:271
  55.4 1.6 %collective-permute-done.18 = bf16[4,384,128]{2,1,0:T(8,128)(2,1)S(1)} collective-permute-done((bf16[4,384,128]{2,1,0:T(8,128)(2,1)S(1)}, bf16[4,384,128]{2,1,0:T(8,128)(2,1)S(1)}, u32[]{:S(2)}, u32[]{:S(2)}) %collective-permute-start.18) | collective-permute-done | bytes 393248 | tf_op jit(solution)/shard_map/ppermute | solution.py:274
  57.1 16.3 %rest.1 = (f32[8,128,128]{2,1,0:T(8,128)}, f32[4096,128]{1,0:T(8,128)}) custom-call(s32[4]{0:T(128)S(1)} %pad_add_fusion.where_ref, f32[8,128]{1,0:T(8,128)S(1)} %copy-done.15, f32[8,128]{1,0:T(8,128)S(1)} %copy-done.16, f32[128,128]{1,0:T(8,128)S(1)} %copy-done.14, bf16[144,128]{1,0:T(8,128)(2,1)S(1)} %copy-done.2, bf16[144,128]{1,0:T(8,128)(2,1)S(1)} %copy-done.9, ...), custom_call_target="tpu_custom_call" | custom-call | tf_op jit(solution)/shard_map/rest/pallas_call | solution.py:249
  (69 shorter events, 5.4 us)
Async XLA Ops:
  4.2 50.8 %copy-start = (bf16[384,128]{1,0:T(8,128)(2,1)S(1)}, bf16[384,128]{1,0:T(8,128)(2,1)}, u32[]{:S(2)}) copy-start(bf16[384,128]{1,0:T(8,128)(2,1)} %get-tuple-element.8.refs_8_) | copy-start | bytes 294916
  4.2 10.5 %collective-permute-start.2 = (bf16[144,128]{1,0:T(8,128)(2,1)}, bf16[144,128]{1,0:T(8,128)(2,1)S(1)}, u32[]{:S(2)}, u32[]{:S(2)}) collective-permute-start(bf16[144,128]{1,0:T(8,128)(2,1)} %get-tuple-element.7), channel_id=1, source_target_pairs={{0,24},{8,16},{16,8},{24,0},{1,25},{9,17},{17,9},{25,1},{2,26},{10... | collective-permute-start | bytes 110600 | tf_op jit(solution)/shard_map/ppermute | solution.py:271
  8.1 6.7 %collective-permute-start.1 = (bf16[144,128]{1,0:T(8,128)(2,1)}, bf16[144,128]{1,0:T(8,128)(2,1)S(1)}, u32[]{:S(2)}, u32[]{:S(2)}) collective-permute-start(bf16[144,128]{1,0:T(8,128)(2,1)} %get-tuple-element.7), channel_id=1, source_target_pairs={{0,16},{8,24},{16,0},{24,8},{1,17},{9,25},{17,1},{25,9},{2,18},{10... | collective-permute-start | bytes 110600 | tf_op jit(solution)/shard_map/ppermute | solution.py:271
  8.6 6.2 %collective-permute-start = (bf16[144,128]{1,0:T(8,128)(2,1)}, bf16[144,128]{1,0:T(8,128)(2,1)S(1)}, u32[]{:S(2)}, u32[]{:S(2)}) collective-permute-start(bf16[144,128]{1,0:T(8,128)(2,1)} %get-tuple-element.7), channel_id=1, source_target_pairs={{0,8},{8,0},{16,24},{24,16},{1,9},{9,1},{17,25},{25,17},{2,10},{10... | collective-permute-start | bytes 110600 | tf_op jit(solution)/shard_map/ppermute | solution.py:271
  8.7 28.1 %collective-permute-start.13 = (bf16[384,128]{1,0:T(8,128)(2,1)}, bf16[384,128]{1,0:T(8,128)(2,1)S(1)}, u32[]{:S(2)}, u32[]{:S(2)}) collective-permute-start(bf16[384,128]{1,0:T(8,128)(2,1)} %get-tuple-element.8.refs_8_), channel_id=1, source_target_pairs={{0,6},{1,7},{2,4},{3,5},{4,2},{5,3},{6,0},{7,1},{8,14},{9,15},{10,... | collective-permute-start | bytes 294920 | tf_op jit(solution)/shard_map/ppermute | solution.py:274
  12.7 25.6 %collective-permute-start.12 = (bf16[384,128]{1,0:T(8,128)(2,1)}, bf16[384,128]{1,0:T(8,128)(2,1)S(1)}, u32[]{:S(2)}, u32[]{:S(2)}) collective-permute-start(bf16[384,128]{1,0:T(8,128)(2,1)} %get-tuple-element.8.refs_8_), channel_id=1, source_target_pairs={{0,4},{1,5},{2,6},{3,7},{4,0},{5,1},{6,2},{7,3},{8,12},{9,13},{10,... | collective-permute-start | bytes 294920 | tf_op jit(solution)/shard_map/ppermute | solution.py:274
  15.5 26.2 %copy-start.1 = (bf16[144,128]{1,0:T(8,128)(2,1)}, bf16[144,128]{1,0:T(8,128)(2,1)S(1)}, u32[]{:S(2)}) copy-start(bf16[144,128]{1,0:T(8,128)(2,1)S(1)} %select_select_fusion.2.refs_0_) | copy-start | bytes 110596
  15.5 5.8 %collective-permute-start.5 = (bf16[144,128]{1,0:T(8,128)(2,1)S(1)}, bf16[144,128]{1,0:T(8,128)(2,1)S(1)}, u32[]{:S(2)}, u32[]{:S(2)}) collective-permute-start(bf16[144,128]{1,0:T(8,128)(2,1)S(1)} %select_select_fusion.2.refs_0_), channel_id=1, source_target_pairs={{0,6},{1,7},{2,4},{3,5},{4,2},{5,3},{6,0},{7,1},{8,14},{9,15},{10,... | collective-permute-start | bytes 110600 | tf_op jit(solution)/shard_map/ppermute | solution.py:274
  17.5 6.0 %collective-permute-start.4 = (bf16[144,128]{1,0:T(8,128)(2,1)S(1)}, bf16[144,128]{1,0:T(8,128)(2,1)S(1)}, u32[]{:S(2)}, u32[]{:S(2)}) collective-permute-start(bf16[144,128]{1,0:T(8,128)(2,1)S(1)} %select_select_fusion.2.refs_0_), channel_id=1, source_target_pairs={{0,4},{1,5},{2,6},{3,7},{4,0},{5,1},{6,2},{7,3},{8,12},{9,13},{10,... | collective-permute-start | bytes 110600 | tf_op jit(solution)/shard_map/ppermute | solution.py:274
  18.6 7.7 %collective-permute-start.3 = (bf16[144,128]{1,0:T(8,128)(2,1)S(1)}, bf16[144,128]{1,0:T(8,128)(2,1)S(1)}, u32[]{:S(2)}, u32[]{:S(2)}) collective-permute-start(bf16[144,128]{1,0:T(8,128)(2,1)S(1)} %select_select_fusion.2.refs_0_), channel_id=1, source_target_pairs={{0,2},{1,3},{2,0},{3,1},{4,6},{5,7},{6,4},{7,5},{8,10},{9,11},{10,... | collective-permute-start | bytes 110600 | tf_op jit(solution)/shard_map/ppermute | solution.py:274
  21.4 20.4 %copy-start.4 = (bf16[144,128]{1,0:T(8,128)(2,1)}, bf16[144,128]{1,0:T(8,128)(2,1)S(1)}, u32[]{:S(2)}) copy-start(bf16[144,128]{1,0:T(8,128)(2,1)S(1)} %collective-permute-done.5.refs_3_) | copy-start | bytes 110596
  21.4 5.4 %collective-permute-start.7 = (bf16[384,128]{1,0:T(8,128)(2,1)}, bf16[384,128]{1,0:T(8,128)(2,1)S(1)}, u32[]{:S(2)}, u32[]{:S(2)}) collective-permute-start(bf16[384,128]{1,0:T(8,128)(2,1)} %get-tuple-element.8.refs_8_), channel_id=1, source_target_pairs={{0,2},{1,3},{2,0},{3,1},{4,6},{5,7},{6,4},{7,5},{8,10},{9,11},{10,... | collective-permute-start | bytes 294920 | tf_op jit(solution)/shard_map/ppermute | solution.py:274
  23.5 18.2 %copy-start.6 = (bf16[144,128]{1,0:T(8,128)(2,1)}, bf16[144,128]{1,0:T(8,128)(2,1)S(1)}, u32[]{:S(2)}) copy-start(bf16[144,128]{1,0:T(8,128)(2,1)S(1)} %collective-permute-done.4.refs_2_) | copy-start | bytes 110596
  23.5 8.6 %collective-permute-start.9 = (bf16[384,128]{1,0:T(8,128)(2,1)}, bf16[384,128]{1,0:T(8,128)(2,1)S(1)}, u32[]{:S(2)}, u32[]{:S(2)}) collective-permute-start(bf16[384,128]{1,0:T(8,128)(2,1)} %get-tuple-element.9.refs_16_), channel_id=1, source_target_pairs={{0,6},{1,7},{2,4},{3,5},{4,2},{5,3},{6,0},{7,1},{8,14},{9,15},{10,... | collective-permute-start | bytes 294920 | tf_op jit(solution)/shard_map/ppermute | solution.py:274
  26.3 15.4 %copy-start.8 = (bf16[144,128]{1,0:T(8,128)(2,1)}, bf16[144,128]{1,0:T(8,128)(2,1)S(1)}, u32[]{:S(2)}) copy-start(bf16[144,128]{1,0:T(8,128)(2,1)S(1)} %collective-permute-done.3.refs_1_) | copy-start | bytes 110596
  26.3 7.9 %collective-permute-start.8 = (bf16[384,128]{1,0:T(8,128)(2,1)}, bf16[384,128]{1,0:T(8,128)(2,1)S(1)}, u32[]{:S(2)}, u32[]{:S(2)}) collective-permute-start(bf16[384,128]{1,0:T(8,128)(2,1)} %get-tuple-element.9.refs_16_), channel_id=1, source_target_pairs={{0,4},{1,5},{2,6},{3,7},{4,0},{5,1},{6,2},{7,3},{8,12},{9,13},{10,... | collective-permute-start | bytes 294920 | tf_op jit(solution)/shard_map/ppermute | solution.py:274
  26.8 12.1 %collective-permute-start.11 = (bf16[384,128]{1,0:T(8,128)(2,1)}, bf16[384,128]{1,0:T(8,128)(2,1)S(1)}, u32[]{:S(2)}, u32[]{:S(2)}) collective-permute-start(bf16[384,128]{1,0:T(8,128)(2,1)} %get-tuple-element.9.refs_16_), channel_id=1, source_target_pairs={{0,2},{1,3},{2,0},{3,1},{4,6},{5,7},{6,4},{7,5},{8,10},{9,11},{10,... | collective-permute-start | bytes 294920 | tf_op jit(solution)/shard_map/ppermute | solution.py:274
  32.1 8.5 %collective-permute-start.6 = (bf16[4,144,128]{2,1,0:T(8,128)(2,1)S(1)}, bf16[4,144,128]{2,1,0:T(8,128)(2,1)S(1)}, u32[]{:S(2)}, u32[]{:S(2)}) collective-permute-start(bf16[4,144,128]{2,1,0:T(8,128)(2,1)S(1)} %pad_maximum_fusion.2), channel_id=1, source_target_pairs={{0,1},{1,0},{2,3},{3,2},{4,5},{5,4},{6,7},{7,6},{8,9},{9,8},{10,11... | collective-permute-start | bytes 442376 | tf_op jit(solution)/shard_map/ppermute | solution.py:274
  35.2 18.4 %collective-permute-start.16 = (bf16[4,384,128]{2,1,0:T(8,128)(2,1)S(1)}, bf16[4,384,128]{2,1,0:T(8,128)(2,1)S(1)}, u32[]{:S(2)}, u32[]{:S(2)}) collective-permute-start(bf16[4,384,128]{2,1,0:T(8,128)(2,1)S(1)} %pad_maximum_fusion), channel_id=1, source_target_pairs={{0,16},{8,24},{16,0},{24,8},{1,17},{9,25},{17,1},{25,9},{2,18},{10... | collective-permute-start | bytes 1179656 | tf_op jit(solution)/shard_map/ppermute | solution.py:271
  36.8 16.8 %collective-permute-start.17 = (bf16[4,384,128]{2,1,0:T(8,128)(2,1)S(1)}, bf16[4,384,128]{2,1,0:T(8,128)(2,1)S(1)}, u32[]{:S(2)}, u32[]{:S(2)}) collective-permute-start(bf16[4,384,128]{2,1,0:T(8,128)(2,1)S(1)} %pad_maximum_fusion), channel_id=1, source_target_pairs={{0,24},{8,16},{16,8},{24,0},{1,25},{9,17},{17,9},{25,1},{2,26},{10... | collective-permute-start | bytes 1179656 | tf_op jit(solution)/shard_map/ppermute | solution.py:271
  38.3 16.7 %collective-permute-start.15 = (bf16[4,384,128]{2,1,0:T(8,128)(2,1)S(1)}, bf16[4,384,128]{2,1,0:T(8,128)(2,1)S(1)}, u32[]{:S(2)}, u32[]{:S(2)}) collective-permute-start(bf16[4,384,128]{2,1,0:T(8,128)(2,1)S(1)} %pad_maximum_fusion), channel_id=1, source_target_pairs={{0,8},{8,0},{16,24},{24,16},{1,9},{9,1},{17,25},{25,17},{2,10},{10... | collective-permute-start | bytes 1179656 | tf_op jit(solution)/shard_map/ppermute | solution.py:271
  38.8 16.5 %collective-permute-start.10 = (bf16[4,384,128]{2,1,0:T(8,128)(2,1)S(1)}, bf16[4,384,128]{2,1,0:T(8,128)(2,1)S(1)}, u32[]{:S(2)}, u32[]{:S(2)}) collective-permute-start(bf16[4,384,128]{2,1,0:T(8,128)(2,1)S(1)} %pad_maximum_fusion), channel_id=1, source_target_pairs={{0,1},{1,0},{2,3},{3,2},{4,5},{5,4},{6,7},{7,6},{8,9},{9,8},{10,11... | collective-permute-start | bytes 1179656 | tf_op jit(solution)/shard_map/ppermute | solution.py:274
  40.6 14.7 %collective-permute-start.14 = (bf16[4,384,128]{2,1,0:T(8,128)(2,1)}, bf16[4,384,128]{2,1,0:T(8,128)(2,1)S(1)}, u32[]{:S(2)}, u32[]{:S(2)}) collective-permute-start(bf16[4,384,128]{2,1,0:T(8,128)(2,1)} %pad_maximum_fusion.1), channel_id=1, source_target_pairs={{0,1},{1,0},{2,3},{3,2},{4,5},{5,4},{6,7},{7,6},{8,9},{9,8},{10,11... | collective-permute-start | bytes 1179656 | tf_op jit(solution)/shard_map/ppermute | solution.py:274
  55.2 1.8 %collective-permute-start.18 = (bf16[4,384,128]{2,1,0:T(8,128)(2,1)S(1)}, bf16[4,384,128]{2,1,0:T(8,128)(2,1)S(1)}, u32[]{:S(2)}, u32[]{:S(2)}) collective-permute-start(bf16[4,384,128]{2,1,0:T(8,128)(2,1)S(1)} %get-tuple-element.14), channel_id=1, source_target_pairs={{0,1},{1,0},{2,3},{3,2},{4,5},{5,4},{6,7},{7,6},{8,9},{9,8},{10,11... | collective-permute-start | bytes 1179656 | tf_op jit(solution)/shard_map/ppermute | solution.py:274
  (12 other events, 23.3 us)

commit v2 on v0

--- a/solution.py
+++ b/solution.py
@@ -1,7 +1,367 @@
+import functools
+
 import jax
 import jax.numpy as jnp
 from jax import lax
+from jax.experimental import pallas as pl
+from jax.experimental.pallas import tpu as pltpu
 from jax.sharding import PartitionSpec as P
+
+LANES = 128
+VMEM_ROWS = 28
+VMEM_TRAIL = 32
+ORDER = (0, 2, 4, 6, 1, 3, 5, 7)
+VM = pl.BlockSpec(memory_space=pltpu.VMEM)
+ANY = pl.BlockSpec(memory_space=pl.ANY)
+
+
+def nt(a, b, precision=None):
+    return lax.dot_general(
+        a, b, (((1,), (1,)), ((), ())), precision=precision, preferred_element_type=jnp.float32
+    )
+
+
+def split2(x):
+    hi = x.astype(jnp.bfloat16)
+    return hi, (x - hi.astype(jnp.float32)).astype(jnp.bfloat16)
+
+
+def split3(x):
+    hi, mid = split2(x)
+    rest = x - hi.astype(jnp.float32) - mid.astype(jnp.float32)
+    return hi, mid, rest.astype(jnp.bfloat16)
+
+
+def slice_weights(length_ref, depth):
+    col_id = lax.axis_index("col")
+    lane = lax.broadcasted_iota(jnp.int32, (8, LANES), 1)
+    row = lax.broadcasted_iota(jnp.int32, (8, LANES), 0)
+    held = jnp.ones((8, LANES), jnp.float32)
+    for s in range(8):
+        chunk, off = divmod(depth * s, LANES)
+        here = jnp.broadcast_to(length_ref[chunk : chunk + 1, :], (8, LANES))
+        if off:
+            here = pltpu.roll(here, LANES - off, 1)
+        if off + depth > LANES:
+            more = jnp.broadcast_to(length_ref[chunk + 1 : chunk + 2, :], (8, LANES))
+            here = jnp.where(lane < LANES - off, here, pltpu.roll(more, LANES - off, 1))
+        for place, k in enumerate(ORDER):
+            held = jnp.where((row == place) & (col_id == (s ^ k)), here, held)
+    inverse = 1.0 / held
+    columns = (inverse * inverse).T
+    return [columns[0:depth, s : s + 1] for s in range(8)]
+
+
+def bcast(v):
+    return jnp.broadcast_to(v, (8, LANES))
+
+
+def inverse_factor(tiles, rows, lanes, m=8):
+    size = 8 * len(tiles)
+    tiles, out = list(tiles), [None] * len(tiles)
+    for k in range(0, size, m):
+        b, j = divmod(k, 8)
+        r = [bcast(tiles[b][j + i : j + i + 1, :]) for i in range(m)]
+        s = [[bcast(r[i][:, k + l : k + l + 1]) if l >= i else None for l in range(m)] for i in range(m)]
+        r = [r[i] + jnp.where(lanes == k + i, 1.0, 0.0) for i in range(m)]
+        inv, f = [], [[None] * m for _ in range(m)]
+        for p in range(m):
+            inv.append(1.0 / s[p][p])
+            for i in range(p + 1, m):
+                f[p][i] = s[p][i] * inv[p]
+            for i in range(p + 1, m):
+                for l in range(i, m):
+                    s[i][l] = s[i][l] - f[p][i] * s[p][l]
+            for i in range(p + 1, m):
+                r[i] = r[i] - f[p][i] * r[p]
+        for i in range(m):
+            w = jnp.where(lanes < k + i, r[i], jnp.where(lanes == k + i, 1.0, 0.0)) * lax.rsqrt(s[i][i])
+            out[b] = w if out[b] is None else jnp.where(rows == j + i, w, out[b])
+        if k + m >= size:
+            break
+        y = [r[i] * inv[i] for i in range(m)]
+        for i in range(m - 1, -1, -1):
+            for l in range(i + 1, m):
+                y[i] = y[i] - f[i][l] * y[l]
+        for i in range(b, len(tiles)):
+            if i == b and j + m >= 8:
+                continue
+            acc = None
+            for q in range(m):
+                c = bcast(tiles[i][:, k + q : k + q + 1])
+                if i == b:
+                    c = jnp.where(rows > j + m - 1, c, 0.0)
+                acc = c * y[q] if acc is None else acc + c * y[q]
+            tiles[i] = tiles[i] - acc
+    return out
+
+
+def gather_kernel(feat_ref, near_ref, far1_ref, far2_ref, noise_ref, out_ref, land, sems):
+    depth = feat_ref.shape[1]
+    sources = (feat_ref.at[0], near_ref.at[0], far1_ref, far2_ref)
+    copies = [pltpu.make_async_copy(src, land.at[k], sems.at[k]) for k, src in enumerate(sources)]
+    for copy in copies:
+        copy.start()
+    row = lax.broadcasted_iota(jnp.int32, (16, LANES), 0)
+    parts = jnp.zeros((16, LANES), jnp.float32)
+    for k, part in enumerate(split3(noise_ref[0:1, :])):
+        parts = jnp.where(row == k, part.astype(jnp.float32), parts)
+    out_ref[4 * depth :, :] = parts.astype(jnp.bfloat16)
+    for k, copy in enumerate(copies):
+        copy.wait()
+        out_ref[k * depth : (k + 1) * depth, :] = land[k]
+
+
+def gather_first(feats, near, far, noise):
+    _, depth, width = feats.shape
+    return pl.pallas_call(
+        gather_kernel,
+        out_shape=jax.ShapeDtypeStruct((4 * depth + 16, width), jnp.bfloat16),
+        in_specs=[ANY] * 4 + [VM],
+        out_specs=VM,
+        scratch_shapes=[pltpu.VMEM((4, depth, width), jnp.bfloat16), pltpu.SemaphoreType.DMA((4,))],
+        name="gather_first",
+    )(feats, near, *far, noise)
+
+
+def first_kernel(length_ref, mine_ref, sib_ref, inv_ref, rows_ref, both_ref, sq_ref, diag_ref, work):
+    width = inv_ref.shape[0]
+    depth = (mine_ref.shape[0] - 16) // 4
+    x = jnp.concatenate([ref[0 : 4 * depth, :] for ref in (mine_ref, sib_ref)], axis=0)
+    w = jnp.concatenate(slice_weights(length_ref, depth), axis=0)
+    xf = x.astype(jnp.float32)
+    xw = xf * w
+    parts = split3(xw)
+    rows_ref[...] = xf.T.astype(jnp.bfloat16)
+    both_ref[...] = jnp.concatenate(parts[:2], axis=1)
+    gram = sum(
+        lax.dot_general(rows_ref[...], part, (((1,), (0,)), ((), ())), preferred_element_type=jnp.float32)
+        for part in parts
+    )
+    sq_row = jnp.sum(xf * xw, axis=0, keepdims=True)
+    sq_ref[...] = jnp.broadcast_to(sq_row, sq_ref.shape)
+    sq_col = jnp.broadcast_to(sq_row, (8, width)).T[:, 0:1]
+    tail = mine_ref[4 * depth :, :].astype(jnp.float32)
+    noise = tail[0:1, :] + tail[1:2, :] + tail[2:3, :]
+    i = lax.broadcasted_iota(jnp.int32, (width, width), 0)
+    j = lax.broadcasted_iota(jnp.int32, (width, width), 1)
+    diag = jnp.where(i == j, noise, 0.0)
+    diag_ref[...] = diag
+    work[...] = jnp.exp(-0.5 * (sq_col + sq_row - 2.0 * gram)) + diag
+    rows = lax.broadcasted_iota(jnp.int32, (8, LANES), 0)
+    lanes = lax.broadcasted_iota(jnp.int32, (8, LANES), 1)
+    tiles = [work[8 * t : 8 * t + 8, :] for t in range(width // 8)]
+    for t, tile in enumerate(inverse_factor(tiles, rows, lanes)):
+        inv_ref[8 * t : 8 * t + 8, :] = tile
+
+
+def first_tile(lengths, mine, sib):
+    width = mine.shape[1]
+    whole = 2 * (mine.shape[0] - 16)
+    return pl.pallas_call(
+        first_kernel,
+        out_shape=(
+            jax.ShapeDtypeStruct((width, width), jnp.float32),
+            jax.ShapeDtypeStruct((width, whole), jnp.bfloat16),
+            jax.ShapeDtypeStruct((whole, 2 * width), jnp.bfloat16),
+            jax.ShapeDtypeStruct((8, width), jnp.float32),
+            jax.ShapeDtypeStruct((width, width), jnp.float32),
+        ),
+        in_specs=[VM] * 3,
+        out_specs=(VM,) * 5,
+        scratch_shapes=[pltpu.VMEM((width, width), jnp.float32)],
+        name="first_tile",
+    )(lengths, mine, sib)
+
+
+def three(x):
+    hi, lo = split2(x)
+    return jnp.concatenate([hi, lo, hi], axis=1)
+
+
+def twice(y):
+    hi, lo = split2(y)
+    return jnp.concatenate([hi, hi, lo], axis=1)
+
+
+def twice_rows(y):
+    hi, lo = split2(y)
+    return jnp.concatenate([hi, hi, lo], axis=0)
+
+
+def mm(a, b):
+    return jnp.dot(a, b, preferred_element_type=jnp.float32)
+
+
+def rows_kernel(length_ref, inv_ref, both_ref, sq0_ref, diag_ref, *refs):
+    sources, (panel_ref, x_ref, sq_ref, land, sems) = refs[:4], refs[4:]
+    depth, width = sources[0].shape[2:]
+    copies = [
+        [pltpu.make_async_copy(src.at[:, t], land.at[n, t], sems.at[n, t]) for n, src in enumerate(sources)]
+        for t in range(4)
+    ]
+    for copy in sum(copies, []):
+        copy.start()
+    row_id, parity = lax.axis_index("row"), lax.axis_index("col") // lax.axis_size("row")
+    w = jnp.concatenate(slice_weights(length_ref, depth), axis=0)
+    inv = twice(inv_ref[...])
+    for t in range(4):
+        rows, sqs = [], []
+        for copy in copies[t]:
+            copy.wait()
+        for n in (0, 2):
+            xf = land[n : n + 2, t].reshape(8 * depth, width).astype(jnp.float32)
+            rows.append(xf.T.astype(jnp.bfloat16))
+            sq = jnp.sum(xf * xf * w, axis=0, keepdims=True)
+            sqs.append(jnp.broadcast_to(sq, (LANES, width)).T)
+        x, sq = jnp.concatenate(rows, axis=0), jnp.concatenate(sqs, axis=0)
+        x_ref[2 * t * width : 2 * (t + 1) * width, :] = x
+        sq_ref[2 * t * width : 2 * (t + 1) * width, :] = sq
+        gram = mm(x, both_ref[...])
+        gram = gram[:, 0:width] + gram[:, width:]
+        kern = jnp.exp(gram - 0.5 * (sq + sq0_ref[0:1, :]))
+        if t == 0:
+            kern = jnp.concatenate(
+                [
+                    kern[h * width : (h + 1) * width]
+                    + jnp.where((row_id == 0) & (parity == h), diag_ref[...], 0.0)
+                    for h in range(2)
+                ],
+                axis=0,
+            )
+        panel = nt(three(kern), inv)
+        panel_ref[2 * t + parity] = panel[0:width]
+        panel_ref[2 * t + 1 - parity] = panel[width:]
+
+
+def make_rows(lengths, first, *halves):
+    inv, _, both, sq0, diag = first
+    depth, width = halves[0].shape[2:]
+    return pl.pallas_call(
+        rows_kernel,
+        out_shape=(
+            jax.ShapeDtypeStruct((8, width, width), jnp.float32),
+            jax.ShapeDtypeStruct((8 * width, 8 * depth), jnp.bfloat16),
+            jax.ShapeDtypeStruct((8 * width, width), jnp.float32),
+        ),
+        in_specs=[VM] * 5 + [ANY] * 4,
+        out_specs=(VM,) * 3,
+        scratch_shapes=[
+            pltpu.VMEM((4, 4, 4, depth, width), jnp.bfloat16),
+            pltpu.SemaphoreType.DMA((4, 4)),
+        ],
+        compiler_params=pltpu.CompilerParams(vmem_limit_bytes=VMEM_ROWS * 1024 * 1024),
+        name="rows",
+    )(lengths, inv, both, sq0, diag, *halves)
+
+
+def trail_kernel(length_ref, noise_ref, inv_ref, a_ref, sq0_ref, diag_ref, panel_ref, x_ref, sq_ref, *refs):
+    sources, (trail_ref, land, sems) = refs[:2], refs[2:]
+    depth, width = sources[0].shape[2:]
+    copies = [
+        [pltpu.make_async_copy(src.at[:, t], land.at[t, n], sems.at[t, n]) for n, src in enumerate(sources)]
+        for t in range(4)
+    ]
+    for copy in sum(copies, []):
+        copy.start()
+    row_id, col_id, n_rows = lax.axis_index("row"), lax.axis_index("col"), lax.axis_size("row")
+    parity, on_diag = col_id // n_rows, row_id == col_id % n_rows
+    w = jnp.concatenate(slice_weights(length_ref, depth), axis=0)
+    his, los, sqs = [], [], []
+    for t in range(4):
+        for copy in copies[t]:
+            copy.wait()
+        c = land[t].reshape(8 * depth, width).astype(jnp.float32)
+        cw = c * w
+        hi, lo = split2(cw)
+        his.append(hi)
+        los.append(lo)
+        sqs.append(jnp.sum(c * cw, axis=0, keepdims=True))
+    hi, lo = jnp.concatenate(his, axis=1), jnp.concatenate(los, axis=1)
+    c_sq = 0.5 * jnp.concatenate(sqs, axis=1)
+
+    eye = lax.broadcasted_iota(jnp.int32, (width, width), 0) == lax.broadcasted_iota(
+        jnp.int32, (width, width), 1
+    )
+    sq0 = sq0_ref[...].T[:, 0:1]
+    kern = jnp.exp(mm(a_ref[...], hi) + mm(a_ref[...], lo) - (0.5 * sq0 + c_sq))
+    kern = jnp.concatenate(
+        [kern[:, 0:width] + jnp.where(col_id == 0, diag_ref[...], 0.0), kern[:, width:]], axis=1
+    )
+    c_panel = twice_rows(mm(three(inv_ref[...]), twice_rows(kern)))
+
+    for t in range(4):
+        x = x_ref[2 * t * width : 2 * (t + 1) * width, :]
+        sq = sq_ref[2 * t * width : 2 * (t + 1) * width, 0:1]
+        panel = jnp.concatenate([panel_ref[2 * t + parity], panel_ref[2 * t + 1 - parity]], axis=0)
+        kern = jnp.exp(mm(x, hi) + mm(x, lo) - (0.5 * sq + c_sq))
+        trail = kern - mm(three(panel), c_panel)
+        for half in range(2):
+            tile = 2 * t + (parity if half == 0 else 1 - parity)
+            for tc in range(4):
+                block = trail[half * width : (half + 1) * width, tc * width : (tc + 1) * width]
+                if half == 0 and tc == t:
+                    block = block + jnp.where(eye & on_diag, noise_ref[pl.ds(tile, 1), :], 0.0)
+                trail_ref[pl.ds(tile * (4 * width) + tc, width, stride=4), :] = block
+
+
+def make_trail(lengths, noise, first, rows, *cols):
+    inv, a, _, sq0, diag = first
+    tiles, width = noise.shape
+    depth = cols[0].shape[2]
+    return pl.pallas_call(
+        trail_kernel,
+        out_shape=jax.ShapeDtypeStruct((tiles * width * 4, width), jnp.float32),
+        in_specs=[VM] * 9 + [ANY] * 2,
+        out_specs=VM,
+        scratch_shapes=[
+            pltpu.VMEM((4, 2, 4, depth, width), jnp.bfloat16),
+            pltpu.SemaphoreType.DMA((4, 2)),
+        ],
+        compiler_params=pltpu.CompilerParams(vmem_limit_bytes=VMEM_TRAIL * 1024 * 1024),
+        name="trail",
+    )(lengths, noise, inv, a, sq0, diag, *rows, *cols)
+
+
+def body(features, lengthscale, noise):
+    tiles, width, depth = features.shape
+    row_id = lax.axis_index("row")
+    col_id = lax.axis_index("col")
+    n_rows, n_cols = lax.axis_size("row"), lax.axis_size("col")
+    home = col_id % n_rows
+    parity = col_id // n_rows
+
+    def over_row(x, k):
+        return lax.ppermute(x, "row", [(i, i ^ k) for i in range(n_rows)])
+
+    def over_col(x, k):
+        return lax.ppermute(x, "col", [(i, i ^ k) for i in range(n_cols)])
+
+    feats = jnp.transpose(features, (0, 2, 1))
+    lengths = lengthscale.reshape(-1, LANES)
+    halves = feats.reshape(4, 2, depth, width)
+    own = lax.dynamic_index_in_dim(halves, parity, 1, keepdims=False)
+    oth = lax.dynamic_index_in_dim(halves, 1 - parity, 1, keepdims=False)
+    near = over_col(feats, 2)
+    far = [over_col(feats[0], 2 * k) for k in (2, 3)]
+    near_own = lax.dynamic_index_in_dim(near.reshape(halves.shape), parity, 1, keepdims=False)
+    near_oth = lax.dynamic_index_in_dim(near.reshape(halves.shape), 1 - parity, 1, keepdims=False)
+    oth_late, far[0], far[1] = lax.optimization_barrier((oth, *far))
+    p = [own, near_own, over_col(oth_late, 4), over_col(oth_late, 6)]
+    stack = gather_first(feats, near, far, noise)
+    stack = lax.select_n(row_id, stack, *[over_row(stack, k) for k in (1, 2, 3)])
+    sib = over_col(stack, 1)
+    first = first_tile(lengths, stack, sib)
+    p_all, stack = lax.optimization_barrier((jnp.stack(p), stack))
+    planes = [p_all] + [over_row(p_all, k) for k in (1, 2, 3)]
+    own_late, _ = lax.optimization_barrier((own, sib))
+    q_all = jnp.stack([oth, near_oth, over_col(own_late, 4), over_col(own_late, 6)])
+    p_late, q_late, _ = lax.optimization_barrier((p_all, q_all, first[0]))
+    rows = make_rows(lengths, first, p_late, over_col(p_late, 1), q_late, over_col(q_late, 1))
+    keep = lax.select_n(row_id ^ home, *planes)
+    give = over_col(lax.select_n(row_id ^ home ^ 1, *planes), 1)
+    trailing = make_trail(lengths, noise, first, rows, keep, give)
+    return rows[0], trailing.reshape(tiles, width, 4, width)
 
 
 def from_root(block, axis, holder):
@@ -9,12 +369,7 @@
     return lax.psum(block, axis)
 
 
-def kernel_block(left, left_sq, right, right_sq):
-    gram = jnp.dot(left, right.T, precision=lax.Precision.HIGHEST)
-    return jnp.exp(-0.5 * (left_sq[:, None] + right_sq[None, :] - 2.0 * gram))
-
-
-def body(features, lengthscale, noise):
+def general_body(features, lengthscale, noise):
     rows_axis = lax.axis_size("row")
     cols_axis = lax.axis_size("col")
     row_id = lax.axis_index("row")
@@ -35,16 +390,14 @@
     right_sq = jnp.sum(right * right, axis=1)
     inner = jnp.arange(width, dtype=jnp.int32)
     row_index = (
-        (jnp.arange(tiles_row, dtype=jnp.int32)[:, None] * rows_axis + row_id) * width
-        + inner[None, :]
+        (jnp.arange(tiles_row, dtype=jnp.int32)[:, None] * rows_axis + row_id) * width + inner[None, :]
     ).reshape(-1)
     col_index = (
-        (jnp.arange(tiles_col, dtype=jnp.int32)[:, None] * cols_axis + col_id) * width
-        + inner[None, :]
+        (jnp.arange(tiles_col, dtype=jnp.int32)[:, None] * cols_axis + col_id) * width + inner[None, :]
     ).reshape(-1)
-    noise_rows = noise.reshape(-1)
-    kern = kernel_block(left, left_sq, right, right_sq)
-    kern = kern + jnp.where(row_index[:, None] == col_index[None, :], noise_rows[:, None], 0.0)
+    gram = jnp.dot(left, right.T, precision=lax.Precision.HIGHEST)
+    kern = jnp.exp(-0.5 * (left_sq[:, None] + right_sq[None, :] - 2.0 * gram))
+    kern = kern + jnp.where(row_index[:, None] == col_index[None, :], noise.reshape(-1)[:, None], 0.0)
     diag_tile = from_root(kern[:width, :width], "row", 0)
     factor = jnp.linalg.cholesky(diag_tile)
     own_rows = jax.scipy.linalg.solve_triangular(factor, kern[:, :width].T, lower=True).T
@@ -61,8 +414,9 @@
 
 def solution(mesh):
     placed = (P(None, "row", "col"), P(), P(None, "row"))
+    small = mesh.shape["row"] == 4 and mesh.shape["col"] == 8
     return jax.shard_map(
-        body,
+        body if small else general_body,
         mesh=mesh,
         in_specs=placed,
         out_specs=(P(None, "row", None), P(None, "row", None, "col")),

time: 282 us -> 57.5 us (0.20)
  waiting for transfers between devices: 217 us -> 10.6 us
  other arithmetic: 30.7 us -> 1.17 us
  Pallas kernels: 0 us -> 20.1 us
  starting transfers between devices: 0.39 us -> 19.9 us
  between operations: 13.9 us -> 0.83 us
  matrix products: 12.4 us -> 0 us
    psum x4 -> x0, waiting for transfers between devices: 188 us -> none  [from_root(): return lax.psum(block, axis)]
    all_gather x1 -> x0, waiting for transfers between devices: 28.9 us -> none  [body(): row_feats = lax.all_gather(features, 'col', axis=2, tiled=True)]
    another operation x5 -> x2, other arithmetic: 22.9 us -> 0.1 us  [the longest x1 0.05 us: body(): p_all, stack = lax.optimization_barrier((jnp.stack(p), stack))]
    pallas_call x0 -> x4, Pallas kernels: none -> 20.1 us  [the longest x1 8.15 us: first_tile(): pl.pallas_call(first_kernel, out_shape=(jax.ShapeDtypeStruct((width, widt...]
    ppermute x0 -> x17, starting transfers between devices: none -> 19.9 us  [the longest x11 12.8 us: over_col(): return lax.ppermute(x, 'col', [(i, i ^ k) for i in range(n_cols)])]
    dot_general x2 -> x0, matrix products: 11 us -> none  [the longest x1 7.41 us: kernel_block(): gram = jnp.dot(left, right.T, precision=lax.Precision.HIGHEST)]
    ppermute x0 -> x17, waiting for transfers between devices: none -> 10.6 us  [the longest x11 7.76 us: over_col(): return lax.ppermute(x, 'col', [(i, i ^ k) for i in range(n_cols)])]
    reduce_sum x2 -> x0, other arithmetic: 3.48 us -> none  [the longest x1 2.07 us: body(): left_sq = jnp.sum(left * left, axis=1)]
  transfers between devices with their start and end apart: 5 -> 17, of which waited for: 5 -> 10; matrix products, arithmetic and copies ran while one was open for 1% -> 5% of each run, Pallas kernels for 0% -> 25%
where the time goes in v2:
time: 57.5 us; the launch traced here: 57 us
  Pallas kernels  20.1 us (35%)
  starting transfers between devices  19.9 us (35%)
  waiting for transfers between devices  10.6 us (18%)
  local copies, waits for them, and re-layouts  4.48 us (8%)
  other arithmetic  1.17 us (2%)
  between operations  0.83 us (1%)
    ppermute x11, starting transfers between devices, over_col(): return lax.ppermute(x, 'col', [(i, i ^ k) for i in range(n_cols)])  12.8 us
    pallas_call x1, Pallas kernels, first_tile(): pl.pallas_call(first_kernel, out_shape=(jax.ShapeDtypeStruct((width, widt...  8.15 us
    ppermute x11, waiting for transfers between devices, over_col(): return lax.ppermute(x, 'col', [(i, i ^ k) for i in range(n_cols)])  7.76 us
    ppermute x6, starting transfers between devices, over_row(): return lax.ppermute(x, 'row', [(i, i ^ k) for i in range(n_rows)])  7.11 us
    pallas_call x1, Pallas kernels, make_trail(): pl.pallas_call(trail_kernel, out_shape=jax.ShapeDtypeStruct((tiles * widt...  5.59 us
    pallas_call x1, Pallas kernels, make_rows(): pl.pallas_call(rows_kernel, out_shape=(jax.ShapeDtypeStruct((8, width, wi...  4.19 us
    ppermute x6, waiting for transfers between devices, over_row(): return lax.ppermute(x, 'row', [(i, i ^ k) for i in range(n_rows)])  2.84 us
    pallas_call x1, Pallas kernels, gather_first(): pl.pallas_call(gather_kernel, out_shape=jax.ShapeDtypeStruct((4 * depth +...  2.15 us
  transfers between devices with their start and end apart: 17, of which 10 were waited for; matrix products, arithmetic and copies ran while one was open for 5% of the time, Pallas kernels for 25%

profile of v2, /device:TPU:0, one launch (start us, length us, event | category | flops | bytes accessed | tf_op | source)
XLA Modules:
  0.0 57.0 jit_solution(12755924577798334599)
XLA Ops:
  0.6 3.1 %collective-permute-start = (bf16[8,96,128]{2,1,0:T(8,128)(2,1)}, bf16[8,96,128]{2,1,0:T(8,128)(2,1)S(1)}, u32[]{:S(2)}, u32[]{:S(2)}) collective-permute-start(bf16[8,96,128]{2,1,0:T(8,128)(2,1)} %bitcast.38), channel_id=1, source_target_pairs={{0,2},{1,3},{2,0},{3,1},{4,6},{5,7},{6,4},{7,5},{8,10},{9,11},{10,... | collective-permute-start | bytes 589832 | tf_op jit(solution)/shard_map/ppermute | solution.py:338
  3.7 0.8 %slice_bitcast_fusion = bf16[96,128]{1,0:T(8,128)(2,1)S(1)} fusion(bf16[8,96,128]{2,1,0:T(8,128)(2,1)} %bitcast.39), kind=kLoop, calls=%fused_computation.11 | loop fusion | bytes 49152 | tf_op jit(solution)/shard_map/squeeze | solution.py:346
  4.5 2.5 %collective-permute-start.2 = (bf16[96,128]{1,0:T(8,128)(2,1)S(1)}, bf16[96,128]{1,0:T(8,128)(2,1)S(1)}, u32[]{:S(2)}, u32[]{:S(2)}) collective-permute-start(bf16[96,128]{1,0:T(8,128)(2,1)S(1)} %slice_bitcast_fusion), channel_id=1, source_target_pairs={{0,6},{1,7},{2,4},{3,5},{4,2},{5,3},{6,0},{7,1},{8,14},{9,15},{10,... | collective-permute-start | bytes 73736 | tf_op jit(solution)/shard_map/ppermute | solution.py:338
  7.1 1.0 %dynamic-slice_bitcast_fusion.5 = (bf16[1,4,96,128]{3,2,1,0:T(8,128)(2,1)S(1)}, bf16[4,96,128]{2,1,0:T(8,128)(2,1)S(1)}, bf16[1,4,96,128]{3,2,1,0:T(8,128)(2,1)S(1)}, bf16[4,96,128]{2,1,0:T(8,128)(2,1)S(1)}) fusion(bf16[4,2,96,128]{3,2,1,0:T(8,128)(2,1)} %bitcast.40, s32[]{:T(128)S(6)} %select_n.106, s32[]{:T(128)S(6)} %select_n.112), kind=kLoop, calls=%fused_computation.10 | loop fusion | bytes 589832 | tf_op jit(solution)/shard_map/stack | solution.py:358
  8.1 3.8 %collective-permute-done.2.far2_ref = bf16[96,128]{1,0:T(8,128)(2,1)S(1)} collective-permute-done((bf16[96,128]{1,0:T(8,128)(2,1)S(1)}, bf16[96,128]{1,0:T(8,128)(2,1)S(1)}, u32[]{:S(2)}, u32[]{:S(2)}) %collective-permute-start.2) | collective-permute-done | bytes 24608 | tf_op jit(solution)/shard_map/ppermute | solution.py:338
  12.2 1.4 %collective-permute-start.8 = (bf16[4,96,128]{2,1,0:T(8,128)(2,1)S(1)}, bf16[4,96,128]{2,1,0:T(8,128)(2,1)S(1)}, u32[]{:S(2)}, u32[]{:S(2)}) collective-permute-start(bf16[4,96,128]{2,1,0:T(8,128)(2,1)S(1)} %get-tuple-element.23), channel_id=1, source_target_pairs={{0,6},{1,7},{2,4},{3,5},{4,2},{5,3},{6,0},{7,1},{8,14},{9,15},{10,... | collective-permute-start | bytes 294920 | tf_op jit(solution)/shard_map/ppermute | solution.py:338
  13.6 0.6 %collective-permute-start.7 = (bf16[4,96,128]{2,1,0:T(8,128)(2,1)S(1)}, bf16[4,96,128]{2,1,0:T(8,128)(2,1)S(1)}, u32[]{:S(2)}, u32[]{:S(2)}) collective-permute-start(bf16[4,96,128]{2,1,0:T(8,128)(2,1)S(1)} %get-tuple-element.23), channel_id=1, source_target_pairs={{0,4},{1,5},{2,6},{3,7},{4,0},{5,1},{6,2},{7,3},{8,12},{9,13},{10,... | collective-permute-start | bytes 294920 | tf_op jit(solution)/shard_map/ppermute | solution.py:338
  14.2 0.7 %copy-done.8 = bf16[8,96,128]{2,1,0:T(8,128)(2,1)} copy-done((bf16[8,96,128]{2,1,0:T(8,128)(2,1)}, bf16[8,96,128]{2,1,0:T(8,128)(2,1)S(1)}, u32[]{:S(2)}) %copy-start.8) | copy-done | bytes 196632
  14.9 2.2 %gather_first.1 = bf16[400,128]{1,0:T(8,128)(2,1)} custom-call(bf16[8,96,128]{2,1,0:T(8,128)(2,1)} %bitcast.41, bf16[8,96,128]{2,1,0:T(8,128)(2,1)} %copy-done.8, bf16[96,128]{1,0:T(8,128)(2,1)} %copy-done.12, bf16[96,128]{1,0:T(8,128)(2,1)} %copy-done.11, f32[8,128]{1,0:T(8,128)} %noise_ref.3), custom_call_target="tpu_custom_call" | custom-call | tf_op jit(solution)/shard_map/gather_first/pallas_call | solution.py:117
  17.1 2.5 %collective-permute-start.5 = (bf16[400,128]{1,0:T(8,128)(2,1)}, bf16[400,128]{1,0:T(8,128)(2,1)S(1)}, u32[]{:S(2)}, u32[]{:S(2)}) collective-permute-start(bf16[400,128]{1,0:T(8,128)(2,1)} %gather_first.1), channel_id=1, source_target_pairs={{0,24},{8,16},{16,8},{24,0},{1,25},{9,17},{17,9},{25,1},{2,26},{10... | collective-permute-start | bytes 307208 | tf_op jit(solution)/shard_map/ppermute | solution.py:335
  20.6 1.0 %dynamic-slice_bitcast_fusion = (bf16[1,4,96,128]{3,2,1,0:T(8,128)(2,1)S(1)}, bf16[1,4,96,128]{3,2,1,0:T(8,128)(2,1)S(1)}) fusion(bf16[4,2,96,128]{3,2,1,0:T(8,128)(2,1)} %bitcast.42, s32[]{:T(128)S(6)} %select_n.106, s32[]{:T(128)S(6)} %select_n.112), kind=kLoop, calls=%fused_computation.5 | loop fusion | bytes 393224 | tf_op jit(solution)/shard_map/stack | solution.py:358
  22.1 1.4 %collective-permute-done.5 = bf16[400,128]{1,0:T(8,128)(2,1)S(1)} collective-permute-done((bf16[400,128]{1,0:T(8,128)(2,1)}, bf16[400,128]{1,0:T(8,128)(2,1)S(1)}, u32[]{:S(2)}, u32[]{:S(2)}) %collective-permute-start.5) | collective-permute-done | bytes 102432 | tf_op jit(solution)/shard_map/ppermute | solution.py:335
  23.5 1.1 %collective-permute-done.4 = bf16[400,128]{1,0:T(8,128)(2,1)S(1)} collective-permute-done((bf16[400,128]{1,0:T(8,128)(2,1)}, bf16[400,128]{1,0:T(8,128)(2,1)S(1)}, u32[]{:S(2)}, u32[]{:S(2)}) %collective-permute-start.4) | collective-permute-done | bytes 102432 | tf_op jit(solution)/shard_map/ppermute | solution.py:335
  24.9 0.9 %select_select_fusion.2.mine_ref = bf16[400,128]{1,0:T(8,128)(2,1)S(1)} fusion(bf16[400,128]{1,0:T(8,128)(2,1)S(1)} %collective-permute-done.4, bf16[400,128]{1,0:T(8,128)(2,1)S(1)} %collective-permute-done.5, bf16[400,128]{1,0:T(8,128)(2,1)} %gather_first.1, bf16[400,128]{1,0:T(8,128)(2,1)S(1)} %collective-permute-done.3, pred[]{:T(512)S(6)} %select_n.108, ...), kind=kLoop, calls=%fused_computation.4 | loop fusion | flops 153600 | bytes 512003 | tf_op jit(solution)/shard_map/select_n | solution.py:352
  25.9 0.8 %collective-permute-start.15 = (bf16[4,4,96,128]{3,2,1,0:T(8,128)(2,1)S(1)}, bf16[4,4,96,128]{3,2,1,0:T(8,128)(2,1)S(1)}, u32[]{:S(2)}, u32[]{:S(2)}) collective-permute-start(bf16[4,4,96,128]{3,2,1,0:T(8,128)(2,1)S(1)} %pad_maximum_fusion.refs_0_), channel_id=1, source_target_pairs={{0,24},{8,16},{16,8},{24,0},{1,25},{9,17},{17,9},{25,1},{2,26},{10... | collective-permute-start | bytes 1179656 | tf_op jit(solution)/shard_map/ppermute | solution.py:335
  27.2 2.3 %collective-permute-start.13 = (bf16[4,4,96,128]{3,2,1,0:T(8,128)(2,1)S(1)}, bf16[4,4,96,128]{3,2,1,0:T(8,128)(2,1)S(1)}, u32[]{:S(2)}, u32[]{:S(2)}) collective-permute-start(bf16[4,4,96,128]{3,2,1,0:T(8,128)(2,1)S(1)} %pad_maximum_fusion.refs_0_), channel_id=1, source_target_pairs={{0,8},{8,0},{16,24},{24,16},{1,9},{9,1},{17,25},{25,17},{2,10},{10... | collective-permute-start | bytes 1179656 | tf_op jit(solution)/shard_map/ppermute | solution.py:335
  29.4 1.3 %collective-permute-done.6.sib_ref = bf16[400,128]{1,0:T(8,128)(2,1)S(1)} collective-permute-done((bf16[400,128]{1,0:T(8,128)(2,1)S(1)}, bf16[400,128]{1,0:T(8,128)(2,1)S(1)}, u32[]{:S(2)}, u32[]{:S(2)}) %collective-permute-start.6) | collective-permute-done | bytes 102432 | tf_op jit(solution)/shard_map/ppermute | solution.py:338
  30.7 1.9 %collective-permute-start.10 = (bf16[4,96,128]{2,1,0:T(8,128)(2,1)S(1)}, bf16[4,96,128]{2,1,0:T(8,128)(2,1)S(1)}, u32[]{:S(2)}, u32[]{:S(2)}) collective-permute-start(bf16[4,96,128]{2,1,0:T(8,128)(2,1)S(1)} %get-tuple-element.25), channel_id=1, source_target_pairs={{0,6},{1,7},{2,4},{3,5},{4,2},{5,3},{6,0},{7,1},{8,14},{9,15},{10,... | collective-permute-start | bytes 294920 | tf_op jit(solution)/shard_map/ppermute | solution.py:338
  32.6 2.5 %collective-permute-start.9 = (bf16[4,96,128]{2,1,0:T(8,128)(2,1)S(1)}, bf16[4,96,128]{2,1,0:T(8,128)(2,1)S(1)}, u32[]{:S(2)}, u32[]{:S(2)}) collective-permute-start(bf16[4,96,128]{2,1,0:T(8,128)(2,1)S(1)} %get-tuple-element.25), channel_id=1, source_target_pairs={{0,4},{1,5},{2,6},{3,7},{4,0},{5,1},{6,2},{7,3},{8,12},{9,13},{10,... | collective-permute-start | bytes 294920 | tf_op jit(solution)/shard_map/ppermute | solution.py:338
  35.1 8.1 %first_tile.1 = (f32[128,128]{1,0:T(8,128)}, bf16[128,768]{1,0:T(8,128)(2,1)}, bf16[768,256]{1,0:T(8,128)(2,1)}, f32[8,128]{1,0:T(8,128)}, f32[128,128]{1,0:T(8,128)}) custom-call(f32[6,128]{1,0:T(8,128)} %bitcast.34, bf16[400,128]{1,0:T(8,128)(2,1)} %copy-done.9, bf16[400,128]{1,0:T(8,128)(2,1)} %copy-done.10), custom_call_target="tpu_custom_call" | custom-call | tf_op jit(solution)/shard_map/first_tile/pallas_call | solution.py:161
  44.7 0.9 %collective-permute-done.11.refs_1_ = bf16[4,4,96,128]{3,2,1,0:T(8,128)(2,1)S(1)} collective-permute-done((bf16[4,4,96,128]{3,2,1,0:T(8,128)(2,1)S(1)}, bf16[4,4,96,128]{3,2,1,0:T(8,128)(2,1)S(1)}, u32[]{:S(2)}, u32[]{:S(2)}) %collective-permute-start.11) | collective-permute-done | bytes 393248 | tf_op jit(solution)/shard_map/ppermute | solution.py:338
  46.2 4.2 %rows.1 = (f32[8,128,128]{2,1,0:T(8,128)}, bf16[1024,768]{1,0:T(8,128)(2,1)S(1)}, f32[1024,128]{1,0:T(8,128)S(1)}) custom-call(f32[6,128]{1,0:T(8,128)S(1)} %bitcast.35, f32[128,128]{1,0:T(8,128)S(1)} %copy-done.2, bf16[768,256]{1,0:T(8,128)(2,1)S(1)} %copy-done.1, f32[8,128]{1,0:T(8,128)S(1)} %copy-done.7, f32[128,128]{1,0:T(8,128)S(1)} %copy-done.3, ...), custom_call_target="tpu_custom_call" | custom-call | tf_op jit(solution)/shard_map/rows/pallas_call | solution.py:240
  50.4 1.0 %copy-done = f32[8,128,128]{2,1,0:T(8,128)S(1)} copy-done((f32[8,128,128]{2,1,0:T(8,128)S(1)}, f32[8,128,128]{2,1,0:T(8,128)}, u32[]{:S(2)}) %copy-start) | copy-done | bytes 524312
  51.5 5.6 %trail.1 = f32[4096,128]{1,0:T(8,128)} custom-call(f32[6,128]{1,0:T(8,128)S(1)} %bitcast.36, f32[8,128]{1,0:T(8,128)S(1)} %copy-done.6, f32[128,128]{1,0:T(8,128)S(1)} %copy-done.2, bf16[128,768]{1,0:T(8,128)(2,1)S(1)} %copy-done.4, f32[8,128]{1,0:T(8,128)S(1)} %copy-done.7, f32[128,128]{1,0:T(8,128)S(1)} %copy-done.3, f32[8,128,128]{2,1,0:T(8,128)S(1)} %copy-done, ...), custom_call_target="tpu_custom_call" | custom-call | tf_op jit(solution)/shard_map/trail/pallas_call | solution.py:312
  (47 shorter events, 4.8 us)
Async XLA Ops:
  0.6 13.6 %collective-permute-start = (bf16[8,96,128]{2,1,0:T(8,128)(2,1)}, bf16[8,96,128]{2,1,0:T(8,128)(2,1)S(1)}, u32[]{:S(2)}, u32[]{:S(2)}) collective-permute-start(bf16[8,96,128]{2,1,0:T(8,128)(2,1)} %bitcast.38), channel_id=1, source_target_pairs={{0,2},{1,3},{2,0},{3,1},{4,6},{5,7},{6,4},{7,5},{8,10},{9,11},{10,... | collective-permute-start | bytes 589832 | tf_op jit(solution)/shard_map/ppermute | solution.py:338
  4.5 7.4 %collective-permute-start.2 = (bf16[96,128]{1,0:T(8,128)(2,1)S(1)}, bf16[96,128]{1,0:T(8,128)(2,1)S(1)}, u32[]{:S(2)}, u32[]{:S(2)}) collective-permute-start(bf16[96,128]{1,0:T(8,128)(2,1)S(1)} %slice_bitcast_fusion), channel_id=1, source_target_pairs={{0,6},{1,7},{2,4},{3,5},{4,2},{5,3},{6,0},{7,1},{8,14},{9,15},{10,... | collective-permute-start | bytes 73736 | tf_op jit(solution)/shard_map/ppermute | solution.py:338
  7.0 5.3 %collective-permute-start.1 = (bf16[96,128]{1,0:T(8,128)(2,1)S(1)}, bf16[96,128]{1,0:T(8,128)(2,1)S(1)}, u32[]{:S(2)}, u32[]{:S(2)}) collective-permute-start(bf16[96,128]{1,0:T(8,128)(2,1)S(1)} %slice_bitcast_fusion), channel_id=1, source_target_pairs={{0,4},{1,5},{2,6},{3,7},{4,0},{5,1},{6,2},{7,3},{8,12},{9,13},{10,... | collective-permute-start | bytes 73736 | tf_op jit(solution)/shard_map/ppermute | solution.py:338
  12.2 9.4 %collective-permute-start.8 = (bf16[4,96,128]{2,1,0:T(8,128)(2,1)S(1)}, bf16[4,96,128]{2,1,0:T(8,128)(2,1)S(1)}, u32[]{:S(2)}, u32[]{:S(2)}) collective-permute-start(bf16[4,96,128]{2,1,0:T(8,128)(2,1)S(1)} %get-tuple-element.23), channel_id=1, source_target_pairs={{0,6},{1,7},{2,4},{3,5},{4,2},{5,3},{6,0},{7,1},{8,14},{9,15},{10,... | collective-permute-start | bytes 294920 | tf_op jit(solution)/shard_map/ppermute | solution.py:338
  13.6 8.5 %collective-permute-start.7 = (bf16[4,96,128]{2,1,0:T(8,128)(2,1)S(1)}, bf16[4,96,128]{2,1,0:T(8,128)(2,1)S(1)}, u32[]{:S(2)}, u32[]{:S(2)}) collective-permute-start(bf16[4,96,128]{2,1,0:T(8,128)(2,1)S(1)} %get-tuple-element.23), channel_id=1, source_target_pairs={{0,4},{1,5},{2,6},{3,7},{4,0},{5,1},{6,2},{7,3},{8,12},{9,13},{10,... | collective-permute-start | bytes 294920 | tf_op jit(solution)/shard_map/ppermute | solution.py:338
  17.1 6.4 %collective-permute-start.5 = (bf16[400,128]{1,0:T(8,128)(2,1)}, bf16[400,128]{1,0:T(8,128)(2,1)S(1)}, u32[]{:S(2)}, u32[]{:S(2)}) collective-permute-start(bf16[400,128]{1,0:T(8,128)(2,1)} %gather_first.1), channel_id=1, source_target_pairs={{0,24},{8,16},{16,8},{24,0},{1,25},{9,17},{17,9},{25,1},{2,26},{10... | collective-permute-start | bytes 307208 | tf_op jit(solution)/shard_map/ppermute | solution.py:335
  19.6 5.0 %collective-permute-start.4 = (bf16[400,128]{1,0:T(8,128)(2,1)}, bf16[400,128]{1,0:T(8,128)(2,1)S(1)}, u32[]{:S(2)}, u32[]{:S(2)}) collective-permute-start(bf16[400,128]{1,0:T(8,128)(2,1)} %gather_first.1), channel_id=1, source_target_pairs={{0,16},{8,24},{16,0},{24,8},{1,17},{9,25},{17,1},{25,9},{2,18},{10... | collective-permute-start | bytes 307208 | tf_op jit(solution)/shard_map/ppermute | solution.py:335
  20.1 4.9 %collective-permute-start.3 = (bf16[400,128]{1,0:T(8,128)(2,1)}, bf16[400,128]{1,0:T(8,128)(2,1)S(1)}, u32[]{:S(2)}, u32[]{:S(2)}) collective-permute-start(bf16[400,128]{1,0:T(8,128)(2,1)} %gather_first.1), channel_id=1, source_target_pairs={{0,8},{8,0},{16,24},{24,16},{1,9},{9,1},{17,25},{25,17},{2,10},{10... | collective-permute-start | bytes 307208 | tf_op jit(solution)/shard_map/ppermute | solution.py:335
  22.1 24.0 %copy-start.5 = (f32[768]{0:T(1024)S(1)}, f32[768]{0:T(1024)}, u32[]{:S(2)}) copy-start(f32[768]{0:T(1024)} %param.4) | copy-start | bytes 9220
  25.9 9.3 %copy-start.9 = (bf16[400,128]{1,0:T(8,128)(2,1)}, bf16[400,128]{1,0:T(8,128)(2,1)S(1)}, u32[]{:S(2)}) copy-start(bf16[400,128]{1,0:T(8,128)(2,1)S(1)} %select_select_fusion.2.mine_ref) | copy-start | bytes 307204
  25.9 18.5 %collective-permute-start.15 = (bf16[4,4,96,128]{3,2,1,0:T(8,128)(2,1)S(1)}, bf16[4,4,96,128]{3,2,1,0:T(8,128)(2,1)S(1)}, u32[]{:S(2)}, u32[]{:S(2)}) collective-permute-start(bf16[4,4,96,128]{3,2,1,0:T(8,128)(2,1)S(1)} %pad_maximum_fusion.refs_0_), channel_id=1, source_target_pairs={{0,24},{8,16},{16,8},{24,0},{1,25},{9,17},{17,9},{25,1},{2,26},{10... | collective-permute-start | bytes 1179656 | tf_op jit(solution)/shard_map/ppermute | solution.py:335
  26.7 17.7 %collective-permute-start.14 = (bf16[4,4,96,128]{3,2,1,0:T(8,128)(2,1)S(1)}, bf16[4,4,96,128]{3,2,1,0:T(8,128)(2,1)S(1)}, u32[]{:S(2)}, u32[]{:S(2)}) collective-permute-start(bf16[4,4,96,128]{3,2,1,0:T(8,128)(2,1)S(1)} %pad_maximum_fusion.refs_0_), channel_id=1, source_target_pairs={{0,16},{8,24},{16,0},{24,8},{1,17},{9,25},{17,1},{25,9},{2,18},{10... | collective-permute-start | bytes 1179656 | tf_op jit(solution)/shard_map/ppermute | solution.py:335
  27.2 17.2 %collective-permute-start.13 = (bf16[4,4,96,128]{3,2,1,0:T(8,128)(2,1)S(1)}, bf16[4,4,96,128]{3,2,1,0:T(8,128)(2,1)S(1)}, u32[]{:S(2)}, u32[]{:S(2)}) collective-permute-start(bf16[4,4,96,128]{3,2,1,0:T(8,128)(2,1)S(1)} %pad_maximum_fusion.refs_0_), channel_id=1, source_target_pairs={{0,8},{8,0},{16,24},{24,16},{1,9},{9,1},{17,25},{25,17},{2,10},{10... | collective-permute-start | bytes 1179656 | tf_op jit(solution)/shard_map/ppermute | solution.py:335
  29.4 1.3 %collective-permute-start.6 = (bf16[400,128]{1,0:T(8,128)(2,1)S(1)}, bf16[400,128]{1,0:T(8,128)(2,1)S(1)}, u32[]{:S(2)}, u32[]{:S(2)}) collective-permute-start(bf16[400,128]{1,0:T(8,128)(2,1)S(1)} %select_select_fusion.2.mine_ref), channel_id=1, source_target_pairs={{0,1},{1,0},{2,3},{3,2},{4,5},{5,4},{6,7},{7,6},{8,9},{9,8},{10,11... | collective-permute-start | bytes 307208 | tf_op jit(solution)/shard_map/ppermute | solution.py:338
  30.7 4.4 %copy-start.10 = (bf16[400,128]{1,0:T(8,128)(2,1)}, bf16[400,128]{1,0:T(8,128)(2,1)S(1)}, u32[]{:S(2)}) copy-start(bf16[400,128]{1,0:T(8,128)(2,1)S(1)} %collective-permute-done.6.sib_ref) | copy-start | bytes 307204
  30.7 12.6 %collective-permute-start.10 = (bf16[4,96,128]{2,1,0:T(8,128)(2,1)S(1)}, bf16[4,96,128]{2,1,0:T(8,128)(2,1)S(1)}, u32[]{:S(2)}, u32[]{:S(2)}) collective-permute-start(bf16[4,96,128]{2,1,0:T(8,128)(2,1)S(1)} %get-tuple-element.25), channel_id=1, source_target_pairs={{0,6},{1,7},{2,4},{3,5},{4,2},{5,3},{6,0},{7,1},{8,14},{9,15},{10,... | collective-permute-start | bytes 294920 | tf_op jit(solution)/shard_map/ppermute | solution.py:338
  32.6 11.1 %collective-permute-start.9 = (bf16[4,96,128]{2,1,0:T(8,128)(2,1)S(1)}, bf16[4,96,128]{2,1,0:T(8,128)(2,1)S(1)}, u32[]{:S(2)}, u32[]{:S(2)}) collective-permute-start(bf16[4,96,128]{2,1,0:T(8,128)(2,1)S(1)} %get-tuple-element.25), channel_id=1, source_target_pairs={{0,4},{1,5},{2,6},{3,7},{4,0},{5,1},{6,2},{7,3},{8,12},{9,13},{10,... | collective-permute-start | bytes 294920 | tf_op jit(solution)/shard_map/ppermute | solution.py:338
  43.3 2.9 %copy-start.3 = (f32[128,128]{1,0:T(8,128)S(1)}, f32[128,128]{1,0:T(8,128)}, u32[]{:S(2)}) copy-start(f32[128,128]{1,0:T(8,128)} %get-tuple-element.22.diag_ref) | copy-start | bytes 196612
  43.3 2.9 %copy-start.7 = (f32[8,128]{1,0:T(8,128)S(1)}, f32[8,128]{1,0:T(8,128)}, u32[]{:S(2)}) copy-start(f32[8,128]{1,0:T(8,128)} %get-tuple-element.21.sq0_ref) | copy-start | bytes 12292
  43.8 6.6 %copy-start.4 = (bf16[128,768]{1,0:T(8,128)(2,1)S(1)}, bf16[128,768]{1,0:T(8,128)(2,1)}, u32[]{:S(2)}) copy-start(bf16[128,768]{1,0:T(8,128)(2,1)} %get-tuple-element.29.a_ref) | copy-start | bytes 589828
  43.8 6.6 %copy-start.6 = (f32[8,128]{1,0:T(8,128)S(1)}, f32[8,128]{1,0:T(8,128)}, u32[]{:S(2)}) copy-start(f32[8,128]{1,0:T(8,128)} %noise_ref.3) | copy-start | bytes 12292
  43.8 1.8 %collective-permute-start.11 = (bf16[4,4,96,128]{3,2,1,0:T(8,128)(2,1)S(1)}, bf16[4,4,96,128]{3,2,1,0:T(8,128)(2,1)S(1)}, u32[]{:S(2)}, u32[]{:S(2)}) collective-permute-start(bf16[4,4,96,128]{3,2,1,0:T(8,128)(2,1)S(1)} %pad_maximum_fusion.refs_0_), channel_id=1, source_target_pairs={{0,1},{1,0},{2,3},{3,2},{4,5},{5,4},{6,7},{7,6},{8,9},{9,8},{10,11... | collective-permute-start | bytes 1179656 | tf_op jit(solution)/shard_map/ppermute | solution.py:338
  43.9 2.2 %collective-permute-start.12 = (bf16[4,4,96,128]{3,2,1,0:T(8,128)(2,1)S(1)}, bf16[4,4,96,128]{3,2,1,0:T(8,128)(2,1)S(1)}, u32[]{:S(2)}, u32[]{:S(2)}) collective-permute-start(bf16[4,4,96,128]{3,2,1,0:T(8,128)(2,1)S(1)} %pad_maximum_fusion.1.refs_2_), channel_id=1, source_target_pairs={{0,1},{1,0},{2,3},{3,2},{4,5},{5,4},{6,7},{7,6},{8,9},{9,8},{10,11... | collective-permute-start | bytes 1179656 | tf_op jit(solution)/shard_map/ppermute | solution.py:338
  44.5 5.9 %collective-permute-start.16 = (bf16[4,4,96,128]{3,2,1,0:T(8,128)(2,1)S(1)}, bf16[4,4,96,128]{3,2,1,0:T(8,128)(2,1)S(1)}, u32[]{:S(2)}, u32[]{:S(2)}) collective-permute-start(bf16[4,4,96,128]{3,2,1,0:T(8,128)(2,1)S(1)} %get-tuple-element.32), channel_id=1, source_target_pairs={{0,1},{1,0},{2,3},{3,2},{4,5},{5,4},{6,7},{7,6},{8,9},{9,8},{10,11... | collective-permute-start | bytes 1179656 | tf_op jit(solution)/shard_map/ppermute | solution.py:338
  (6 other events, 11.7 us)

commit v3 on v0

--- a/solution.py
+++ b/solution.py
@@ -1,7 +1,391 @@
+import functools
+
 import jax
 import jax.numpy as jnp
 from jax import lax
+from jax.experimental import pallas as pl
+from jax.experimental.pallas import tpu as pltpu
 from jax.sharding import PartitionSpec as P
+
+LANES = 128
+VMEM_REST = 32
+ORDER = (0, 2, 4, 6, 1, 3, 5, 7)
+VM = pl.BlockSpec(memory_space=pltpu.VMEM)
+
+
+def nt(a, b, precision=None):
+    return lax.dot_general(
+        a, b, (((1,), (1,)), ((), ())), precision=precision, preferred_element_type=jnp.float32
+    )
+
+
+def split2(x):
+    hi = x.astype(jnp.bfloat16)
+    return hi, (x - hi.astype(jnp.float32)).astype(jnp.bfloat16)
+
+
+def split3(x):
+    hi, mid = split2(x)
+    rest = x - hi.astype(jnp.float32) - mid.astype(jnp.float32)
+    return hi, mid, rest.astype(jnp.bfloat16)
+
+
+def pack_kernel(feat_ref, both_ref, own_ref, oth_ref):
+    tiles, depth, width = feat_ref.shape
+    left = LANES - depth
+    parity = lax.axis_index("col") // lax.axis_size("row")
+    for half, out_ref in ((0, own_ref), (1, oth_ref)):
+        tile = [feat_ref[2 * k + (parity if half == 0 else 1 - parity)] for k in range(4)]
+        for k in range(3):
+            block = jnp.concatenate([tile[k], tile[3][left * k : left * (k + 1)]], axis=0).T
+            out_ref[k * width : (k + 1) * width, :] = block
+            both_ref[(3 * half + k) * width : (3 * half + k + 1) * width, :] = block
+
+
+def pack(feats):
+    width = feats.shape[2]
+    half = jax.ShapeDtypeStruct((3 * width, width), jnp.bfloat16)
+    return pl.pallas_call(
+        pack_kernel,
+        out_shape=(jax.ShapeDtypeStruct((6 * width, width), jnp.bfloat16), half, half),
+        in_specs=[VM],
+        out_specs=(VM,) * 3,
+        name="pack",
+    )(feats)
+
+
+def slice_weights(length_ref, depth):
+    col_id = lax.axis_index("col")
+    lane = lax.broadcasted_iota(jnp.int32, (8, LANES), 1)
+    row = lax.broadcasted_iota(jnp.int32, (8, LANES), 0)
+    held = jnp.ones((8, LANES), jnp.float32)
+    for s in range(8):
+        chunk, off = divmod(depth * s, LANES)
+        here = jnp.broadcast_to(length_ref[chunk : chunk + 1, :], (8, LANES))
+        if off:
+            here = pltpu.roll(here, LANES - off, 1)
+        if off + depth > LANES:
+            more = jnp.broadcast_to(length_ref[chunk + 1 : chunk + 2, :], (8, LANES))
+            here = jnp.where(lane < LANES - off, here, pltpu.roll(more, LANES - off, 1))
+        for place, k in enumerate(ORDER):
+            held = jnp.where((row == place) & (col_id == (s ^ k)), here, held)
+    inverse = 1.0 / held
+    columns = (inverse * inverse).T
+    return [columns[0:depth, s : s + 1] for s in range(8)]
+
+
+def bcast(v):
+    return jnp.broadcast_to(v, (8, LANES))
+
+
+def inverse_factor(tiles, rows, lanes, m=8, g=4):
+    size = 8 * len(tiles)
+    tiles, out = list(tiles), [None] * len(tiles)
+
+    def total(terms):
+        while len(terms) > 1:
+            terms = [sum(terms[z : z + 2]) for z in range(0, len(terms), 2)]
+        return terms[0]
+
+    for k in range(0, size, m):
+        b, j = divmod(k, 8)
+        r = [bcast(tiles[b][j + i : j + i + 1, :]) for i in range(m)]
+        s = [[bcast(r[i][:, k + l : k + l + 1]) if l >= i else None for l in range(m)] for i in range(m)]
+        r = [r[i] + jnp.where(lanes == k + i, 1.0, 0.0) for i in range(m)]
+        inv = [None] * m
+        for q in range(0, m, g):
+            scale, roots = None, []
+            for p in range(q, q + g):
+                product = s[p][p] if scale is None else scale * s[p][p]
+                root = lax.rsqrt(product)
+                inv[p] = root if scale is None else root * scale
+                roots.append(root)
+                for i in range(p + 1, q + g):
+                    for l in range(m - 1, i - 1, -1):
+                        s[i][l] = s[p][p] * s[i][l] - s[p][i] * s[p][l]
+                    r[i] = s[p][p] * r[i] - s[p][i] * r[p]
+                scale = product
+            for p in range(q, q + g):
+                r[p] = r[p] * roots[p - q]
+                for l in range(p + 1, m):
+                    s[p][l] = s[p][l] * roots[p - q]
+            for i in range(q + g, m):
+                for l in range(i, m):
+                    s[i][l] = s[i][l] - total([s[p][i] * s[p][l] for p in range(q, q + g)])
+                r[i] = r[i] - total([s[p][i] * r[p] for p in range(q, q + g)])
+        for i in range(m):
+            w = jnp.where(lanes < k + i, r[i], jnp.where(lanes == k + i, inv[i], 0.0))
+            out[b] = w if out[b] is None else jnp.where(rows == j + i, w, out[b])
+        if k + m >= size:
+            break
+        y = [r[i] * inv[i] for i in range(m)]
+        for i in range(m):
+            for l in range(i + 1, m):
+                s[i][l] = s[i][l] * inv[i]
+        for l in range(m - 1, 0, -1):
+            for i in range(l - 1, -1, -1):
+                y[i] = y[i] - s[i][l] * y[l]
+        for i in range(b, len(tiles)):
+            if i == b and j + m >= 8:
+                continue
+            terms = []
+            for q in range(m):
+                c = bcast(tiles[i][:, k + q : k + q + 1])
+                if i == b:
+                    c = jnp.where(rows > j + m - 1, c, 0.0)
+                terms.append(c * y[q])
+            tiles[i] = tiles[i] - total(terms)
+    return out
+
+
+def dense_rows(x, depth):
+    left = LANES - depth
+    blocks = []
+    for g in range(0, 8, 4):
+        for b in range(3):
+            blocks.append(x[(g + b) * depth : (g + b + 1) * depth])
+            last = (g + 3) * depth + left * b
+            blocks.append(x[last : last + left])
+    return jnp.concatenate(blocks, axis=0)
+
+
+def first_kernel(length_ref, mine_ref, sib_ref, inv_ref, both_ref, sq_ref, diag_ref, work):
+    width = inv_ref.shape[0]
+    depth = (mine_ref.shape[0] - 16) // 4
+    x = jnp.concatenate([ref[0 : 4 * depth, :] for ref in (mine_ref, sib_ref)], axis=0)
+    w = jnp.concatenate(slice_weights(length_ref, depth), axis=0)
+    xf = x.astype(jnp.float32)
+    xw = xf * w
+    parts = split3(xw)
+    both_ref[...] = dense_rows(jnp.concatenate(parts[:2], axis=1), depth)
+    turned = x.T
+    gram = sum(jnp.dot(turned, part, preferred_element_type=jnp.float32) for part in parts)
+    sq_row = jnp.sum(xf * xw, axis=0, keepdims=True)
+    sq_ref[...] = jnp.broadcast_to(sq_row, sq_ref.shape)
+    sq_col = jnp.broadcast_to(sq_row, (8, width)).T[:, 0:1]
+    tail = mine_ref[4 * depth :, :].astype(jnp.float32)
+    noise = tail[0:1, :] + tail[1:2, :] + tail[2:3, :]
+    i = lax.broadcasted_iota(jnp.int32, (width, width), 0)
+    j = lax.broadcasted_iota(jnp.int32, (width, width), 1)
+    diag = jnp.where(i == j, noise, 0.0)
+    diag_ref[...] = diag
+    work[...] = jnp.exp(-0.5 * (sq_col + sq_row - 2.0 * gram)) + diag
+    rows = lax.broadcasted_iota(jnp.int32, (8, LANES), 0)
+    lanes = lax.broadcasted_iota(jnp.int32, (8, LANES), 1)
+    tiles = [work[8 * t : 8 * t + 8, :] for t in range(width // 8)]
+    for t, tile in enumerate(inverse_factor(tiles, rows, lanes)):
+        inv_ref[8 * t : 8 * t + 8, :] = tile
+
+
+def first_tile(lengths, mine, sib):
+    width = mine.shape[1]
+    whole = 2 * (mine.shape[0] - 16)
+    return pl.pallas_call(
+        first_kernel,
+        out_shape=(
+            jax.ShapeDtypeStruct((width, width), jnp.float32),
+            jax.ShapeDtypeStruct((whole, 2 * width), jnp.bfloat16),
+            jax.ShapeDtypeStruct((8, width), jnp.float32),
+            jax.ShapeDtypeStruct((width, width), jnp.float32),
+        ),
+        in_specs=[VM] * 3,
+        out_specs=(VM,) * 4,
+        scratch_shapes=[pltpu.VMEM((width, width), jnp.float32)],
+        name="first_tile",
+    )(lengths, mine, sib)
+
+
+def dense(refs, t, width, depth):
+    left = LANES - depth
+    lane = lax.broadcasted_iota(jnp.int32, (width, LANES), 1)
+    blocks = []
+    for g in range(0, 8, 4):
+        if t < 3:
+            parts = [ref[t * width : (t + 1) * width, :] for ref in refs[g : g + 4]]
+            for b in range(3):
+                moved = pltpu.roll(parts[3], depth - left * b, 1)
+                blocks.append(jnp.where(lane < depth, parts[b], moved))
+        else:
+            for b in range(3):
+                block = refs[g + 3][b * width : (b + 1) * width, :]
+                for k in range(3):
+                    moved = pltpu.roll(
+                        refs[g + b][k * width : (k + 1) * width, :], LANES - depth + left * k, 1
+                    )
+                    block = jnp.where((lane >= left * k) & (lane < left * (k + 1)), moved, block)
+                blocks.append(block)
+    return jnp.concatenate(blocks, axis=1)
+
+
+def dense_weights(length_ref, depth):
+    parts = dense_rows(jnp.concatenate(slice_weights(length_ref, depth), axis=0), depth)
+    return jnp.broadcast_to(parts, (8 * depth, LANES)).T[0:1, :]
+
+
+def three(x):
+    hi, lo = split2(x)
+    return jnp.concatenate([hi, lo, hi], axis=1)
+
+
+def twice(y):
+    hi, lo = split2(y)
+    return jnp.concatenate([hi, hi, lo], axis=1)
+
+
+def rest_kernel(depth, length_ref, noise_ref, inv_ref, both_ref, sq0_ref, diag_ref, *refs):
+    row_refs, col_refs, (panel_ref, trail_ref) = refs[:9], refs[9:13], refs[13:]
+    width = inv_ref.shape[0]
+    h = 3 * width
+    w0, w1, p, q2, q3, s0, s1, sp, sq = row_refs
+    third = lambda ref, k: ref.at[pl.ds(k * h, h)]
+    row_own = [third(w0, 0), third(w1, 0), third(p, 1), third(p, 2)]
+    row_own += [third(s0, 0), third(s1, 0), third(sp, 1), third(sp, 2)]
+    row_oth = [third(w0, 1), third(w1, 1), q2, q3, third(s0, 1), third(s1, 1), third(sq, 0), third(sq, 1)]
+    cols = []
+    for near, far in (col_refs[0:2], col_refs[2:4]):
+        cols += [near, third(far, 0), third(far, 1), third(far, 2)]
+    row_id, col_id, n_rows = lax.axis_index("row"), lax.axis_index("col"), lax.axis_size("row")
+    parity, on_diag = col_id // n_rows, row_id == col_id % n_rows
+
+    w = dense_weights(length_ref, depth)
+    blocks = w.shape[1] // LANES
+
+    def squares(xf, xw):
+        partial = xf[:, 0:LANES] * xw[:, 0:LANES]
+        for s in range(1, blocks):
+            cut = slice(s * LANES, (s + 1) * LANES)
+            partial = partial + xf[:, cut] * xw[:, cut]
+        return partial
+
+    eye = lax.broadcasted_iota(jnp.int32, (width, width), 0) == lax.broadcasted_iota(
+        jnp.int32, (width, width), 1
+    )
+    inv = twice(inv_ref[...])
+    sq0 = sq0_ref[0:1, :]
+
+    def panel_of(x, sq, heads):
+        gram = jnp.dot(x, both_ref[...], preferred_element_type=jnp.float32)
+        gram = gram[:, 0:width] + gram[:, width:]
+        kern = jnp.exp(gram - 0.5 * (sq + sq0))
+        if heads:
+            tops = [
+                kern[h * width : (h + 1) * width] + jnp.where(c, diag_ref[...], 0.0)
+                for h, c in enumerate(heads)
+            ]
+            if len(heads) * width < kern.shape[0]:
+                tops.append(kern[len(heads) * width :])
+            kern = jnp.concatenate(tops, axis=0)
+        return nt(three(kern), inv)
+
+    c_hi, c_lo, c_sq, c_panel = [], [], [], []
+    for t in range(4):
+        c = dense(cols, t, width, depth)
+        cf = c.astype(jnp.float32)
+        cw = cf * w
+        partial = squares(cf, cw)
+        hi, lo = split2(cw)
+        c_hi.append(hi)
+        c_lo.append(lo)
+        c_sq.append(jnp.sum(partial.T, axis=0, keepdims=True))
+        sq = jnp.sum(partial, axis=1, keepdims=True)
+        c_panel.append(panel_of(c, sq, [col_id == 0] if t == 0 else []))
+    c_hi, c_lo = jnp.concatenate(c_hi, axis=0), jnp.concatenate(c_lo, axis=0)
+    c_sq = jnp.concatenate(c_sq, axis=1)
+    c_panel = twice(jnp.concatenate(c_panel, axis=0))
+
+    for t in range(4):
+        x = jnp.concatenate([dense(row_own, t, width, depth), dense(row_oth, t, width, depth)], axis=0)
+        xf = x.astype(jnp.float32)
+        sq = jnp.sum(squares(xf, xf * w), axis=1, keepdims=True)
+        heads = [(row_id == 0) & (parity == h) for h in range(2)] if t == 0 else []
+        panel = panel_of(x, sq, heads)
+        gram = nt(x, c_hi) + nt(x, c_lo)
+        kern = jnp.exp(gram - 0.5 * (sq + c_sq))
+        trail = kern - nt(three(panel), c_panel)
+        for half in range(2):
+            tile = 2 * t + (parity if half == 0 else 1 - parity)
+            low = half * width
+            panel_ref[tile] = panel[low : low + width]
+            for tc in range(4):
+                block = trail[low : low + width, tc * width : (tc + 1) * width]
+                if half == 0 and tc == t:
+                    block = block + jnp.where(eye & on_diag, noise_ref[pl.ds(tile, 1), :], 0.0)
+                trail_ref[pl.ds(tile * (4 * width) + tc, width, stride=4), :] = block
+
+
+def rest(depth, lengths, noise, first, *slices):
+    tiles, width = noise.shape
+    return pl.pallas_call(
+        functools.partial(rest_kernel, depth),
+        out_shape=(
+            jax.ShapeDtypeStruct((tiles, width, width), jnp.float32),
+            jax.ShapeDtypeStruct((tiles * width * 4, width), jnp.float32),
+        ),
+        in_specs=[VM] * 19,
+        out_specs=(VM, VM),
+        compiler_params=pltpu.CompilerParams(vmem_limit_bytes=VMEM_REST * 1024 * 1024),
+        name="rest",
+    )(lengths, noise, *first, *slices)
+
+
+def noise_parts(noise):
+    rest, parts = noise[0:1], []
+    for _ in range(3):
+        part = lax.reduce_precision(rest, 8, 7)
+        parts.append(part.astype(jnp.bfloat16))
+        rest = rest - part
+    return jnp.concatenate(parts + [jnp.zeros((13, noise.shape[1]), jnp.bfloat16)], axis=0)
+
+
+def body(features, lengthscale, noise):
+    tiles, width, depth = features.shape
+    row_id = lax.axis_index("row")
+    col_id = lax.axis_index("col")
+    n_rows, n_cols = lax.axis_size("row"), lax.axis_size("col")
+    home = col_id % n_rows
+    parity = col_id // n_rows
+
+    def over_row(x, k):
+        return lax.ppermute(x, "row", [(i, i ^ k) for i in range(n_rows)])
+
+    def over_col(x, k):
+        return lax.ppermute(x, "col", [(i, i ^ k) for i in range(n_cols)])
+
+    feats = jnp.transpose(features, (0, 2, 1))
+    lengths = lengthscale.reshape(-1, LANES)
+
+    def after(x, *others):
+        return lax.optimization_barrier((x, *others))[0]
+
+    head = feats[0]
+    far = [over_col(head, 2 * k) for k in (1, 2, 3)]
+    both, own, oth = pack(after(feats, head))
+    both, oth, *far = lax.optimization_barrier((both, oth, *far))
+    near, p2, p3 = over_col(both, 2), over_col(oth, 4), over_col(oth, 6)
+    size, low = own.shape[0], 4 * depth + 16
+    early = jnp.concatenate([head] + far + [noise_parts(noise), own], axis=0)
+    early = [early] + [over_row(early, k) for k in (1, 2, 3)]
+    *early, p2, p3 = lax.optimization_barrier((*early, p2, p3))
+    stack = lax.select_n(row_id, *[v[:low] for v in early])
+    sib = over_col(stack, 1)
+    p = jnp.concatenate([near[:size], p2, p3], axis=0)
+    planes = [p] + [over_row(p, k) for k in (1, 2, 3)]
+    own_late = after(own, sib)
+    q2, q3 = over_col(own_late, 4), over_col(own_late, 6)
+    first = first_tile(lengths, stack, sib)
+    q2, q3, *planes, sib_both, sib_near, sib_p, _ = lax.optimization_barrier(
+        (q2, q3, *planes, both, near, p, first[0])
+    )
+    sib_both, sib_near, sib_p = (over_col(v, 1) for v in (sib_both, sib_near, sib_p))
+    sib_q = over_col(jnp.concatenate([q2, q3], axis=0), 1)
+    early = [v[low:] for v in early]
+    take = lambda k: [lax.select_n(k, *v) for v in (early, planes)]
+    keep = take(row_id ^ home)
+    give = [over_col(v, 1) for v in take(row_id ^ home ^ 1)]
+    panel, trailing = rest(
+        depth, lengths, noise, first, both, near, p, q2, q3, sib_both, sib_near, sib_p, sib_q, *keep, *give
+    )
+    return panel, trailing.reshape(tiles, width, 4, width)
 
 
 def from_root(block, axis, holder):
@@ -9,12 +393,7 @@
     return lax.psum(block, axis)
 
 
-def kernel_block(left, left_sq, right, right_sq):
-    gram = jnp.dot(left, right.T, precision=lax.Precision.HIGHEST)
-    return jnp.exp(-0.5 * (left_sq[:, None] + right_sq[None, :] - 2.0 * gram))
-
-
-def body(features, lengthscale, noise):
+def general_body(features, lengthscale, noise):
     rows_axis = lax.axis_size("row")
     cols_axis = lax.axis_size("col")
     row_id = lax.axis_index("row")
@@ -35,16 +414,14 @@
     right_sq = jnp.sum(right * right, axis=1)
     inner = jnp.arange(width, dtype=jnp.int32)
     row_index = (
-        (jnp.arange(tiles_row, dtype=jnp.int32)[:, None] * rows_axis + row_id) * width
-        + inner[None, :]
+        (jnp.arange(tiles_row, dtype=jnp.int32)[:, None] * rows_axis + row_id) * width + inner[None, :]
     ).reshape(-1)
     col_index = (
-        (jnp.arange(tiles_col, dtype=jnp.int32)[:, None] * cols_axis + col_id) * width
-        + inner[None, :]
+        (jnp.arange(tiles_col, dtype=jnp.int32)[:, None] * cols_axis + col_id) * width + inner[None, :]
     ).reshape(-1)
-    noise_rows = noise.reshape(-1)
-    kern = kernel_block(left, left_sq, right, right_sq)
-    kern = kern + jnp.where(row_index[:, None] == col_index[None, :], noise_rows[:, None], 0.0)
+    gram = jnp.dot(left, right.T, precision=lax.Precision.HIGHEST)
+    kern = jnp.exp(-0.5 * (left_sq[:, None] + right_sq[None, :] - 2.0 * gram))
+    kern = kern + jnp.where(row_index[:, None] == col_index[None, :], noise.reshape(-1)[:, None], 0.0)
     diag_tile = from_root(kern[:width, :width], "row", 0)
     factor = jnp.linalg.cholesky(diag_tile)
     own_rows = jax.scipy.linalg.solve_triangular(factor, kern[:, :width].T, lower=True).T
@@ -61,8 +438,9 @@
 
 def solution(mesh):
     placed = (P(None, "row", "col"), P(), P(None, "row"))
+    small = mesh.shape["row"] == 4 and mesh.shape["col"] == 8
     return jax.shard_map(
-        body,
+        body if small else general_body,
         mesh=mesh,
         in_specs=placed,
         out_specs=(P(None, "row", None), P(None, "row", None, "col")),

time: 282 us -> 53.9 us (0.19)
  waiting for transfers between devices: 217 us -> 14.7 us
  other arithmetic: 30.7 us -> 0.86 us
  starting transfers between devices: 0.39 us -> 19.8 us
  Pallas kernels: 0 us -> 15.5 us
  between operations: 13.9 us -> 0.81 us
  matrix products: 12.4 us -> 0 us
  local copies, waits for them, and re-layouts: 7.25 us -> 1.88 us
    psum x4 -> x0, waiting for transfers between devices: 188 us -> none  [from_root(): return lax.psum(block, axis)]
    all_gather x1 -> x0, waiting for transfers between devices: 28.9 us -> none  [body(): row_feats = lax.all_gather(features, 'col', axis=2, tiled=True)]
    another operation x5 -> x0, other arithmetic: 22.9 us -> none  [the longest x3 12.4 us: body(): factor = jnp.linalg.cholesky(diag_tile)]
    ppermute x0 -> x21, starting transfers between devices: none -> 19.8 us  [the longest x15 12.7 us: over_col(): return lax.ppermute(x, 'col', [(i, i ^ k) for i in range(n_cols)])]
    pallas_call x0 -> x3, Pallas kernels: none -> 15.5 us  [the longest x1 7.27 us: rest(): pl.pallas_call(functools.partial(rest_kernel, depth), out_shape=(jax.Shap...]
    ppermute x0 -> x21, waiting for transfers between devices: none -> 14.7 us  [the longest x15 12 us: over_col(): return lax.ppermute(x, 'col', [(i, i ^ k) for i in range(n_cols)])]
    dot_general x2 -> x0, matrix products: 11 us -> none  [the longest x1 7.41 us: kernel_block(): gram = jnp.dot(left, right.T, precision=lax.Precision.HIGHEST)]
    reduce_sum x2 -> x0, other arithmetic: 3.48 us -> none  [the longest x1 2.07 us: body(): left_sq = jnp.sum(left * left, axis=1)]
  transfers between devices with their start and end apart: 5 -> 21, of which waited for: 5 -> 9; matrix products, arithmetic and copies ran while one was open for 1% -> 4% of each run, Pallas kernels for 0% -> 15%
where the time goes in v3:
time: 53.9 us; the launch traced here: 53.6 us
  starting transfers between devices  19.8 us (37%)
  Pallas kernels  15.5 us (29%)
  waiting for transfers between devices  14.7 us (27%)
  local copies, waits for them, and re-layouts  1.88 us (3%)
  other arithmetic  0.86 us (2%)
  between operations  0.81 us (2%)
    ppermute x15, starting transfers between devices, over_col(): return lax.ppermute(x, 'col', [(i, i ^ k) for i in range(n_cols)])  12.7 us
    ppermute x15, waiting for transfers between devices, over_col(): return lax.ppermute(x, 'col', [(i, i ^ k) for i in range(n_cols)])  12 us
    pallas_call x1, Pallas kernels, rest(): pl.pallas_call(functools.partial(rest_kernel, depth), out_shape=(jax.Shap...  7.27 us
    ppermute x6, starting transfers between devices, over_row(): return lax.ppermute(x, 'row', [(i, i ^ k) for i in range(n_rows)])  7.11 us
    pallas_call x1, Pallas kernels, first_tile(): pl.pallas_call(first_kernel, out_shape=(jax.ShapeDtypeStruct((width, widt...  6.52 us
    ppermute x6, waiting for transfers between devices, over_row(): return lax.ppermute(x, 'row', [(i, i ^ k) for i in range(n_rows)])  2.66 us
    pallas_call x1, Pallas kernels, pack(): pl.pallas_call(pack_kernel, out_shape=(jax.ShapeDtypeStruct((6 * width, w...  1.76 us
    concatenate x1, local copies, waits for them, and re-layouts, body(): early = jnp.concatenate([head] + far + [noise_parts(noise), own], axis=0)  1.08 us
  transfers between devices with their start and end apart: 21, of which 9 were waited for; matrix products, arithmetic and copies ran while one was open for 4% of the time, Pallas kernels for 15%

profile of v3, /device:TPU:0, one launch (start us, length us, event | category | flops | bytes accessed | tf_op | source)
XLA Modules:
  0.0 53.6 jit_solution(17662026988949644442)
XLA Ops:
  0.6 0.7 %slice_bitcast_fusion = bf16[96,128]{1,0:T(8,128)(2,1)S(1)} fusion(bf16[8,96,128]{2,1,0:T(8,128)(2,1)} %bitcast.7), kind=kLoop, calls=%fused_computation.7 | loop fusion | bytes 49152 | tf_op jit(solution)/shard_map/squeeze | solution.py:360
  1.4 5.0 %collective-permute-start.2 = (bf16[96,128]{1,0:T(8,128)(2,1)S(1)}, bf16[96,128]{1,0:T(8,128)(2,1)S(1)}, u32[]{:S(2)}, u32[]{:S(2)}) collective-permute-start(bf16[96,128]{1,0:T(8,128)(2,1)S(1)} %slice_bitcast_fusion), channel_id=1, source_target_pairs={{0,6},{1,7},{2,4},{3,5},{4,2},{5,3},{6,0},{7,1},{8,14},{9,15},{10,... | collective-permute-start | bytes 73736 | tf_op jit(solution)/shard_map/ppermute | solution.py:352
  6.4 0.6 %collective-permute-start = (bf16[96,128]{1,0:T(8,128)(2,1)S(1)}, bf16[96,128]{1,0:T(8,128)(2,1)S(1)}, u32[]{:S(2)}, u32[]{:S(2)}) collective-permute-start(bf16[96,128]{1,0:T(8,128)(2,1)S(1)} %slice_bitcast_fusion), channel_id=1, source_target_pairs={{0,2},{1,3},{2,0},{3,1},{4,6},{5,7},{6,4},{7,5},{8,10},{9,11},{10,... | collective-permute-start | bytes 73736 | tf_op jit(solution)/shard_map/ppermute | solution.py:352
  7.0 1.8 %pack.1 = (bf16[768,128]{1,0:T(8,128)(2,1)}, bf16[384,128]{1,0:T(8,128)(2,1)}, bf16[384,128]{1,0:T(8,128)(2,1)}) custom-call(bf16[8,96,128]{2,1,0:T(8,128)(2,1)} %bitcast.8), custom_call_target="tpu_custom_call" | custom-call | tf_op jit(solution)/shard_map/pack/pallas_call | solution.py:48
  8.8 2.4 %collective-permute-done.1 = bf16[96,128]{1,0:T(8,128)(2,1)S(1)} collective-permute-done((bf16[96,128]{1,0:T(8,128)(2,1)S(1)}, bf16[96,128]{1,0:T(8,128)(2,1)S(1)}, u32[]{:S(2)}, u32[]{:S(2)}) %collective-permute-start.1) | collective-permute-done | bytes 24608 | tf_op jit(solution)/shard_map/ppermute | solution.py:352
  11.2 0.7 %fusion.1 = (bf16[1,128]{1,0:T(2,128)(2,1)S(1)}, bf16[1,128]{1,0:T(2,128)(2,1)S(1)}, bf16[1,128]{1,0:T(2,128)(2,1)S(1)}) fusion(f32[8,128]{1,0:T(8,128)} %noise_ref.1), kind=kLoop, calls=%fused_computation.13 | loop fusion | flops 1024 | bytes 1280 | tf_op jit(solution)/shard_map/convert_element_type | solution.py:335
  11.9 1.1 %concatenate.9 = bf16[784,128]{1,0:T(8,128)(2,1)S(1)} concatenate(bf16[96,128]{1,0:T(8,128)(2,1)S(1)} %slice_bitcast_fusion, bf16[96,128]{1,0:T(8,128)(2,1)S(1)} %collective-permute-done, bf16[96,128]{1,0:T(8,128)(2,1)S(1)} %collective-permute-done.1, bf16[96,128]{1,0:T(8,128)(2,1)S(1)} %collective-permute-done.2, bf16[1,128]{1,0:T(2,128)(2,1)S(1)} %get-tuple-element.70, ...), dimensions={0} | concatenate | bytes 401408 | tf_op jit(solution)/shard_map/concatenate | solution.py:366
  12.9 2.5 %collective-permute-start.5 = (bf16[784,128]{1,0:T(8,128)(2,1)S(1)}, bf16[784,128]{1,0:T(8,128)(2,1)S(1)}, u32[]{:S(2)}, u32[]{:S(2)}) collective-permute-start(bf16[784,128]{1,0:T(8,128)(2,1)S(1)} %concatenate.9), channel_id=1, source_target_pairs={{0,24},{8,16},{16,8},{24,0},{1,25},{9,17},{17,9},{25,1},{2,26},{10... | collective-permute-start | bytes 602120 | tf_op jit(solution)/shard_map/ppermute | solution.py:349
  15.5 0.5 collective-permute-start.4
  16.0 0.5 collective-permute-start.3
  16.5 3.5 %collective-permute-start.7 = (bf16[384,128]{1,0:T(8,128)(2,1)}, bf16[384,128]{1,0:T(8,128)(2,1)S(1)}, u32[]{:S(2)}, u32[]{:S(2)}) collective-permute-start(bf16[384,128]{1,0:T(8,128)(2,1)} %get-tuple-element.40), channel_id=1, source_target_pairs={{0,6},{1,7},{2,4},{3,5},{4,2},{5,3},{6,0},{7,1},{8,14},{9,15},{10,... | collective-permute-start | bytes 294920 | tf_op jit(solution)/shard_map/ppermute | solution.py:352
  20.0 3.2 %collective-permute-done.7 = bf16[384,128]{1,0:T(8,128)(2,1)S(1)} collective-permute-done((bf16[384,128]{1,0:T(8,128)(2,1)}, bf16[384,128]{1,0:T(8,128)(2,1)S(1)}, u32[]{:S(2)}, u32[]{:S(2)}) %collective-permute-start.7) | collective-permute-done | bytes 98336 | tf_op jit(solution)/shard_map/ppermute | solution.py:352
  23.2 3.2 %collective-permute-done.6 = bf16[384,128]{1,0:T(8,128)(2,1)S(1)} collective-permute-done((bf16[384,128]{1,0:T(8,128)(2,1)}, bf16[384,128]{1,0:T(8,128)(2,1)S(1)}, u32[]{:S(2)}, u32[]{:S(2)}) %collective-permute-start.6) | collective-permute-done | bytes 98336 | tf_op jit(solution)/shard_map/ppermute | solution.py:352
  26.6 2.5 %collective-permute-start.14 = (bf16[1152,128]{1,0:T(8,128)(2,1)S(1)}, bf16[1152,128]{1,0:T(8,128)(2,1)S(1)}, u32[]{:S(2)}, u32[]{:S(2)}) collective-permute-start(bf16[1152,128]{1,0:T(8,128)(2,1)S(1)} %pad_maximum_fusion.refs_2_), channel_id=1, source_target_pairs={{0,24},{8,16},{16,8},{24,0},{1,25},{9,17},{17,9},{25,1},{2,26},{10... | collective-permute-start | bytes 884744 | tf_op jit(solution)/shard_map/ppermute | solution.py:349
  29.1 0.5 collective-permute-start.13
  29.7 0.5 collective-permute-start.12
  30.2 2.2 %collective-permute-start.11 = (bf16[384,128]{1,0:T(8,128)(2,1)}, bf16[384,128]{1,0:T(8,128)(2,1)S(1)}, u32[]{:S(2)}, u32[]{:S(2)}) collective-permute-start(bf16[384,128]{1,0:T(8,128)(2,1)} %get-tuple-element.52), channel_id=1, source_target_pairs={{0,6},{1,7},{2,4},{3,5},{4,2},{5,3},{6,0},{7,1},{8,14},{9,15},{10,... | collective-permute-start | bytes 294920 | tf_op jit(solution)/shard_map/ppermute | solution.py:352
  32.5 6.5 %first_tile.1 = (f32[128,128]{1,0:T(8,128)}, bf16[768,256]{1,0:T(8,128)(2,1)}, f32[8,128]{1,0:T(8,128)}, f32[128,128]{1,0:T(8,128)}) custom-call(f32[6,128]{1,0:T(8,128)} %bitcast.5, bf16[400,128]{1,0:T(8,128)(2,1)} %copy-done.7, bf16[400,128]{1,0:T(8,128)(2,1)} %copy-done.8), custom_call_target="tpu_custom_call" | custom-call | tf_op jit(solution)/shard_map/first_tile/pallas_call | solution.py:183
  39.1 1.7 %collective-permute-done.10.refs_3_ = bf16[384,128]{1,0:T(8,128)(2,1)S(1)} collective-permute-done((bf16[384,128]{1,0:T(8,128)(2,1)}, bf16[384,128]{1,0:T(8,128)(2,1)S(1)}, u32[]{:S(2)}, u32[]{:S(2)}) %collective-permute-start.10) | collective-permute-done | bytes 98336 | tf_op jit(solution)/shard_map/ppermute | solution.py:352
  40.8 2.6 %collective-permute-done.13 = bf16[1152,128]{1,0:T(8,128)(2,1)S(1)} collective-permute-done((bf16[1152,128]{1,0:T(8,128)(2,1)S(1)}, bf16[1152,128]{1,0:T(8,128)(2,1)S(1)}, u32[]{:S(2)}, u32[]{:S(2)}) %collective-permute-start.13) | collective-permute-done | bytes 294944 | tf_op jit(solution)/shard_map/ppermute | solution.py:349
  43.5 0.6 %collective-permute-start.20 = (bf16[1152,128]{1,0:T(8,128)(2,1)S(1)}, bf16[1152,128]{1,0:T(8,128)(2,1)S(1)}, u32[]{:S(2)}, u32[]{:S(2)}) collective-permute-start(bf16[1152,128]{1,0:T(8,128)(2,1)S(1)} %get-tuple-element.64), channel_id=1, source_target_pairs={{0,1},{1,0},{2,3},{3,2},{4,5},{5,4},{6,7},{7,6},{8,9},{9,8},{10,11... | collective-permute-start | bytes 884744 | tf_op jit(solution)/shard_map/ppermute | solution.py:352
  44.2 0.5 collective-permute-start.15
  44.8 1.0 %collective-permute-done.18.refs_8_ = bf16[768,128]{1,0:T(8,128)(2,1)S(1)} collective-permute-done((bf16[768,128]{1,0:T(8,128)(2,1)S(1)}, bf16[768,128]{1,0:T(8,128)(2,1)S(1)}, u32[]{:S(2)}, u32[]{:S(2)}) %collective-permute-start.18) | collective-permute-done | bytes 196640 | tf_op jit(solution)/shard_map/ppermute | solution.py:352
  46.3 7.3 %rest.1 = (f32[8,128,128]{2,1,0:T(8,128)}, f32[4096,128]{1,0:T(8,128)}) custom-call(f32[6,128]{1,0:T(8,128)S(1)} %bitcast.6, f32[8,128]{1,0:T(8,128)S(1)} %copy-done.5, f32[128,128]{1,0:T(8,128)S(1)} %copy-done.2, bf16[768,256]{1,0:T(8,128)(2,1)S(1)} %copy-done, f32[8,128]{1,0:T(8,128)S(1)} %copy-done.6, f32[128,128]{1,0:T(8,128)S(1)} %copy-done.3, ...), custom_call_target="tpu_custom_call" | custom-call | tf_op jit(solution)/shard_map/rest/pallas_call | solution.py:318
  (49 shorter events, 1.2 us)
Async XLA Ops:
  1.4 7.4 %collective-permute-start.2 = (bf16[96,128]{1,0:T(8,128)(2,1)S(1)}, bf16[96,128]{1,0:T(8,128)(2,1)S(1)}, u32[]{:S(2)}, u32[]{:S(2)}) collective-permute-start(bf16[96,128]{1,0:T(8,128)(2,1)S(1)} %slice_bitcast_fusion), channel_id=1, source_target_pairs={{0,6},{1,7},{2,4},{3,5},{4,2},{5,3},{6,0},{7,1},{8,14},{9,15},{10,... | collective-permute-start | bytes 73736 | tf_op jit(solution)/shard_map/ppermute | solution.py:352
  6.4 4.7 %collective-permute-start.1 = (bf16[96,128]{1,0:T(8,128)(2,1)S(1)}, bf16[96,128]{1,0:T(8,128)(2,1)S(1)}, u32[]{:S(2)}, u32[]{:S(2)}) collective-permute-start(bf16[96,128]{1,0:T(8,128)(2,1)S(1)} %slice_bitcast_fusion), channel_id=1, source_target_pairs={{0,4},{1,5},{2,6},{3,7},{4,0},{5,1},{6,2},{7,3},{8,12},{9,13},{10,... | collective-permute-start | bytes 73736 | tf_op jit(solution)/shard_map/ppermute | solution.py:352
  6.4 4.7 %collective-permute-start = (bf16[96,128]{1,0:T(8,128)(2,1)S(1)}, bf16[96,128]{1,0:T(8,128)(2,1)S(1)}, u32[]{:S(2)}, u32[]{:S(2)}) collective-permute-start(bf16[96,128]{1,0:T(8,128)(2,1)S(1)} %slice_bitcast_fusion), channel_id=1, source_target_pairs={{0,2},{1,3},{2,0},{3,1},{4,6},{5,7},{6,4},{7,5},{8,10},{9,11},{10,... | collective-permute-start | bytes 73736 | tf_op jit(solution)/shard_map/ppermute | solution.py:352
  11.2 8.8 %collective-permute-start.9 = (bf16[768,128]{1,0:T(8,128)(2,1)}, bf16[768,128]{1,0:T(8,128)(2,1)S(1)}, u32[]{:S(2)}, u32[]{:S(2)}) collective-permute-start(bf16[768,128]{1,0:T(8,128)(2,1)} %get-tuple-element.55.refs_0_), channel_id=1, source_target_pairs={{0,2},{1,3},{2,0},{3,1},{4,6},{5,7},{6,4},{7,5},{8,10},{9,11},{10,... | collective-permute-start | bytes 589832 | tf_op jit(solution)/shard_map/ppermute | solution.py:352
  12.9 13.5 %collective-permute-start.5 = (bf16[784,128]{1,0:T(8,128)(2,1)S(1)}, bf16[784,128]{1,0:T(8,128)(2,1)S(1)}, u32[]{:S(2)}, u32[]{:S(2)}) collective-permute-start(bf16[784,128]{1,0:T(8,128)(2,1)S(1)} %concatenate.9), channel_id=1, source_target_pairs={{0,24},{8,16},{16,8},{24,0},{1,25},{9,17},{17,9},{25,1},{2,26},{10... | collective-permute-start | bytes 602120 | tf_op jit(solution)/shard_map/ppermute | solution.py:349
  15.5 11.0 %collective-permute-start.4 = (bf16[784,128]{1,0:T(8,128)(2,1)S(1)}, bf16[784,128]{1,0:T(8,128)(2,1)S(1)}, u32[]{:S(2)}, u32[]{:S(2)}) collective-permute-start(bf16[784,128]{1,0:T(8,128)(2,1)S(1)} %concatenate.9), channel_id=1, source_target_pairs={{0,16},{8,24},{16,0},{24,8},{1,17},{9,25},{17,1},{25,9},{2,18},{10... | collective-permute-start | bytes 602120 | tf_op jit(solution)/shard_map/ppermute | solution.py:349
  16.0 10.5 %collective-permute-start.3 = (bf16[784,128]{1,0:T(8,128)(2,1)S(1)}, bf16[784,128]{1,0:T(8,128)(2,1)S(1)}, u32[]{:S(2)}, u32[]{:S(2)}) collective-permute-start(bf16[784,128]{1,0:T(8,128)(2,1)S(1)} %concatenate.9), channel_id=1, source_target_pairs={{0,8},{8,0},{16,24},{24,16},{1,9},{9,1},{17,25},{25,17},{2,10},{10... | collective-permute-start | bytes 602120 | tf_op jit(solution)/shard_map/ppermute | solution.py:349
  16.5 6.7 %collective-permute-start.7 = (bf16[384,128]{1,0:T(8,128)(2,1)}, bf16[384,128]{1,0:T(8,128)(2,1)S(1)}, u32[]{:S(2)}, u32[]{:S(2)}) collective-permute-start(bf16[384,128]{1,0:T(8,128)(2,1)} %get-tuple-element.40), channel_id=1, source_target_pairs={{0,6},{1,7},{2,4},{3,5},{4,2},{5,3},{6,0},{7,1},{8,14},{9,15},{10,... | collective-permute-start | bytes 294920 | tf_op jit(solution)/shard_map/ppermute | solution.py:352
  20.0 6.5 %collective-permute-start.6 = (bf16[384,128]{1,0:T(8,128)(2,1)}, bf16[384,128]{1,0:T(8,128)(2,1)S(1)}, u32[]{:S(2)}, u32[]{:S(2)}) collective-permute-start(bf16[384,128]{1,0:T(8,128)(2,1)} %get-tuple-element.40), channel_id=1, source_target_pairs={{0,4},{1,5},{2,6},{3,7},{4,0},{5,1},{6,2},{7,3},{8,12},{9,13},{10,... | collective-permute-start | bytes 294920 | tf_op jit(solution)/shard_map/ppermute | solution.py:352
  20.0 24.2 %copy-start.1 = (bf16[768,128]{1,0:T(8,128)(2,1)S(1)}, bf16[768,128]{1,0:T(8,128)(2,1)}, u32[]{:S(2)}) copy-start(bf16[768,128]{1,0:T(8,128)(2,1)} %get-tuple-element.55.refs_0_) | copy-start | bytes 589828
  20.0 26.3 %copy-start.4 = (f32[768]{0:T(1024)S(1)}, f32[768]{0:T(1024)}, u32[]{:S(2)}) copy-start(f32[768]{0:T(1024)} %param.4) | copy-start | bytes 9220
  20.0 26.3 %copy-start.5 = (f32[8,128]{1,0:T(8,128)S(1)}, f32[8,128]{1,0:T(8,128)}, u32[]{:S(2)}) copy-start(f32[8,128]{1,0:T(8,128)} %noise_ref.1) | copy-start | bytes 12292
  26.5 3.7 %collective-permute-start.8 = (bf16[400,128]{1,0:T(8,128)(2,1)S(1)}, bf16[400,128]{1,0:T(8,128)(2,1)S(1)}, u32[]{:S(2)}, u32[]{:S(2)}) collective-permute-start(bf16[400,128]{1,0:T(8,128)(2,1)S(1)} %select_select_fusion.2.mine_ref), channel_id=1, source_target_pairs={{0,1},{1,0},{2,3},{3,2},{4,5},{5,4},{6,7},{7,6},{8,9},{9,8},{10,11... | collective-permute-start | bytes 307208 | tf_op jit(solution)/shard_map/ppermute | solution.py:352
  26.6 14.1 %collective-permute-start.14 = (bf16[1152,128]{1,0:T(8,128)(2,1)S(1)}, bf16[1152,128]{1,0:T(8,128)(2,1)S(1)}, u32[]{:S(2)}, u32[]{:S(2)}) collective-permute-start(bf16[1152,128]{1,0:T(8,128)(2,1)S(1)} %pad_maximum_fusion.refs_2_), channel_id=1, source_target_pairs={{0,24},{8,16},{16,8},{24,0},{1,25},{9,17},{17,9},{25,1},{2,26},{10... | collective-permute-start | bytes 884744 | tf_op jit(solution)/shard_map/ppermute | solution.py:349
  29.1 14.2 %collective-permute-start.13 = (bf16[1152,128]{1,0:T(8,128)(2,1)S(1)}, bf16[1152,128]{1,0:T(8,128)(2,1)S(1)}, u32[]{:S(2)}, u32[]{:S(2)}) collective-permute-start(bf16[1152,128]{1,0:T(8,128)(2,1)S(1)} %pad_maximum_fusion.refs_2_), channel_id=1, source_target_pairs={{0,16},{8,24},{16,0},{24,8},{1,17},{9,25},{17,1},{25,9},{2,18},{10... | collective-permute-start | bytes 884744 | tf_op jit(solution)/shard_map/ppermute | solution.py:349
  29.7 13.8 %collective-permute-start.12 = (bf16[1152,128]{1,0:T(8,128)(2,1)S(1)}, bf16[1152,128]{1,0:T(8,128)(2,1)S(1)}, u32[]{:S(2)}, u32[]{:S(2)}) collective-permute-start(bf16[1152,128]{1,0:T(8,128)(2,1)S(1)} %pad_maximum_fusion.refs_2_), channel_id=1, source_target_pairs={{0,8},{8,0},{16,24},{24,16},{1,9},{9,1},{17,25},{25,17},{2,10},{10... | collective-permute-start | bytes 884744 | tf_op jit(solution)/shard_map/ppermute | solution.py:349
  30.2 8.8 %collective-permute-start.11 = (bf16[384,128]{1,0:T(8,128)(2,1)}, bf16[384,128]{1,0:T(8,128)(2,1)S(1)}, u32[]{:S(2)}, u32[]{:S(2)}) collective-permute-start(bf16[384,128]{1,0:T(8,128)(2,1)} %get-tuple-element.52), channel_id=1, source_target_pairs={{0,6},{1,7},{2,4},{3,5},{4,2},{5,3},{6,0},{7,1},{8,14},{9,15},{10,... | collective-permute-start | bytes 294920 | tf_op jit(solution)/shard_map/ppermute | solution.py:352
  32.4 8.4 %collective-permute-start.10 = (bf16[384,128]{1,0:T(8,128)(2,1)}, bf16[384,128]{1,0:T(8,128)(2,1)S(1)}, u32[]{:S(2)}, u32[]{:S(2)}) collective-permute-start(bf16[384,128]{1,0:T(8,128)(2,1)} %get-tuple-element.52), channel_id=1, source_target_pairs={{0,4},{1,5},{2,6},{3,7},{4,0},{5,1},{6,2},{7,3},{8,12},{9,13},{10,... | collective-permute-start | bytes 294920 | tf_op jit(solution)/shard_map/ppermute | solution.py:352
  39.0 5.6 %collective-permute-start.19 = (bf16[384,128]{1,0:T(8,128)(2,1)S(1)}, bf16[384,128]{1,0:T(8,128)(2,1)S(1)}, u32[]{:S(2)}, u32[]{:S(2)}) collective-permute-start(bf16[384,128]{1,0:T(8,128)(2,1)S(1)} %get-tuple-element.66), channel_id=1, source_target_pairs={{0,1},{1,0},{2,3},{3,2},{4,5},{5,4},{6,7},{7,6},{8,9},{9,8},{10,11... | collective-permute-start | bytes 294920 | tf_op jit(solution)/shard_map/ppermute | solution.py:352
  43.4 2.9 %collective-permute-start.17 = (bf16[1152,128]{1,0:T(8,128)(2,1)S(1)}, bf16[1152,128]{1,0:T(8,128)(2,1)S(1)}, u32[]{:S(2)}, u32[]{:S(2)}) collective-permute-start(bf16[1152,128]{1,0:T(8,128)(2,1)S(1)} %pad_maximum_fusion.refs_2_), channel_id=1, source_target_pairs={{0,1},{1,0},{2,3},{3,2},{4,5},{5,4},{6,7},{7,6},{8,9},{9,8},{10,11... | collective-permute-start | bytes 884744 | tf_op jit(solution)/shard_map/ppermute | solution.py:352
  43.5 2.8 %collective-permute-start.20 = (bf16[1152,128]{1,0:T(8,128)(2,1)S(1)}, bf16[1152,128]{1,0:T(8,128)(2,1)S(1)}, u32[]{:S(2)}, u32[]{:S(2)}) collective-permute-start(bf16[1152,128]{1,0:T(8,128)(2,1)S(1)} %get-tuple-element.64), channel_id=1, source_target_pairs={{0,1},{1,0},{2,3},{3,2},{4,5},{5,4},{6,7},{7,6},{8,9},{9,8},{10,11... | collective-permute-start | bytes 884744 | tf_op jit(solution)/shard_map/ppermute | solution.py:352
  44.1 1.6 %collective-permute-start.18 = (bf16[768,128]{1,0:T(8,128)(2,1)S(1)}, bf16[768,128]{1,0:T(8,128)(2,1)S(1)}, u32[]{:S(2)}, u32[]{:S(2)}) collective-permute-start(bf16[768,128]{1,0:T(8,128)(2,1)S(1)} %pad_maximum_fusion.1), channel_id=1, source_target_pairs={{0,1},{1,0},{2,3},{3,2},{4,5},{5,4},{6,7},{7,6},{8,9},{9,8},{10,11... | collective-permute-start | bytes 589832 | tf_op jit(solution)/shard_map/ppermute | solution.py:352
  44.2 1.8 %collective-permute-start.15 = (bf16[768,128]{1,0:T(8,128)(2,1)S(1)}, bf16[768,128]{1,0:T(8,128)(2,1)S(1)}, u32[]{:S(2)}, u32[]{:S(2)}) collective-permute-start(bf16[768,128]{1,0:T(8,128)(2,1)S(1)} %copy-done.1), channel_id=1, source_target_pairs={{0,1},{1,0},{2,3},{3,2},{4,5},{5,4},{6,7},{7,6},{8,9},{9,8},{10,11... | collective-permute-start | bytes 589832 | tf_op jit(solution)/shard_map/ppermute | solution.py:352
  44.7 1.6 %collective-permute-start.16 = (bf16[768,128]{1,0:T(8,128)(2,1)S(1)}, bf16[768,128]{1,0:T(8,128)(2,1)S(1)}, u32[]{:S(2)}, u32[]{:S(2)}) collective-permute-start(bf16[768,128]{1,0:T(8,128)(2,1)S(1)} %collective-permute-done.9.refs_1_), channel_id=1, source_target_pairs={{0,1},{1,0},{2,3},{3,2},{4,5},{5,4},{6,7},{7,6},{8,9},{9,8},{10,11... | collective-permute-start | bytes 589832 | tf_op jit(solution)/shard_map/ppermute | solution.py:352
  (6 other events, 37.4 us)

commit v4 on v3

--- a/solution.py
+++ b/solution.py
@@ -11,6 +11,7 @@
 VMEM_REST = 32
 ORDER = (0, 2, 4, 6, 1, 3, 5, 7)
 VM = pl.BlockSpec(memory_space=pltpu.VMEM)
+ANY = pl.BlockSpec(memory_space=pl.ANY)
 
 
 def nt(a, b, precision=None):
@@ -30,28 +31,40 @@
     return hi, mid, rest.astype(jnp.bfloat16)
 
 
-def pack_kernel(feat_ref, both_ref, own_ref, oth_ref):
+def pack_kernel(feat_ref, noise_ref, own_ref, oth_ref, own_long_ref, oth_long_ref):
     tiles, depth, width = feat_ref.shape
     left = LANES - depth
     parity = lax.axis_index("col") // lax.axis_size("row")
-    for half, out_ref in ((0, own_ref), (1, oth_ref)):
+    for half, outs in ((0, (own_ref, own_long_ref)), (1, (oth_ref, oth_long_ref))):
         tile = [feat_ref[2 * k + (parity if half == 0 else 1 - parity)] for k in range(4)]
         for k in range(3):
             block = jnp.concatenate([tile[k], tile[3][left * k : left * (k + 1)]], axis=0).T
-            out_ref[k * width : (k + 1) * width, :] = block
-            both_ref[(3 * half + k) * width : (3 * half + k + 1) * width, :] = block
-
-
-def pack(feats):
-    width = feats.shape[2]
-    half = jax.ShapeDtypeStruct((3 * width, width), jnp.bfloat16)
+            for out_ref in outs:
+                out_ref[k * width : (k + 1) * width, :] = block
+    row = lax.broadcasted_iota(jnp.int32, (16, width), 0)
+    parts = jnp.zeros((16, width), jnp.float32)
+    for k, part in enumerate(split3(noise_ref[0:1, :])):
+        parts = jnp.where(row == k, part.astype(jnp.float32), parts)
+    for out_ref in (own_long_ref, oth_long_ref):
+        out_ref[3 * width : 3 * width + depth, :] = feat_ref[0]
+        out_ref[3 * width + depth :, :] = parts.astype(jnp.bfloat16)
+
+
+def pack(feats, noise):
+    _, depth, width = feats.shape
+    rows = lambda n: jax.ShapeDtypeStruct((n, width), jnp.bfloat16)
     return pl.pallas_call(
         pack_kernel,
-        out_shape=(jax.ShapeDtypeStruct((6 * width, width), jnp.bfloat16), half, half),
-        in_specs=[VM],
-        out_specs=(VM,) * 3,
+        out_shape=(
+            rows(3 * width),
+            rows(3 * width),
+            rows(3 * width + depth + 16),
+            rows(3 * width + depth + 16),
+        ),
+        in_specs=[VM, VM],
+        out_specs=(VM,) * 4,
         name="pack",
-    )(feats)
+    )(feats, noise)
 
 
 def slice_weights(length_ref, depth):
@@ -149,47 +162,48 @@
     return jnp.concatenate(blocks, axis=0)
 
 
-def first_kernel(length_ref, mine_ref, sib_ref, inv_ref, both_ref, sq_ref, diag_ref, work):
-    width = inv_ref.shape[0]
-    depth = (mine_ref.shape[0] - 16) // 4
-    x = jnp.concatenate([ref[0 : 4 * depth, :] for ref in (mine_ref, sib_ref)], axis=0)
+def first_kernel(length_ref, mine_ref, sib_ref, out_ref, work):
+    width = work.shape[0]
+    each = mine_ref.shape[0] // 4
+    depth = each - 16
+    starts = range(0, 4 * each, each)
+    x = jnp.concatenate([ref[k : k + depth, :] for ref in (mine_ref, sib_ref) for k in starts], axis=0)
     w = jnp.concatenate(slice_weights(length_ref, depth), axis=0)
     xf = x.astype(jnp.float32)
     xw = xf * w
     parts = split3(xw)
-    both_ref[...] = dense_rows(jnp.concatenate(parts[:2], axis=1), depth)
+    whole = 8 * depth
+    out_ref[0:whole, :] = dense_rows(jnp.concatenate(parts[:2], axis=1), depth)
     turned = x.T
     gram = sum(jnp.dot(turned, part, preferred_element_type=jnp.float32) for part in parts)
     sq_row = jnp.sum(xf * xw, axis=0, keepdims=True)
-    sq_ref[...] = jnp.broadcast_to(sq_row, sq_ref.shape)
     sq_col = jnp.broadcast_to(sq_row, (8, width)).T[:, 0:1]
-    tail = mine_ref[4 * depth :, :].astype(jnp.float32)
+    tail = mine_ref[depth:each, :].astype(jnp.float32)
     noise = tail[0:1, :] + tail[1:2, :] + tail[2:3, :]
     i = lax.broadcasted_iota(jnp.int32, (width, width), 0)
     j = lax.broadcasted_iota(jnp.int32, (width, width), 1)
-    diag = jnp.where(i == j, noise, 0.0)
-    diag_ref[...] = diag
-    work[...] = jnp.exp(-0.5 * (sq_col + sq_row - 2.0 * gram)) + diag
+    work[...] = jnp.exp(-0.5 * (sq_col + sq_row - 2.0 * gram)) + jnp.where(i == j, noise, 0.0)
+    both = jnp.concatenate([sq_row, noise], axis=1)
+    row = lax.broadcasted_iota(jnp.int32, (16, 2 * width), 0)
+    rest = jnp.zeros((16, 2 * width), jnp.float32)
+    for k, part in enumerate(split3(both)):
+        rest = jnp.where(row == k, part.astype(jnp.float32), rest)
+    out_ref[whole + width :, :] = rest.astype(jnp.bfloat16)
     rows = lax.broadcasted_iota(jnp.int32, (8, LANES), 0)
     lanes = lax.broadcasted_iota(jnp.int32, (8, LANES), 1)
     tiles = [work[8 * t : 8 * t + 8, :] for t in range(width // 8)]
-    for t, tile in enumerate(inverse_factor(tiles, rows, lanes)):
-        inv_ref[8 * t : 8 * t + 8, :] = tile
+    inverse = jnp.concatenate(inverse_factor(tiles, rows, lanes), axis=0)
+    out_ref[whole : whole + width, :] = jnp.concatenate(split2(inverse), axis=1)
 
 
 def first_tile(lengths, mine, sib):
     width = mine.shape[1]
-    whole = 2 * (mine.shape[0] - 16)
+    whole = 2 * (mine.shape[0] - 64)
     return pl.pallas_call(
         first_kernel,
-        out_shape=(
-            jax.ShapeDtypeStruct((width, width), jnp.float32),
-            jax.ShapeDtypeStruct((whole, 2 * width), jnp.bfloat16),
-            jax.ShapeDtypeStruct((8, width), jnp.float32),
-            jax.ShapeDtypeStruct((width, width), jnp.float32),
-        ),
+        out_shape=jax.ShapeDtypeStruct((whole + width + 16, 2 * width), jnp.bfloat16),
         in_specs=[VM] * 3,
-        out_specs=(VM,) * 4,
+        out_specs=VM,
         scratch_shapes=[pltpu.VMEM((width, width), jnp.float32)],
         name="first_tile",
     )(lengths, mine, sib)
@@ -232,18 +246,16 @@
     return jnp.concatenate([hi, hi, lo], axis=1)
 
 
-def rest_kernel(depth, length_ref, noise_ref, inv_ref, both_ref, sq0_ref, diag_ref, *refs):
-    row_refs, col_refs, (panel_ref, trail_ref) = refs[:9], refs[9:13], refs[13:]
-    width = inv_ref.shape[0]
+def rest_kernel(depth, length_ref, noise_ref, first_hbm, *refs):
+    row_refs, col_refs, (panel_hbm, trail_hbm, first_ref, panel_ref, trail_ref, sems) = refs[:4], refs[4:8], refs[8:]
+    width, whole = noise_ref.shape[1], 8 * depth
+    copy = pltpu.make_async_copy(first_hbm, first_ref, sems.at[0])
+    copy.start()
     h = 3 * width
-    w0, w1, p, q2, q3, s0, s1, sp, sq = row_refs
-    third = lambda ref, k: ref.at[pl.ds(k * h, h)]
-    row_own = [third(w0, 0), third(w1, 0), third(p, 1), third(p, 2)]
-    row_own += [third(s0, 0), third(s1, 0), third(sp, 1), third(sp, 2)]
-    row_oth = [third(w0, 1), third(w1, 1), q2, q3, third(s0, 1), third(s1, 1), third(sq, 0), third(sq, 1)]
-    cols = []
-    for near, far in (col_refs[0:2], col_refs[2:4]):
-        cols += [near, third(far, 0), third(far, 1), third(far, 2)]
+    cut = lambda ref, k: ref.at[pl.ds(k * h, h)]
+    cuts = lambda ref: [ref.at[pl.ds(k * h, h)] for k in range(ref.shape[0] // h)]
+    row_own, row_oth = cuts(row_refs[0]) + cuts(row_refs[1]), cuts(row_refs[2]) + cuts(row_refs[3])
+    cols = sum((cuts(ref) for ref in col_refs), [])
     row_id, col_id, n_rows = lax.axis_index("row"), lax.axis_index("col"), lax.axis_size("row")
     parity, on_diag = col_id // n_rows, row_id == col_id % n_rows
 
@@ -260,16 +272,20 @@
     eye = lax.broadcasted_iota(jnp.int32, (width, width), 0) == lax.broadcasted_iota(
         jnp.int32, (width, width), 1
     )
-    inv = twice(inv_ref[...])
-    sq0 = sq0_ref[0:1, :]
+    copy.wait()
+    inv = first_ref[whole : whole + width, :]
+    inv = jnp.concatenate([inv[:, 0:width], inv], axis=1)
+    tail = first_ref[whole + width :, :].astype(jnp.float32)
+    tail = tail[0:1, :] + tail[1:2, :] + tail[2:3, :]
+    sq0, diag0 = tail[:, 0:width], jnp.where(eye, tail[:, width:], 0.0)
 
     def panel_of(x, sq, heads):
-        gram = jnp.dot(x, both_ref[...], preferred_element_type=jnp.float32)
+        gram = jnp.dot(x, first_ref[0:whole, :], preferred_element_type=jnp.float32)
         gram = gram[:, 0:width] + gram[:, width:]
         kern = jnp.exp(gram - 0.5 * (sq + sq0))
         if heads:
             tops = [
-                kern[h * width : (h + 1) * width] + jnp.where(c, diag_ref[...], 0.0)
+                kern[h * width : (h + 1) * width] + jnp.where(c, diag0, 0.0)
                 for h, c in enumerate(heads)
             ]
             if len(heads) * width < kern.shape[0]:
@@ -293,6 +309,7 @@
     c_sq = jnp.concatenate(c_sq, axis=1)
     c_panel = twice(jnp.concatenate(c_panel, axis=0))
 
+    outs = []
     for t in range(4):
         x = jnp.concatenate([dense(row_own, t, width, depth), dense(row_oth, t, width, depth)], axis=0)
         xf = x.astype(jnp.float32)
@@ -311,6 +328,14 @@
                 if half == 0 and tc == t:
                     block = block + jnp.where(eye & on_diag, noise_ref[pl.ds(tile, 1), :], 0.0)
                 trail_ref[pl.ds(tile * (4 * width) + tc, width, stride=4), :] = block
+            span = pl.ds(tile * (4 * width), 4 * width)
+            for n, (src, dst) in enumerate(
+                ((panel_ref.at[tile], panel_hbm.at[tile]), (trail_ref.at[span], trail_hbm.at[span]))
+            ):
+                outs.append(pltpu.make_async_copy(src, dst, sems.at[1 + 4 * t + 2 * half + n]))
+                outs[-1].start()
+    for copy in outs:
+        copy.wait()
 
 
 def rest(depth, lengths, noise, first, *slices):
@@ -321,20 +346,17 @@
             jax.ShapeDtypeStruct((tiles, width, width), jnp.float32),
             jax.ShapeDtypeStruct((tiles * width * 4, width), jnp.float32),
         ),
-        in_specs=[VM] * 19,
-        out_specs=(VM, VM),
+        in_specs=[VM] * 2 + [ANY] + [VM] * 8,
+        out_specs=(ANY, ANY),
+        scratch_shapes=[
+            pltpu.VMEM(first.shape, first.dtype),
+            pltpu.VMEM((tiles, width, width), jnp.float32),
+            pltpu.VMEM((tiles * width * 4, width), jnp.float32),
+            pltpu.SemaphoreType.DMA((17,)),
+        ],
         compiler_params=pltpu.CompilerParams(vmem_limit_bytes=VMEM_REST * 1024 * 1024),
         name="rest",
-    )(lengths, noise, *first, *slices)
-
-
-def noise_parts(noise):
-    rest, parts = noise[0:1], []
-    for _ in range(3):
-        part = lax.reduce_precision(rest, 8, 7)
-        parts.append(part.astype(jnp.bfloat16))
-        rest = rest - part
-    return jnp.concatenate(parts + [jnp.zeros((13, noise.shape[1]), jnp.bfloat16)], axis=0)
+    )(lengths, noise, first, *slices)
 
 
 def body(features, lengthscale, noise):
@@ -357,34 +379,26 @@
     def after(x, *others):
         return lax.optimization_barrier((x, *others))[0]
 
-    head = feats[0]
-    far = [over_col(head, 2 * k) for k in (1, 2, 3)]
-    both, own, oth = pack(after(feats, head))
-    both, oth, *far = lax.optimization_barrier((both, oth, *far))
-    near, p2, p3 = over_col(both, 2), over_col(oth, 4), over_col(oth, 6)
-    size, low = own.shape[0], 4 * depth + 16
-    early = jnp.concatenate([head] + far + [noise_parts(noise), own], axis=0)
-    early = [early] + [over_row(early, k) for k in (1, 2, 3)]
-    *early, p2, p3 = lax.optimization_barrier((*early, p2, p3))
-    stack = lax.select_n(row_id, *[v[:low] for v in early])
-    sib = over_col(stack, 1)
-    p = jnp.concatenate([near[:size], p2, p3], axis=0)
+    own, oth, own_long, oth_long = pack(feats, noise)
+    size = own.shape[0]
+    near, p2, p3 = over_col(own, 2), over_col(oth, 4), over_col(oth, 6)
+    first_planes = [own_long] + [over_row(own_long, k) for k in (1, 2, 3)]
+    head = lax.select_n(row_id, *[v[size:] for v in first_planes])
+    q1 = over_col(lax.dynamic_update_slice(oth_long, head, (size, 0)), 2)
+    half = lax.dynamic_update_slice(own_long, head, (size, 0))
+    q2, q3 = over_col(half, 4), over_col(half, 6)
+    p = jnp.concatenate([near, p2, p3], axis=0)
     planes = [p] + [over_row(p, k) for k in (1, 2, 3)]
-    own_late = after(own, sib)
-    q2, q3 = over_col(own_late, 4), over_col(own_late, 6)
-    first = first_tile(lengths, stack, sib)
-    q2, q3, *planes, sib_both, sib_near, sib_p, _ = lax.optimization_barrier(
-        (q2, q3, *planes, both, near, p, first[0])
-    )
-    sib_both, sib_near, sib_p = (over_col(v, 1) for v in (sib_both, sib_near, sib_p))
-    sib_q = over_col(jnp.concatenate([q2, q3], axis=0), 1)
-    early = [v[low:] for v in early]
-    take = lambda k: [lax.select_n(k, *v) for v in (early, planes)]
-    keep = take(row_id ^ home)
-    give = [over_col(v, 1) for v in take(row_id ^ home ^ 1)]
-    panel, trailing = rest(
-        depth, lengths, noise, first, both, near, p, q2, q3, sib_both, sib_near, sib_p, sib_q, *keep, *give
-    )
+    p = jnp.concatenate([own, near, p2, p3], axis=0)
+    stack = jnp.concatenate([head] + [v[size:] for v in (q1, q2, q3)], axis=0)
+    first = first_tile(lengths, stack, over_col(stack, 1))
+    q = jnp.concatenate([oth] + [v[:size] for v in (q1, q2, q3)], axis=0)
+    sibs = [over_col(v, 1) for v in (p, q)]
+    *planes, _ = lax.optimization_barrier((*planes, first))
+    first_planes = [v[:size] for v in first_planes]
+    keep = [lax.select_n(row_id ^ home, *v) for v in (first_planes, planes)]
+    give = [over_col(lax.select_n(row_id ^ home ^ 1, *v), 1) for v in (first_planes, planes)]
+    panel, trailing = rest(depth, lengths, noise, first, p, sibs[0], q, sibs[1], *keep, *give)
     return panel, trailing.reshape(tiles, width, 4, width)
 
 

time: 53.9 us -> 49.5 us (0.918)
  waiting for transfers between devices: 14.7 us -> 6.18 us
  starting transfers between devices: 19.8 us -> 21.8 us
  other arithmetic: 0.86 us -> 2.44 us
    ppermute x15 -> x11, waiting for transfers between devices: 12 us -> 6.17 us  [over_col(): return lax.ppermute(x, 'col', [(i, i ^ k) for i in range(n_cols)])]
    ppermute x6, waiting for transfers between devices: 2.66 us -> 0.02 us  [over_row(): return lax.ppermute(x, 'row', [(i, i ^ k) for i in range(n_rows)])]
    ppermute x6, starting transfers between devices: 7.11 us -> 9.02 us  [over_row(): return lax.ppermute(x, 'row', [(i, i ^ k) for i in range(n_rows)])]
    unnamed x18 -> x15, local copies, waits for them, and re-layouts: 0.04 us -> 1.48 us
    dynamic_update_slice x0 -> x1, other arithmetic: none -> 1.38 us  [body(): q1 = over_col(lax.dynamic_update_slice(oth_long, head, (size, 0)), 2)]
    concatenate x1, local copies, waits for them, and re-layouts: 1.08 us -> 0.03 us  [body(): p = jnp.concatenate([near, p2, p3], axis=0)]
    select_n x3 -> x2, other arithmetic: 0.13 us -> 1.02 us  [body(): lax.select_n(row_id ^ home ^ 1, *v)]
    squeeze x1 -> x0, local copies, waits for them, and re-layouts: 0.74 us -> none  [body(): head = feats[0]]
  transfers between devices with their start and end apart: 21 -> 17, of which waited for: 9 -> 4; matrix products, arithmetic and copies ran while one was open for 4% -> 8% of each run, Pallas kernels for 15% -> 14%
where the time goes in v4:
time: 49.5 us; the launch traced here: 49.2 us
  starting transfers between devices  21.8 us (44%)
  Pallas kernels  15.8 us (32%)
  waiting for transfers between devices  6.18 us (12%)
  other arithmetic  2.44 us (5%)
  local copies, waits for them, and re-layouts  2.17 us (4%)
  between operations  0.8 us (2%)
    ppermute x11, starting transfers between devices, over_col(): return lax.ppermute(x, 'col', [(i, i ^ k) for i in range(n_cols)])  12.7 us
    ppermute x6, starting transfers between devices, over_row(): return lax.ppermute(x, 'row', [(i, i ^ k) for i in range(n_rows)])  9.02 us
    pallas_call x1, Pallas kernels, rest(): pl.pallas_call(functools.partial(rest_kernel, depth), out_shape=(jax.Shap...  7.36 us
    pallas_call x1, Pallas kernels, first_tile(): pl.pallas_call(first_kernel, out_shape=jax.ShapeDtypeStruct((whole + widt...  6.69 us
    ppermute x11, waiting for transfers between devices, over_col(): return lax.ppermute(x, 'col', [(i, i ^ k) for i in range(n_cols)])  6.17 us
    pallas_call x1, Pallas kernels, pack(): pl.pallas_call(pack_kernel, out_shape=(rows(3 * width), rows(3 * width),...  1.79 us
    unnamed x15, local copies, waits for them, and re-layouts  1.48 us
    dynamic_update_slice x1, other arithmetic, body(): q1 = over_col(lax.dynamic_update_slice(oth_long, head, (size, 0)), 2)  1.38 us
  transfers between devices with their start and end apart: 17, of which 4 were waited for; matrix products, arithmetic and copies ran while one was open for 8% of the time, Pallas kernels for 14%

profile of v4, /device:TPU:0, one launch (start us, length us, event | category | flops | bytes accessed | tf_op | source)
XLA Modules:
  0.0 49.2 jit_solution(1745117946352427495)
XLA Ops:
  0.6 1.8 %pack.1 = (bf16[384,128]{1,0:T(8,128)(2,1)}, bf16[384,128]{1,0:T(8,128)(2,1)}, bf16[496,128]{1,0:T(8,128)(2,1)}, bf16[496,128]{1,0:T(8,128)(2,1)}) custom-call(bf16[8,96,128]{2,1,0:T(8,128)(2,1)} %bitcast.5, f32[8,128]{1,0:T(8,128)} %noise_ref.3), custom_call_target="tpu_custom_call" | custom-call | tf_op jit(solution)/shard_map/pack/pallas_call | solution.py:56
  2.4 3.9 %collective-permute-start.2 = (bf16[496,128]{1,0:T(8,128)(2,1)}, bf16[496,128]{1,0:T(8,128)(2,1)S(1)}, u32[]{:S(2)}, u32[]{:S(2)}) collective-permute-start(bf16[496,128]{1,0:T(8,128)(2,1)} %get-tuple-element.12), channel_id=1, source_target_pairs={{0,24},{8,16},{16,8},{24,0},{1,25},{9,17},{17,9},{25,1},{2,26},{10... | collective-permute-start | bytes 380936 | tf_op jit(solution)/shard_map/ppermute | solution.py:371
  6.3 0.5 %collective-permute-start.1 = (bf16[496,128]{1,0:T(8,128)(2,1)}, bf16[496,128]{1,0:T(8,128)(2,1)S(1)}, u32[]{:S(2)}, u32[]{:S(2)}) collective-permute-start(bf16[496,128]{1,0:T(8,128)(2,1)} %get-tuple-element.12), channel_id=1, source_target_pairs={{0,16},{8,24},{16,0},{24,8},{1,17},{9,25},{17,1},{25,9},{2,18},{10... | collective-permute-start | bytes 380936 | tf_op jit(solution)/shard_map/ppermute | solution.py:371
  6.9 2.0 %collective-permute-start.7 = (bf16[384,128]{1,0:T(8,128)(2,1)}, bf16[384,128]{1,0:T(8,128)(2,1)S(1)}, u32[]{:S(2)}, u32[]{:S(2)}) collective-permute-start(bf16[384,128]{1,0:T(8,128)(2,1)} %get-tuple-element.14), channel_id=1, source_target_pairs={{0,2},{1,3},{2,0},{3,1},{4,6},{5,7},{6,4},{7,5},{8,10},{9,11},{10,... | collective-permute-start | bytes 294920 | tf_op jit(solution)/shard_map/ppermute | solution.py:374
  8.9 2.5 %collective-permute-start.9 = (bf16[384,128]{1,0:T(8,128)(2,1)}, bf16[384,128]{1,0:T(8,128)(2,1)S(1)}, u32[]{:S(2)}, u32[]{:S(2)}) collective-permute-start(bf16[384,128]{1,0:T(8,128)(2,1)} %get-tuple-element.15), channel_id=1, source_target_pairs={{0,6},{1,7},{2,4},{3,5},{4,2},{5,3},{6,0},{7,1},{8,14},{9,15},{10,... | collective-permute-start | bytes 294920 | tf_op jit(solution)/shard_map/ppermute | solution.py:374
  11.4 0.9 %constant_dynamic-update-slice_fusion.3 = bf16[1536,128]{1,0:T(8,128)(2,1)S(1)} fusion(bf16[384,128]{1,0:T(8,128)(2,1)} %get-tuple-element.14), kind=kLoop, calls=%fused_computation.12 | loop fusion | bytes 196608
  12.3 2.6 %collective-permute-start.8 = (bf16[384,128]{1,0:T(8,128)(2,1)}, bf16[384,128]{1,0:T(8,128)(2,1)S(1)}, u32[]{:S(2)}, u32[]{:S(2)}) collective-permute-start(bf16[384,128]{1,0:T(8,128)(2,1)} %get-tuple-element.15), channel_id=1, source_target_pairs={{0,4},{1,5},{2,6},{3,7},{4,0},{5,1},{6,2},{7,3},{8,12},{9,13},{10,... | collective-permute-start | bytes 294920 | tf_op jit(solution)/shard_map/ppermute | solution.py:374
  15.0 1.4 %constant_dynamic-update-slice_fusion.8 = (bf16[496,128]{1,0:T(8,128)(2,1)}, bf16[112,128]{1,0:T(8,128)(2,1)S(1)}) fusion(bf16[496,128]{1,0:T(8,128)(2,1)} %get-tuple-element.13, bf16[496,128]{1,0:T(8,128)(2,1)S(1)} %collective-permute-done.2, bf16[496,128]{1,0:T(8,128)(2,1)S(1)} %collective-permute-done.1, pred[]{:T(512)S(6)} %select_n.135, ...), kind=kLoop, calls=%fused_computation.17 | loop fusion | flops 43008 | bytes 172035 | tf_op jit(solution)/shard_map/dynamic_update_slice | solution.py:387
  16.4 0.9 %select_select_fusion.2 = (bf16[384,128]{1,0:T(8,128)(2,1)S(1)}, bf16[384,128]{1,0:T(8,128)(2,1)S(1)}) fusion(pred[]{:T(512)S(6)} %select_n.160, pred[]{:T(512)S(6)} %select_n.157, pred[]{:T(512)S(6)} %select_n.155, bf16[496,128]{1,0:T(8,128)(2,1)S(1)} %collective-permute-done.2, bf16[496,128]{1,0:T(8,128)(2,1)S(1)} %collective-permute-done.1, ...), kind=kLoop, calls=%fused_computation.4 | loop fusion | flops 294912 | bytes 589830 | tf_op jit(solution)/shard_map/select_n | solution.py:400
  17.3 0.6 %constant_dynamic-update-slice_fusion.7 = bf16[496,128]{1,0:T(8,128)(2,1)} fusion(bf16[496,128]{1,0:T(8,128)(2,1)} %get-tuple-element.12, bf16[112,128]{1,0:T(8,128)(2,1)S(1)} %get-tuple-element.23), kind=kLoop, calls=%fused_computation.16 | loop fusion | bytes 57344 | tf_op jit(solution)/shard_map/dynamic_update_slice | solution.py:388
  17.9 2.0 %collective-permute-start.5 = (bf16[496,128]{1,0:T(8,128)(2,1)}, bf16[496,128]{1,0:T(8,128)(2,1)S(1)}, u32[]{:S(2)}, u32[]{:S(2)}) collective-permute-start(bf16[496,128]{1,0:T(8,128)(2,1)} %constant_dynamic-update-slice_fusion.7), channel_id=1, source_target_pairs={{0,6},{1,7},{2,4},{3,5},{4,2},{5,3},{6,0},{7,1},{8,14},{9,15},{10,... | collective-permute-start | bytes 380936 | tf_op jit(solution)/shard_map/ppermute | solution.py:374
  19.9 1.9 %collective-permute-start.4 = (bf16[496,128]{1,0:T(8,128)(2,1)}, bf16[496,128]{1,0:T(8,128)(2,1)S(1)}, u32[]{:S(2)}, u32[]{:S(2)}) collective-permute-start(bf16[496,128]{1,0:T(8,128)(2,1)} %constant_dynamic-update-slice_fusion.7), channel_id=1, source_target_pairs={{0,4},{1,5},{2,6},{3,7},{4,0},{5,1},{6,2},{7,3},{8,12},{9,13},{10,... | collective-permute-start | bytes 380936 | tf_op jit(solution)/shard_map/ppermute | solution.py:374
  21.9 0.4 collective-permute-start.3
  22.4 2.5 %collective-permute-start.14 = (bf16[1152,128]{1,0:T(8,128)(2,1)S(1)}, bf16[1152,128]{1,0:T(8,128)(2,1)S(1)}, u32[]{:S(2)}, u32[]{:S(2)}) collective-permute-start(bf16[1152,128]{1,0:T(8,128)(2,1)S(1)} %get-tuple-element.16), channel_id=1, source_target_pairs={{0,24},{8,16},{16,8},{24,0},{1,25},{9,17},{17,9},{25,1},{2,26},{10... | collective-permute-start | bytes 884744 | tf_op jit(solution)/shard_map/ppermute | solution.py:371
  24.9 0.5 %collective-permute-start.13 = (bf16[1152,128]{1,0:T(8,128)(2,1)S(1)}, bf16[1152,128]{1,0:T(8,128)(2,1)S(1)}, u32[]{:S(2)}, u32[]{:S(2)}) collective-permute-start(bf16[1152,128]{1,0:T(8,128)(2,1)S(1)} %get-tuple-element.16), channel_id=1, source_target_pairs={{0,16},{8,24},{16,0},{24,8},{1,17},{9,25},{17,1},{25,9},{2,18},{10... | collective-permute-start | bytes 884744 | tf_op jit(solution)/shard_map/ppermute | solution.py:371
  25.8 1.5 %collective-permute-start.12 = (bf16[1152,128]{1,0:T(8,128)(2,1)S(1)}, bf16[1152,128]{1,0:T(8,128)(2,1)S(1)}, u32[]{:S(2)}, u32[]{:S(2)}) collective-permute-start(bf16[1152,128]{1,0:T(8,128)(2,1)S(1)} %get-tuple-element.16), channel_id=1, source_target_pairs={{0,8},{8,0},{16,24},{24,16},{1,9},{9,1},{17,25},{25,17},{2,10},{10... | collective-permute-start | bytes 884744 | tf_op jit(solution)/shard_map/ppermute | solution.py:371
  27.3 3.4 %collective-permute-done.4 = bf16[496,128]{1,0:T(8,128)(2,1)S(1)} collective-permute-done((bf16[496,128]{1,0:T(8,128)(2,1)}, bf16[496,128]{1,0:T(8,128)(2,1)S(1)}, u32[]{:S(2)}, u32[]{:S(2)}) %collective-permute-start.4) | collective-permute-done | bytes 127008 | tf_op jit(solution)/shard_map/ppermute | solution.py:374
  30.7 0.6 %collective-permute-start.6 = (bf16[448,128]{1,0:T(8,128)(2,1)S(1)}, bf16[448,128]{1,0:T(8,128)(2,1)S(1)}, u32[]{:S(2)}, u32[]{:S(2)}) collective-permute-start(bf16[448,128]{1,0:T(8,128)(2,1)S(1)} %pad_maximum_fusion.1.mine_ref), channel_id=1, source_target_pairs={{0,1},{1,0},{2,3},{3,2},{4,5},{5,4},{6,7},{7,6},{8,9},{9,8},{10,11... | collective-permute-start | bytes 344072 | tf_op jit(solution)/shard_map/ppermute | solution.py:374
  31.4 1.2 %collective-permute-done.6.sib_ref = bf16[448,128]{1,0:T(8,128)(2,1)S(1)} collective-permute-done((bf16[448,128]{1,0:T(8,128)(2,1)S(1)}, bf16[448,128]{1,0:T(8,128)(2,1)S(1)}, u32[]{:S(2)}, u32[]{:S(2)}) %collective-permute-start.6) | collective-permute-done | bytes 114720 | tf_op jit(solution)/shard_map/ppermute | solution.py:374
  32.7 0.5 %copy-done.4 = bf16[448,128]{1,0:T(8,128)(2,1)} copy-done((bf16[448,128]{1,0:T(8,128)(2,1)}, bf16[448,128]{1,0:T(8,128)(2,1)S(1)}, u32[]{:S(2)}) %copy-start.4) | copy-done | bytes 114712
  33.2 6.7 %first_tile.1.first_hbm = bf16[912,256]{1,0:T(8,128)(2,1)} custom-call(f32[6,128]{1,0:T(8,128)} %bitcast.3, bf16[448,128]{1,0:T(8,128)(2,1)} %copy-done.3, bf16[448,128]{1,0:T(8,128)(2,1)} %copy-done.4), custom_call_target="tpu_custom_call" | custom-call | tf_op jit(solution)/shard_map/first_tile/pallas_call | solution.py:202
  40.2 0.4 collective-permute-start.15
  40.6 1.2 %collective-permute-done.15.refs_6_ = bf16[384,128]{1,0:T(8,128)(2,1)S(1)} collective-permute-done((bf16[384,128]{1,0:T(8,128)(2,1)S(1)}, bf16[384,128]{1,0:T(8,128)(2,1)S(1)}, u32[]{:S(2)}, u32[]{:S(2)}) %collective-permute-start.15) | collective-permute-done | bytes 98336 | tf_op jit(solution)/shard_map/ppermute | solution.py:374
  41.8 7.4 %rest.1 = (f32[8,128,128]{2,1,0:T(8,128)}, f32[4096,128]{1,0:T(8,128)}) custom-call(f32[6,128]{1,0:T(8,128)S(1)} %bitcast.4, f32[8,128]{1,0:T(8,128)S(1)} %copy-done.2, bf16[912,256]{1,0:T(8,128)(2,1)S(1)} %copy-done, bf16[1536,128]{1,0:T(8,128)(2,1)S(1)} %get-tuple-element.29.refs_0_, bf16[1536,128]{1,0:T(8,128)(2,1)S(1)} %collective-permute-done.10.refs_1_, ...), custom_call_target="tpu_custom_call" | custom-call | tf_op jit(solution)/shard_map/rest/pallas_call | solution.py:343
  (41 shorter events, 1.1 us)
Async XLA Ops:
  2.4 28.9 %copy-start.5 = (bf16[384,128]{1,0:T(8,128)(2,1)S(1)}, bf16[384,128]{1,0:T(8,128)(2,1)}, u32[]{:S(2)}) copy-start(bf16[384,128]{1,0:T(8,128)(2,1)} %get-tuple-element.15) | copy-start | bytes 294916
  2.4 12.5 %collective-permute-start.2 = (bf16[496,128]{1,0:T(8,128)(2,1)}, bf16[496,128]{1,0:T(8,128)(2,1)S(1)}, u32[]{:S(2)}, u32[]{:S(2)}) collective-permute-start(bf16[496,128]{1,0:T(8,128)(2,1)} %get-tuple-element.12), channel_id=1, source_target_pairs={{0,24},{8,16},{16,8},{24,0},{1,25},{9,17},{17,9},{25,1},{2,26},{10... | collective-permute-start | bytes 380936 | tf_op jit(solution)/shard_map/ppermute | solution.py:371
  6.3 8.6 %collective-permute-start.1 = (bf16[496,128]{1,0:T(8,128)(2,1)}, bf16[496,128]{1,0:T(8,128)(2,1)S(1)}, u32[]{:S(2)}, u32[]{:S(2)}) collective-permute-start(bf16[496,128]{1,0:T(8,128)(2,1)} %get-tuple-element.12), channel_id=1, source_target_pairs={{0,16},{8,24},{16,0},{24,8},{1,17},{9,25},{17,1},{25,9},{2,18},{10... | collective-permute-start | bytes 380936 | tf_op jit(solution)/shard_map/ppermute | solution.py:371
  6.8 8.2 %collective-permute-start = (bf16[496,128]{1,0:T(8,128)(2,1)}, bf16[496,128]{1,0:T(8,128)(2,1)S(1)}, u32[]{:S(2)}, u32[]{:S(2)}) collective-permute-start(bf16[496,128]{1,0:T(8,128)(2,1)} %get-tuple-element.12), channel_id=1, source_target_pairs={{0,8},{8,0},{16,24},{24,16},{1,9},{9,1},{17,25},{25,17},{2,10},{10... | collective-permute-start | bytes 380936 | tf_op jit(solution)/shard_map/ppermute | solution.py:371
  6.9 5.4 %collective-permute-start.7 = (bf16[384,128]{1,0:T(8,128)(2,1)}, bf16[384,128]{1,0:T(8,128)(2,1)S(1)}, u32[]{:S(2)}, u32[]{:S(2)}) collective-permute-start(bf16[384,128]{1,0:T(8,128)(2,1)} %get-tuple-element.14), channel_id=1, source_target_pairs={{0,2},{1,3},{2,0},{3,1},{4,6},{5,7},{6,4},{7,5},{8,10},{9,11},{10,... | collective-permute-start | bytes 294920 | tf_op jit(solution)/shard_map/ppermute | solution.py:374
  8.9 13.4 %collective-permute-start.9 = (bf16[384,128]{1,0:T(8,128)(2,1)}, bf16[384,128]{1,0:T(8,128)(2,1)S(1)}, u32[]{:S(2)}, u32[]{:S(2)}) collective-permute-start(bf16[384,128]{1,0:T(8,128)(2,1)} %get-tuple-element.15), channel_id=1, source_target_pairs={{0,6},{1,7},{2,4},{3,5},{4,2},{5,3},{6,0},{7,1},{8,14},{9,15},{10,... | collective-permute-start | bytes 294920 | tf_op jit(solution)/shard_map/ppermute | solution.py:374
  12.3 10.0 %collective-permute-start.8 = (bf16[384,128]{1,0:T(8,128)(2,1)}, bf16[384,128]{1,0:T(8,128)(2,1)S(1)}, u32[]{:S(2)}, u32[]{:S(2)}) collective-permute-start(bf16[384,128]{1,0:T(8,128)(2,1)} %get-tuple-element.15), channel_id=1, source_target_pairs={{0,4},{1,5},{2,6},{3,7},{4,0},{5,1},{6,2},{7,3},{8,12},{9,13},{10,... | collective-permute-start | bytes 294920 | tf_op jit(solution)/shard_map/ppermute | solution.py:374
  17.9 7.9 %collective-permute-start.5 = (bf16[496,128]{1,0:T(8,128)(2,1)}, bf16[496,128]{1,0:T(8,128)(2,1)S(1)}, u32[]{:S(2)}, u32[]{:S(2)}) collective-permute-start(bf16[496,128]{1,0:T(8,128)(2,1)} %constant_dynamic-update-slice_fusion.7), channel_id=1, source_target_pairs={{0,6},{1,7},{2,4},{3,5},{4,2},{5,3},{6,0},{7,1},{8,14},{9,15},{10,... | collective-permute-start | bytes 380936 | tf_op jit(solution)/shard_map/ppermute | solution.py:374
  19.9 10.7 %collective-permute-start.4 = (bf16[496,128]{1,0:T(8,128)(2,1)}, bf16[496,128]{1,0:T(8,128)(2,1)S(1)}, u32[]{:S(2)}, u32[]{:S(2)}) collective-permute-start(bf16[496,128]{1,0:T(8,128)(2,1)} %constant_dynamic-update-slice_fusion.7), channel_id=1, source_target_pairs={{0,4},{1,5},{2,6},{3,7},{4,0},{5,1},{6,2},{7,3},{8,12},{9,13},{10,... | collective-permute-start | bytes 380936 | tf_op jit(solution)/shard_map/ppermute | solution.py:374
  21.9 8.8 %collective-permute-start.3 = (bf16[496,128]{1,0:T(8,128)(2,1)}, bf16[496,128]{1,0:T(8,128)(2,1)S(1)}, u32[]{:S(2)}, u32[]{:S(2)}) collective-permute-start(bf16[496,128]{1,0:T(8,128)(2,1)} %get-tuple-element.22), channel_id=1, source_target_pairs={{0,2},{1,3},{2,0},{3,1},{4,6},{5,7},{6,4},{7,5},{8,10},{9,11},{10,... | collective-permute-start | bytes 380936 | tf_op jit(solution)/shard_map/ppermute | solution.py:374
  22.4 17.5 %collective-permute-start.14 = (bf16[1152,128]{1,0:T(8,128)(2,1)S(1)}, bf16[1152,128]{1,0:T(8,128)(2,1)S(1)}, u32[]{:S(2)}, u32[]{:S(2)}) collective-permute-start(bf16[1152,128]{1,0:T(8,128)(2,1)S(1)} %get-tuple-element.16), channel_id=1, source_target_pairs={{0,24},{8,16},{16,8},{24,0},{1,25},{9,17},{17,9},{25,1},{2,26},{10... | collective-permute-start | bytes 884744 | tf_op jit(solution)/shard_map/ppermute | solution.py:371
  24.9 15.0 %collective-permute-start.13 = (bf16[1152,128]{1,0:T(8,128)(2,1)S(1)}, bf16[1152,128]{1,0:T(8,128)(2,1)S(1)}, u32[]{:S(2)}, u32[]{:S(2)}) collective-permute-start(bf16[1152,128]{1,0:T(8,128)(2,1)S(1)} %get-tuple-element.16), channel_id=1, source_target_pairs={{0,16},{8,24},{16,0},{24,8},{1,17},{9,25},{17,1},{25,9},{2,18},{10... | collective-permute-start | bytes 884744 | tf_op jit(solution)/shard_map/ppermute | solution.py:371
  25.8 14.1 %collective-permute-start.12 = (bf16[1152,128]{1,0:T(8,128)(2,1)S(1)}, bf16[1152,128]{1,0:T(8,128)(2,1)S(1)}, u32[]{:S(2)}, u32[]{:S(2)}) collective-permute-start(bf16[1152,128]{1,0:T(8,128)(2,1)S(1)} %get-tuple-element.16), channel_id=1, source_target_pairs={{0,8},{8,0},{16,24},{24,16},{1,9},{9,1},{17,25},{25,17},{2,10},{10... | collective-permute-start | bytes 884744 | tf_op jit(solution)/shard_map/ppermute | solution.py:371
  30.7 11.1 %copy-start.1 = (f32[768]{0:T(1024)S(1)}, f32[768]{0:T(1024)}, u32[]{:S(2)}) copy-start(f32[768]{0:T(1024)} %param.4) | copy-start | bytes 9220
  30.7 11.2 %copy-start.2 = (f32[8,128]{1,0:T(8,128)S(1)}, f32[8,128]{1,0:T(8,128)}, u32[]{:S(2)}) copy-start(f32[8,128]{1,0:T(8,128)} %noise_ref.3) | copy-start | bytes 12292
  30.7 11.1 %collective-permute-start.10 = (bf16[1536,128]{1,0:T(8,128)(2,1)S(1)}, bf16[1536,128]{1,0:T(8,128)(2,1)S(1)}, u32[]{:S(2)}, u32[]{:S(2)}) collective-permute-start(bf16[1536,128]{1,0:T(8,128)(2,1)S(1)} %get-tuple-element.29.refs_0_), channel_id=1, source_target_pairs={{0,1},{1,0},{2,3},{3,2},{4,5},{5,4},{6,7},{7,6},{8,9},{9,8},{10,11... | collective-permute-start | bytes 1179656 | tf_op jit(solution)/shard_map/ppermute | solution.py:374
  30.7 2.0 %copy-start.3 = (bf16[448,128]{1,0:T(8,128)(2,1)}, bf16[448,128]{1,0:T(8,128)(2,1)S(1)}, u32[]{:S(2)}) copy-start(bf16[448,128]{1,0:T(8,128)(2,1)S(1)} %pad_maximum_fusion.1.mine_ref) | copy-start | bytes 344068
  30.7 1.8 %collective-permute-start.6 = (bf16[448,128]{1,0:T(8,128)(2,1)S(1)}, bf16[448,128]{1,0:T(8,128)(2,1)S(1)}, u32[]{:S(2)}, u32[]{:S(2)}) collective-permute-start(bf16[448,128]{1,0:T(8,128)(2,1)S(1)} %pad_maximum_fusion.1.mine_ref), channel_id=1, source_target_pairs={{0,1},{1,0},{2,3},{3,2},{4,5},{5,4},{6,7},{7,6},{8,9},{9,8},{10,11... | collective-permute-start | bytes 344072 | tf_op jit(solution)/shard_map/ppermute | solution.py:374
  32.6 0.6 %copy-start.4 = (bf16[448,128]{1,0:T(8,128)(2,1)}, bf16[448,128]{1,0:T(8,128)(2,1)S(1)}, u32[]{:S(2)}) copy-start(bf16[448,128]{1,0:T(8,128)(2,1)S(1)} %collective-permute-done.6.sib_ref) | copy-start | bytes 344068
  32.6 9.2 %collective-permute-start.11 = (bf16[1536,128]{1,0:T(8,128)(2,1)S(1)}, bf16[1536,128]{1,0:T(8,128)(2,1)S(1)}, u32[]{:S(2)}, u32[]{:S(2)}) collective-permute-start(bf16[1536,128]{1,0:T(8,128)(2,1)S(1)} %pad_maximum_fusion.refs_2_), channel_id=1, source_target_pairs={{0,1},{1,0},{2,3},{3,2},{4,5},{5,4},{6,7},{7,6},{8,9},{9,8},{10,11... | collective-permute-start | bytes 1179656 | tf_op jit(solution)/shard_map/ppermute | solution.py:374
  39.9 1.9 %copy-start = (bf16[912,256]{1,0:T(8,128)(2,1)S(1)}, bf16[912,256]{1,0:T(8,128)(2,1)}, u32[]{:S(2)}) copy-start(bf16[912,256]{1,0:T(8,128)(2,1)} %first_tile.1.first_hbm) | copy-start | bytes 1400836
  40.0 1.8 %collective-permute-start.16 = (bf16[1152,128]{1,0:T(8,128)(2,1)S(1)}, bf16[1152,128]{1,0:T(8,128)(2,1)S(1)}, u32[]{:S(2)}, u32[]{:S(2)}) collective-permute-start(bf16[1152,128]{1,0:T(8,128)(2,1)S(1)} %get-tuple-element.24), channel_id=1, source_target_pairs={{0,1},{1,0},{2,3},{3,2},{4,5},{5,4},{6,7},{7,6},{8,9},{9,8},{10,11... | collective-permute-start | bytes 884744 | tf_op jit(solution)/shard_map/ppermute | solution.py:374
  40.2 1.6 %collective-permute-start.15 = (bf16[384,128]{1,0:T(8,128)(2,1)S(1)}, bf16[384,128]{1,0:T(8,128)(2,1)S(1)}, u32[]{:S(2)}, u32[]{:S(2)}) collective-permute-start(bf16[384,128]{1,0:T(8,128)(2,1)S(1)} %get-tuple-element.26), channel_id=1, source_target_pairs={{0,1},{1,0},{2,3},{3,2},{4,5},{5,4},{6,7},{7,6},{8,9},{9,8},{10,11... | collective-permute-start | bytes 294920 | tf_op jit(solution)/shard_map/ppermute | solution.py:374

commit v5 on v4

--- a/solution.py
+++ b/solution.py
@@ -279,7 +279,7 @@
     tail = tail[0:1, :] + tail[1:2, :] + tail[2:3, :]
     sq0, diag0 = tail[:, 0:width], jnp.where(eye, tail[:, width:], 0.0)
 
-    def panel_of(x, sq, heads):
+    def kern_of(x, sq, heads):
         gram = jnp.dot(x, first_ref[0:whole, :], preferred_element_type=jnp.float32)
         gram = gram[:, 0:width] + gram[:, width:]
         kern = jnp.exp(gram - 0.5 * (sq + sq0))
@@ -291,7 +291,7 @@
             if len(heads) * width < kern.shape[0]:
                 tops.append(kern[len(heads) * width :])
             kern = jnp.concatenate(tops, axis=0)
-        return nt(three(kern), inv)
+        return kern
 
     c_hi, c_lo, c_sq, c_panel = [], [], [], []
     for t in range(4):
@@ -304,36 +304,44 @@
         c_lo.append(lo)
         c_sq.append(jnp.sum(partial.T, axis=0, keepdims=True))
         sq = jnp.sum(partial, axis=1, keepdims=True)
-        c_panel.append(panel_of(c, sq, [col_id == 0] if t == 0 else []))
+        c_panel.append(kern_of(c, sq, [col_id == 0] if t == 0 else []))
     c_hi, c_lo = jnp.concatenate(c_hi, axis=0), jnp.concatenate(c_lo, axis=0)
     c_sq = jnp.concatenate(c_sq, axis=1)
-    c_panel = twice(jnp.concatenate(c_panel, axis=0))
-
-    outs = []
+    c_panel = twice(nt(three(jnp.concatenate(c_panel, axis=0)), inv))
+
+    outs, xs, sqs, kerns = [], [], [], []
     for t in range(4):
         x = jnp.concatenate([dense(row_own, t, width, depth), dense(row_oth, t, width, depth)], axis=0)
         xf = x.astype(jnp.float32)
         sq = jnp.sum(squares(xf, xf * w), axis=1, keepdims=True)
         heads = [(row_id == 0) & (parity == h) for h in range(2)] if t == 0 else []
-        panel = panel_of(x, sq, heads)
-        gram = nt(x, c_hi) + nt(x, c_lo)
-        kern = jnp.exp(gram - 0.5 * (sq + c_sq))
-        trail = kern - nt(three(panel), c_panel)
+        xs.append(x)
+        sqs.append(sq)
+        kerns.append(kern_of(x, sq, heads))
+    parts = []
+    for t in range(4):
+        panel = nt(three(kerns[t]), inv)
+        parts.append(three(panel))
+        for half in range(2):
+            tile = 2 * t + (parity if half == 0 else 1 - parity)
+            panel_ref[tile] = panel[half * width : (half + 1) * width]
+            outs.append(pltpu.make_async_copy(panel_ref.at[tile], panel_hbm.at[tile], sems.at[1 + 2 * t + half]))
+            outs[-1].start()
+    for t in range(4):
+        gram = nt(xs[t], c_hi) + nt(xs[t], c_lo)
+        update = nt(parts[t], c_panel)
+        trail = jnp.exp(gram - 0.5 * (sqs[t] + c_sq)) - update
         for half in range(2):
             tile = 2 * t + (parity if half == 0 else 1 - parity)
             low = half * width
-            panel_ref[tile] = panel[low : low + width]
             for tc in range(4):
                 block = trail[low : low + width, tc * width : (tc + 1) * width]
                 if half == 0 and tc == t:
                     block = block + jnp.where(eye & on_diag, noise_ref[pl.ds(tile, 1), :], 0.0)
                 trail_ref[pl.ds(tile * (4 * width) + tc, width, stride=4), :] = block
             span = pl.ds(tile * (4 * width), 4 * width)
-            for n, (src, dst) in enumerate(
-                ((panel_ref.at[tile], panel_hbm.at[tile]), (trail_ref.at[span], trail_hbm.at[span]))
-            ):
-                outs.append(pltpu.make_async_copy(src, dst, sems.at[1 + 4 * t + 2 * half + n]))
-                outs[-1].start()
+            outs.append(pltpu.make_async_copy(trail_ref.at[span], trail_hbm.at[span], sems.at[9 + 2 * t + half]))
+            outs[-1].start()
     for copy in outs:
         copy.wait()
 

time: 49.5 us -> 48.4 us (0.978)
  Pallas kernels: 15.8 us -> 14.7 us
    pallas_call x1, Pallas kernels: 7.36 us -> 6.27 us  [rest(): pl.pallas_call(functools.partial(rest_kernel, depth), out_shape=(jax.Shap...]
where the time goes in v5:
time: 48.4 us; the launch traced here: 48.1 us
  starting transfers between devices  21.8 us (45%)
  Pallas kernels  14.7 us (30%)
  waiting for transfers between devices  6.18 us (13%)
  other arithmetic  2.44 us (5%)
  local copies, waits for them, and re-layouts  2.17 us (4%)
  between operations  0.8 us (2%)
    ppermute x11, starting transfers between devices, over_col(): return lax.ppermute(x, 'col', [(i, i ^ k) for i in range(n_cols)])  12.7 us
    ppermute x6, starting transfers between devices, over_row(): return lax.ppermute(x, 'row', [(i, i ^ k) for i in range(n_rows)])  9.02 us
    pallas_call x1, Pallas kernels, first_tile(): pl.pallas_call(first_kernel, out_shape=jax.ShapeDtypeStruct((whole + widt...  6.69 us
    pallas_call x1, Pallas kernels, rest(): pl.pallas_call(functools.partial(rest_kernel, depth), out_shape=(jax.Shap...  6.27 us
    ppermute x11, waiting for transfers between devices, over_col(): return lax.ppermute(x, 'col', [(i, i ^ k) for i in range(n_cols)])  6.17 us
    pallas_call x1, Pallas kernels, pack(): pl.pallas_call(pack_kernel, out_shape=(rows(3 * width), rows(3 * width),...  1.79 us
    unnamed x15, local copies, waits for them, and re-layouts  1.48 us
    dynamic_update_slice x1, other arithmetic, body(): q1 = over_col(lax.dynamic_update_slice(oth_long, head, (size, 0)), 2)  1.38 us
  transfers between devices with their start and end apart: 17, of which 4 were waited for; matrix products, arithmetic and copies ran while one was open for 8% of the time, Pallas kernels for 14%

profile of v5, /device:TPU:0, one launch (start us, length us, event | category | flops | bytes accessed | tf_op | source)
XLA Modules:
  0.0 48.1 jit_solution(14995831234205145851)
XLA Ops:
  0.6 1.8 %pack.1 = (bf16[384,128]{1,0:T(8,128)(2,1)}, bf16[384,128]{1,0:T(8,128)(2,1)}, bf16[496,128]{1,0:T(8,128)(2,1)}, bf16[496,128]{1,0:T(8,128)(2,1)}) custom-call(bf16[8,96,128]{2,1,0:T(8,128)(2,1)} %bitcast.5, f32[8,128]{1,0:T(8,128)} %noise_ref.3), custom_call_target="tpu_custom_call" | custom-call | tf_op jit(solution)/shard_map/pack/pallas_call | solution.py:56
  2.4 3.9 %collective-permute-start.2 = (bf16[496,128]{1,0:T(8,128)(2,1)}, bf16[496,128]{1,0:T(8,128)(2,1)S(1)}, u32[]{:S(2)}, u32[]{:S(2)}) collective-permute-start(bf16[496,128]{1,0:T(8,128)(2,1)} %get-tuple-element.12), channel_id=1, source_target_pairs={{0,24},{8,16},{16,8},{24,0},{1,25},{9,17},{17,9},{25,1},{2,26},{10... | collective-permute-start | bytes 380936 | tf_op jit(solution)/shard_map/ppermute | solution.py:379
  6.3 0.5 %collective-permute-start.1 = (bf16[496,128]{1,0:T(8,128)(2,1)}, bf16[496,128]{1,0:T(8,128)(2,1)S(1)}, u32[]{:S(2)}, u32[]{:S(2)}) collective-permute-start(bf16[496,128]{1,0:T(8,128)(2,1)} %get-tuple-element.12), channel_id=1, source_target_pairs={{0,16},{8,24},{16,0},{24,8},{1,17},{9,25},{17,1},{25,9},{2,18},{10... | collective-permute-start | bytes 380936 | tf_op jit(solution)/shard_map/ppermute | solution.py:379
  6.9 2.0 %collective-permute-start.7 = (bf16[384,128]{1,0:T(8,128)(2,1)}, bf16[384,128]{1,0:T(8,128)(2,1)S(1)}, u32[]{:S(2)}, u32[]{:S(2)}) collective-permute-start(bf16[384,128]{1,0:T(8,128)(2,1)} %get-tuple-element.14), channel_id=1, source_target_pairs={{0,2},{1,3},{2,0},{3,1},{4,6},{5,7},{6,4},{7,5},{8,10},{9,11},{10,... | collective-permute-start | bytes 294920 | tf_op jit(solution)/shard_map/ppermute | solution.py:382
  8.9 2.5 %collective-permute-start.9 = (bf16[384,128]{1,0:T(8,128)(2,1)}, bf16[384,128]{1,0:T(8,128)(2,1)S(1)}, u32[]{:S(2)}, u32[]{:S(2)}) collective-permute-start(bf16[384,128]{1,0:T(8,128)(2,1)} %get-tuple-element.15), channel_id=1, source_target_pairs={{0,6},{1,7},{2,4},{3,5},{4,2},{5,3},{6,0},{7,1},{8,14},{9,15},{10,... | collective-permute-start | bytes 294920 | tf_op jit(solution)/shard_map/ppermute | solution.py:382
  11.4 0.9 %constant_dynamic-update-slice_fusion.3 = bf16[1536,128]{1,0:T(8,128)(2,1)S(1)} fusion(bf16[384,128]{1,0:T(8,128)(2,1)} %get-tuple-element.14), kind=kLoop, calls=%fused_computation.12 | loop fusion | bytes 196608
  12.3 2.6 %collective-permute-start.8 = (bf16[384,128]{1,0:T(8,128)(2,1)}, bf16[384,128]{1,0:T(8,128)(2,1)S(1)}, u32[]{:S(2)}, u32[]{:S(2)}) collective-permute-start(bf16[384,128]{1,0:T(8,128)(2,1)} %get-tuple-element.15), channel_id=1, source_target_pairs={{0,4},{1,5},{2,6},{3,7},{4,0},{5,1},{6,2},{7,3},{8,12},{9,13},{10,... | collective-permute-start | bytes 294920 | tf_op jit(solution)/shard_map/ppermute | solution.py:382
  15.0 1.4 %constant_dynamic-update-slice_fusion.8 = (bf16[496,128]{1,0:T(8,128)(2,1)}, bf16[112,128]{1,0:T(8,128)(2,1)S(1)}) fusion(bf16[496,128]{1,0:T(8,128)(2,1)} %get-tuple-element.13, bf16[496,128]{1,0:T(8,128)(2,1)S(1)} %collective-permute-done.2, bf16[496,128]{1,0:T(8,128)(2,1)S(1)} %collective-permute-done.1, pred[]{:T(512)S(6)} %select_n.135, ...), kind=kLoop, calls=%fused_computation.17 | loop fusion | flops 43008 | bytes 172035 | tf_op jit(solution)/shard_map/dynamic_update_slice | solution.py:395
  16.4 0.9 %select_select_fusion.2 = (bf16[384,128]{1,0:T(8,128)(2,1)S(1)}, bf16[384,128]{1,0:T(8,128)(2,1)S(1)}) fusion(pred[]{:T(512)S(6)} %select_n.160, pred[]{:T(512)S(6)} %select_n.157, pred[]{:T(512)S(6)} %select_n.155, bf16[496,128]{1,0:T(8,128)(2,1)S(1)} %collective-permute-done.2, bf16[496,128]{1,0:T(8,128)(2,1)S(1)} %collective-permute-done.1, ...), kind=kLoop, calls=%fused_computation.4 | loop fusion | flops 294912 | bytes 589830 | tf_op jit(solution)/shard_map/select_n | solution.py:408
  17.3 0.6 %constant_dynamic-update-slice_fusion.7 = bf16[496,128]{1,0:T(8,128)(2,1)} fusion(bf16[496,128]{1,0:T(8,128)(2,1)} %get-tuple-element.12, bf16[112,128]{1,0:T(8,128)(2,1)S(1)} %get-tuple-element.23), kind=kLoop, calls=%fused_computation.16 | loop fusion | bytes 57344 | tf_op jit(solution)/shard_map/dynamic_update_slice | solution.py:396
  17.9 2.0 %collective-permute-start.5 = (bf16[496,128]{1,0:T(8,128)(2,1)}, bf16[496,128]{1,0:T(8,128)(2,1)S(1)}, u32[]{:S(2)}, u32[]{:S(2)}) collective-permute-start(bf16[496,128]{1,0:T(8,128)(2,1)} %constant_dynamic-update-slice_fusion.7), channel_id=1, source_target_pairs={{0,6},{1,7},{2,4},{3,5},{4,2},{5,3},{6,0},{7,1},{8,14},{9,15},{10,... | collective-permute-start | bytes 380936 | tf_op jit(solution)/shard_map/ppermute | solution.py:382
  19.9 1.9 %collective-permute-start.4 = (bf16[496,128]{1,0:T(8,128)(2,1)}, bf16[496,128]{1,0:T(8,128)(2,1)S(1)}, u32[]{:S(2)}, u32[]{:S(2)}) collective-permute-start(bf16[496,128]{1,0:T(8,128)(2,1)} %constant_dynamic-update-slice_fusion.7), channel_id=1, source_target_pairs={{0,4},{1,5},{2,6},{3,7},{4,0},{5,1},{6,2},{7,3},{8,12},{9,13},{10,... | collective-permute-start | bytes 380936 | tf_op jit(solution)/shard_map/ppermute | solution.py:382
  21.9 0.4 collective-permute-start.3
  22.4 2.5 %collective-permute-start.14 = (bf16[1152,128]{1,0:T(8,128)(2,1)S(1)}, bf16[1152,128]{1,0:T(8,128)(2,1)S(1)}, u32[]{:S(2)}, u32[]{:S(2)}) collective-permute-start(bf16[1152,128]{1,0:T(8,128)(2,1)S(1)} %get-tuple-element.16), channel_id=1, source_target_pairs={{0,24},{8,16},{16,8},{24,0},{1,25},{9,17},{17,9},{25,1},{2,26},{10... | collective-permute-start | bytes 884744 | tf_op jit(solution)/shard_map/ppermute | solution.py:379
  24.9 0.5 %collective-permute-start.13 = (bf16[1152,128]{1,0:T(8,128)(2,1)S(1)}, bf16[1152,128]{1,0:T(8,128)(2,1)S(1)}, u32[]{:S(2)}, u32[]{:S(2)}) collective-permute-start(bf16[1152,128]{1,0:T(8,128)(2,1)S(1)} %get-tuple-element.16), channel_id=1, source_target_pairs={{0,16},{8,24},{16,0},{24,8},{1,17},{9,25},{17,1},{25,9},{2,18},{10... | collective-permute-start | bytes 884744 | tf_op jit(solution)/shard_map/ppermute | solution.py:379
  25.8 1.5 %collective-permute-start.12 = (bf16[1152,128]{1,0:T(8,128)(2,1)S(1)}, bf16[1152,128]{1,0:T(8,128)(2,1)S(1)}, u32[]{:S(2)}, u32[]{:S(2)}) collective-permute-start(bf16[1152,128]{1,0:T(8,128)(2,1)S(1)} %get-tuple-element.16), channel_id=1, source_target_pairs={{0,8},{8,0},{16,24},{24,16},{1,9},{9,1},{17,25},{25,17},{2,10},{10... | collective-permute-start | bytes 884744 | tf_op jit(solution)/shard_map/ppermute | solution.py:379
  27.3 3.4 %collective-permute-done.4 = bf16[496,128]{1,0:T(8,128)(2,1)S(1)} collective-permute-done((bf16[496,128]{1,0:T(8,128)(2,1)}, bf16[496,128]{1,0:T(8,128)(2,1)S(1)}, u32[]{:S(2)}, u32[]{:S(2)}) %collective-permute-start.4) | collective-permute-done | bytes 127008 | tf_op jit(solution)/shard_map/ppermute | solution.py:382
  30.7 0.6 %collective-permute-start.6 = (bf16[448,128]{1,0:T(8,128)(2,1)S(1)}, bf16[448,128]{1,0:T(8,128)(2,1)S(1)}, u32[]{:S(2)}, u32[]{:S(2)}) collective-permute-start(bf16[448,128]{1,0:T(8,128)(2,1)S(1)} %pad_maximum_fusion.1.mine_ref), channel_id=1, source_target_pairs={{0,1},{1,0},{2,3},{3,2},{4,5},{5,4},{6,7},{7,6},{8,9},{9,8},{10,11... | collective-permute-start | bytes 344072 | tf_op jit(solution)/shard_map/ppermute | solution.py:382
  31.4 1.2 %collective-permute-done.6.sib_ref = bf16[448,128]{1,0:T(8,128)(2,1)S(1)} collective-permute-done((bf16[448,128]{1,0:T(8,128)(2,1)S(1)}, bf16[448,128]{1,0:T(8,128)(2,1)S(1)}, u32[]{:S(2)}, u32[]{:S(2)}) %collective-permute-start.6) | collective-permute-done | bytes 114720 | tf_op jit(solution)/shard_map/ppermute | solution.py:382
  32.7 0.5 %copy-done.4 = bf16[448,128]{1,0:T(8,128)(2,1)} copy-done((bf16[448,128]{1,0:T(8,128)(2,1)}, bf16[448,128]{1,0:T(8,128)(2,1)S(1)}, u32[]{:S(2)}) %copy-start.4) | copy-done | bytes 114712
  33.2 6.7 %first_tile.1.first_hbm = bf16[912,256]{1,0:T(8,128)(2,1)} custom-call(f32[6,128]{1,0:T(8,128)} %bitcast.3, bf16[448,128]{1,0:T(8,128)(2,1)} %copy-done.3, bf16[448,128]{1,0:T(8,128)(2,1)} %copy-done.4), custom_call_target="tpu_custom_call" | custom-call | tf_op jit(solution)/shard_map/first_tile/pallas_call | solution.py:202
  40.2 0.4 collective-permute-start.15
  40.6 1.2 %collective-permute-done.15.refs_6_ = bf16[384,128]{1,0:T(8,128)(2,1)S(1)} collective-permute-done((bf16[384,128]{1,0:T(8,128)(2,1)S(1)}, bf16[384,128]{1,0:T(8,128)(2,1)S(1)}, u32[]{:S(2)}, u32[]{:S(2)}) %collective-permute-start.15) | collective-permute-done | bytes 98336 | tf_op jit(solution)/shard_map/ppermute | solution.py:382
  41.8 6.3 %rest.1 = (f32[8,128,128]{2,1,0:T(8,128)}, f32[4096,128]{1,0:T(8,128)}) custom-call(f32[6,128]{1,0:T(8,128)S(1)} %bitcast.4, f32[8,128]{1,0:T(8,128)S(1)} %copy-done.2, bf16[912,256]{1,0:T(8,128)(2,1)S(1)} %copy-done, bf16[1536,128]{1,0:T(8,128)(2,1)S(1)} %get-tuple-element.29.refs_0_, bf16[1536,128]{1,0:T(8,128)(2,1)S(1)} %collective-permute-done.10.refs_1_, ...), custom_call_target="tpu_custom_call" | custom-call | tf_op jit(solution)/shard_map/rest/pallas_call | solution.py:351
  (41 shorter events, 1.1 us)
Async XLA Ops:
  2.4 28.9 %copy-start.5 = (bf16[384,128]{1,0:T(8,128)(2,1)S(1)}, bf16[384,128]{1,0:T(8,128)(2,1)}, u32[]{:S(2)}) copy-start(bf16[384,128]{1,0:T(8,128)(2,1)} %get-tuple-element.15) | copy-start | bytes 294916
  2.4 12.5 %collective-permute-start.2 = (bf16[496,128]{1,0:T(8,128)(2,1)}, bf16[496,128]{1,0:T(8,128)(2,1)S(1)}, u32[]{:S(2)}, u32[]{:S(2)}) collective-permute-start(bf16[496,128]{1,0:T(8,128)(2,1)} %get-tuple-element.12), channel_id=1, source_target_pairs={{0,24},{8,16},{16,8},{24,0},{1,25},{9,17},{17,9},{25,1},{2,26},{10... | collective-permute-start | bytes 380936 | tf_op jit(solution)/shard_map/ppermute | solution.py:379
  6.3 8.6 %collective-permute-start.1 = (bf16[496,128]{1,0:T(8,128)(2,1)}, bf16[496,128]{1,0:T(8,128)(2,1)S(1)}, u32[]{:S(2)}, u32[]{:S(2)}) collective-permute-start(bf16[496,128]{1,0:T(8,128)(2,1)} %get-tuple-element.12), channel_id=1, source_target_pairs={{0,16},{8,24},{16,0},{24,8},{1,17},{9,25},{17,1},{25,9},{2,18},{10... | collective-permute-start | bytes 380936 | tf_op jit(solution)/shard_map/ppermute | solution.py:379
  6.8 8.2 %collective-permute-start = (bf16[496,128]{1,0:T(8,128)(2,1)}, bf16[496,128]{1,0:T(8,128)(2,1)S(1)}, u32[]{:S(2)}, u32[]{:S(2)}) collective-permute-start(bf16[496,128]{1,0:T(8,128)(2,1)} %get-tuple-element.12), channel_id=1, source_target_pairs={{0,8},{8,0},{16,24},{24,16},{1,9},{9,1},{17,25},{25,17},{2,10},{10... | collective-permute-start | bytes 380936 | tf_op jit(solution)/shard_map/ppermute | solution.py:379
  6.9 5.4 %collective-permute-start.7 = (bf16[384,128]{1,0:T(8,128)(2,1)}, bf16[384,128]{1,0:T(8,128)(2,1)S(1)}, u32[]{:S(2)}, u32[]{:S(2)}) collective-permute-start(bf16[384,128]{1,0:T(8,128)(2,1)} %get-tuple-element.14), channel_id=1, source_target_pairs={{0,2},{1,3},{2,0},{3,1},{4,6},{5,7},{6,4},{7,5},{8,10},{9,11},{10,... | collective-permute-start | bytes 294920 | tf_op jit(solution)/shard_map/ppermute | solution.py:382
  8.9 13.4 %collective-permute-start.9 = (bf16[384,128]{1,0:T(8,128)(2,1)}, bf16[384,128]{1,0:T(8,128)(2,1)S(1)}, u32[]{:S(2)}, u32[]{:S(2)}) collective-permute-start(bf16[384,128]{1,0:T(8,128)(2,1)} %get-tuple-element.15), channel_id=1, source_target_pairs={{0,6},{1,7},{2,4},{3,5},{4,2},{5,3},{6,0},{7,1},{8,14},{9,15},{10,... | collective-permute-start | bytes 294920 | tf_op jit(solution)/shard_map/ppermute | solution.py:382
  12.3 10.0 %collective-permute-start.8 = (bf16[384,128]{1,0:T(8,128)(2,1)}, bf16[384,128]{1,0:T(8,128)(2,1)S(1)}, u32[]{:S(2)}, u32[]{:S(2)}) collective-permute-start(bf16[384,128]{1,0:T(8,128)(2,1)} %get-tuple-element.15), channel_id=1, source_target_pairs={{0,4},{1,5},{2,6},{3,7},{4,0},{5,1},{6,2},{7,3},{8,12},{9,13},{10,... | collective-permute-start | bytes 294920 | tf_op jit(solution)/shard_map/ppermute | solution.py:382
  17.9 7.9 %collective-permute-start.5 = (bf16[496,128]{1,0:T(8,128)(2,1)}, bf16[496,128]{1,0:T(8,128)(2,1)S(1)}, u32[]{:S(2)}, u32[]{:S(2)}) collective-permute-start(bf16[496,128]{1,0:T(8,128)(2,1)} %constant_dynamic-update-slice_fusion.7), channel_id=1, source_target_pairs={{0,6},{1,7},{2,4},{3,5},{4,2},{5,3},{6,0},{7,1},{8,14},{9,15},{10,... | collective-permute-start | bytes 380936 | tf_op jit(solution)/shard_map/ppermute | solution.py:382
  19.9 10.7 %collective-permute-start.4 = (bf16[496,128]{1,0:T(8,128)(2,1)}, bf16[496,128]{1,0:T(8,128)(2,1)S(1)}, u32[]{:S(2)}, u32[]{:S(2)}) collective-permute-start(bf16[496,128]{1,0:T(8,128)(2,1)} %constant_dynamic-update-slice_fusion.7), channel_id=1, source_target_pairs={{0,4},{1,5},{2,6},{3,7},{4,0},{5,1},{6,2},{7,3},{8,12},{9,13},{10,... | collective-permute-start | bytes 380936 | tf_op jit(solution)/shard_map/ppermute | solution.py:382
  21.9 8.8 %collective-permute-start.3 = (bf16[496,128]{1,0:T(8,128)(2,1)}, bf16[496,128]{1,0:T(8,128)(2,1)S(1)}, u32[]{:S(2)}, u32[]{:S(2)}) collective-permute-start(bf16[496,128]{1,0:T(8,128)(2,1)} %get-tuple-element.22), channel_id=1, source_target_pairs={{0,2},{1,3},{2,0},{3,1},{4,6},{5,7},{6,4},{7,5},{8,10},{9,11},{10,... | collective-permute-start | bytes 380936 | tf_op jit(solution)/shard_map/ppermute | solution.py:382
  22.4 17.5 %collective-permute-start.14 = (bf16[1152,128]{1,0:T(8,128)(2,1)S(1)}, bf16[1152,128]{1,0:T(8,128)(2,1)S(1)}, u32[]{:S(2)}, u32[]{:S(2)}) collective-permute-start(bf16[1152,128]{1,0:T(8,128)(2,1)S(1)} %get-tuple-element.16), channel_id=1, source_target_pairs={{0,24},{8,16},{16,8},{24,0},{1,25},{9,17},{17,9},{25,1},{2,26},{10... | collective-permute-start | bytes 884744 | tf_op jit(solution)/shard_map/ppermute | solution.py:379
  24.9 15.0 %collective-permute-start.13 = (bf16[1152,128]{1,0:T(8,128)(2,1)S(1)}, bf16[1152,128]{1,0:T(8,128)(2,1)S(1)}, u32[]{:S(2)}, u32[]{:S(2)}) collective-permute-start(bf16[1152,128]{1,0:T(8,128)(2,1)S(1)} %get-tuple-element.16), channel_id=1, source_target_pairs={{0,16},{8,24},{16,0},{24,8},{1,17},{9,25},{17,1},{25,9},{2,18},{10... | collective-permute-start | bytes 884744 | tf_op jit(solution)/shard_map/ppermute | solution.py:379
  25.8 14.1 %collective-permute-start.12 = (bf16[1152,128]{1,0:T(8,128)(2,1)S(1)}, bf16[1152,128]{1,0:T(8,128)(2,1)S(1)}, u32[]{:S(2)}, u32[]{:S(2)}) collective-permute-start(bf16[1152,128]{1,0:T(8,128)(2,1)S(1)} %get-tuple-element.16), channel_id=1, source_target_pairs={{0,8},{8,0},{16,24},{24,16},{1,9},{9,1},{17,25},{25,17},{2,10},{10... | collective-permute-start | bytes 884744 | tf_op jit(solution)/shard_map/ppermute | solution.py:379
  30.7 11.1 %copy-start.1 = (f32[768]{0:T(1024)S(1)}, f32[768]{0:T(1024)}, u32[]{:S(2)}) copy-start(f32[768]{0:T(1024)} %param.4) | copy-start | bytes 9220
  30.7 11.2 %copy-start.2 = (f32[8,128]{1,0:T(8,128)S(1)}, f32[8,128]{1,0:T(8,128)}, u32[]{:S(2)}) copy-start(f32[8,128]{1,0:T(8,128)} %noise_ref.3) | copy-start | bytes 12292
  30.7 11.1 %collective-permute-start.10 = (bf16[1536,128]{1,0:T(8,128)(2,1)S(1)}, bf16[1536,128]{1,0:T(8,128)(2,1)S(1)}, u32[]{:S(2)}, u32[]{:S(2)}) collective-permute-start(bf16[1536,128]{1,0:T(8,128)(2,1)S(1)} %get-tuple-element.29.refs_0_), channel_id=1, source_target_pairs={{0,1},{1,0},{2,3},{3,2},{4,5},{5,4},{6,7},{7,6},{8,9},{9,8},{10,11... | collective-permute-start | bytes 1179656 | tf_op jit(solution)/shard_map/ppermute | solution.py:382
  30.7 2.0 %copy-start.3 = (bf16[448,128]{1,0:T(8,128)(2,1)}, bf16[448,128]{1,0:T(8,128)(2,1)S(1)}, u32[]{:S(2)}) copy-start(bf16[448,128]{1,0:T(8,128)(2,1)S(1)} %pad_maximum_fusion.1.mine_ref) | copy-start | bytes 344068
  30.7 1.8 %collective-permute-start.6 = (bf16[448,128]{1,0:T(8,128)(2,1)S(1)}, bf16[448,128]{1,0:T(8,128)(2,1)S(1)}, u32[]{:S(2)}, u32[]{:S(2)}) collective-permute-start(bf16[448,128]{1,0:T(8,128)(2,1)S(1)} %pad_maximum_fusion.1.mine_ref), channel_id=1, source_target_pairs={{0,1},{1,0},{2,3},{3,2},{4,5},{5,4},{6,7},{7,6},{8,9},{9,8},{10,11... | collective-permute-start | bytes 344072 | tf_op jit(solution)/shard_map/ppermute | solution.py:382
  32.6 0.6 %copy-start.4 = (bf16[448,128]{1,0:T(8,128)(2,1)}, bf16[448,128]{1,0:T(8,128)(2,1)S(1)}, u32[]{:S(2)}) copy-start(bf16[448,128]{1,0:T(8,128)(2,1)S(1)} %collective-permute-done.6.sib_ref) | copy-start | bytes 344068
  32.6 9.2 %collective-permute-start.11 = (bf16[1536,128]{1,0:T(8,128)(2,1)S(1)}, bf16[1536,128]{1,0:T(8,128)(2,1)S(1)}, u32[]{:S(2)}, u32[]{:S(2)}) collective-permute-start(bf16[1536,128]{1,0:T(8,128)(2,1)S(1)} %pad_maximum_fusion.refs_2_), channel_id=1, source_target_pairs={{0,1},{1,0},{2,3},{3,2},{4,5},{5,4},{6,7},{7,6},{8,9},{9,8},{10,11... | collective-permute-start | bytes 1179656 | tf_op jit(solution)/shard_map/ppermute | solution.py:382
  39.9 1.9 %copy-start = (bf16[912,256]{1,0:T(8,128)(2,1)S(1)}, bf16[912,256]{1,0:T(8,128)(2,1)}, u32[]{:S(2)}) copy-start(bf16[912,256]{1,0:T(8,128)(2,1)} %first_tile.1.first_hbm) | copy-start | bytes 1400836
  40.0 1.8 %collective-permute-start.16 = (bf16[1152,128]{1,0:T(8,128)(2,1)S(1)}, bf16[1152,128]{1,0:T(8,128)(2,1)S(1)}, u32[]{:S(2)}, u32[]{:S(2)}) collective-permute-start(bf16[1152,128]{1,0:T(8,128)(2,1)S(1)} %get-tuple-element.24), channel_id=1, source_target_pairs={{0,1},{1,0},{2,3},{3,2},{4,5},{5,4},{6,7},{7,6},{8,9},{9,8},{10,11... | collective-permute-start | bytes 884744 | tf_op jit(solution)/shard_map/ppermute | solution.py:382
  40.2 1.6 %collective-permute-start.15 = (bf16[384,128]{1,0:T(8,128)(2,1)S(1)}, bf16[384,128]{1,0:T(8,128)(2,1)S(1)}, u32[]{:S(2)}, u32[]{:S(2)}) collective-permute-start(bf16[384,128]{1,0:T(8,128)(2,1)S(1)} %get-tuple-element.26), channel_id=1, source_target_pairs={{0,1},{1,0},{2,3},{3,2},{4,5},{5,4},{6,7},{7,6},{8,9},{9,8},{10,11... | collective-permute-start | bytes 294920 | tf_op jit(solution)/shard_map/ppermute | solution.py:382

commit v6 on v5

--- a/solution.py
+++ b/solution.py
@@ -359,7 +359,7 @@
         scratch_shapes=[
             pltpu.VMEM(first.shape, first.dtype),
             pltpu.VMEM((tiles, width, width), jnp.float32),
-            pltpu.VMEM((tiles * width * 4, width), jnp.float32),
+            pltpu.VMEM((tiles * width * 4 + 8, width), jnp.float32),
             pltpu.SemaphoreType.DMA((17,)),
         ],
         compiler_params=pltpu.CompilerParams(vmem_limit_bytes=VMEM_REST * 1024 * 1024),

time: 48.4 us -> 48.4 us (level)
  no operation moved by 1% of the time
where the time goes in v6:
time: 48.4 us; the launch traced here: 48.1 us
  starting transfers between devices  21.8 us (45%)
  Pallas kernels  14.7 us (30%)
  waiting for transfers between devices  6.18 us (13%)
  other arithmetic  2.44 us (5%)
  local copies, waits for them, and re-layouts  2.17 us (4%)
  between operations  0.8 us (2%)
    ppermute x11, starting transfers between devices, over_col(): return lax.ppermute(x, 'col', [(i, i ^ k) for i in range(n_cols)])  12.7 us
    ppermute x6, starting transfers between devices, over_row(): return lax.ppermute(x, 'row', [(i, i ^ k) for i in range(n_rows)])  9.02 us
    pallas_call x1, Pallas kernels, first_tile(): pl.pallas_call(first_kernel, out_shape=jax.ShapeDtypeStruct((whole + widt...  6.69 us
    pallas_call x1, Pallas kernels, rest(): pl.pallas_call(functools.partial(rest_kernel, depth), out_shape=(jax.Shap...  6.27 us
    ppermute x11, waiting for transfers between devices, over_col(): return lax.ppermute(x, 'col', [(i, i ^ k) for i in range(n_cols)])  6.17 us
    pallas_call x1, Pallas kernels, pack(): pl.pallas_call(pack_kernel, out_shape=(rows(3 * width), rows(3 * width),...  1.79 us
    unnamed x15, local copies, waits for them, and re-layouts  1.48 us
    dynamic_update_slice x1, other arithmetic, body(): q1 = over_col(lax.dynamic_update_slice(oth_long, head, (size, 0)), 2)  1.38 us
  transfers between devices with their start and end apart: 17, of which 4 were waited for; matrix products, arithmetic and copies ran while one was open for 8% of the time, Pallas kernels for 14%

profile of v6, /device:TPU:0, one launch (start us, length us, event | category | flops | bytes accessed | tf_op | source)
XLA Modules:
  0.0 48.1 jit_solution(11642309375538831598)
XLA Ops:
  0.6 1.8 %pack.1 = (bf16[384,128]{1,0:T(8,128)(2,1)}, bf16[384,128]{1,0:T(8,128)(2,1)}, bf16[496,128]{1,0:T(8,128)(2,1)}, bf16[496,128]{1,0:T(8,128)(2,1)}) custom-call(bf16[8,96,128]{2,1,0:T(8,128)(2,1)} %bitcast.5, f32[8,128]{1,0:T(8,128)} %noise_ref.3), custom_call_target="tpu_custom_call" | custom-call | tf_op jit(solution)/shard_map/pack/pallas_call | solution.py:56
  2.4 3.9 %collective-permute-start.2 = (bf16[496,128]{1,0:T(8,128)(2,1)}, bf16[496,128]{1,0:T(8,128)(2,1)S(1)}, u32[]{:S(2)}, u32[]{:S(2)}) collective-permute-start(bf16[496,128]{1,0:T(8,128)(2,1)} %get-tuple-element.12), channel_id=1, source_target_pairs={{0,24},{8,16},{16,8},{24,0},{1,25},{9,17},{17,9},{25,1},{2,26},{10... | collective-permute-start | bytes 380936 | tf_op jit(solution)/shard_map/ppermute | solution.py:379
  6.3 0.5 %collective-permute-start.1 = (bf16[496,128]{1,0:T(8,128)(2,1)}, bf16[496,128]{1,0:T(8,128)(2,1)S(1)}, u32[]{:S(2)}, u32[]{:S(2)}) collective-permute-start(bf16[496,128]{1,0:T(8,128)(2,1)} %get-tuple-element.12), channel_id=1, source_target_pairs={{0,16},{8,24},{16,0},{24,8},{1,17},{9,25},{17,1},{25,9},{2,18},{10... | collective-permute-start | bytes 380936 | tf_op jit(solution)/shard_map/ppermute | solution.py:379
  6.9 2.0 %collective-permute-start.7 = (bf16[384,128]{1,0:T(8,128)(2,1)}, bf16[384,128]{1,0:T(8,128)(2,1)S(1)}, u32[]{:S(2)}, u32[]{:S(2)}) collective-permute-start(bf16[384,128]{1,0:T(8,128)(2,1)} %get-tuple-element.14), channel_id=1, source_target_pairs={{0,2},{1,3},{2,0},{3,1},{4,6},{5,7},{6,4},{7,5},{8,10},{9,11},{10,... | collective-permute-start | bytes 294920 | tf_op jit(solution)/shard_map/ppermute | solution.py:382
  8.9 2.5 %collective-permute-start.9 = (bf16[384,128]{1,0:T(8,128)(2,1)}, bf16[384,128]{1,0:T(8,128)(2,1)S(1)}, u32[]{:S(2)}, u32[]{:S(2)}) collective-permute-start(bf16[384,128]{1,0:T(8,128)(2,1)} %get-tuple-element.15), channel_id=1, source_target_pairs={{0,6},{1,7},{2,4},{3,5},{4,2},{5,3},{6,0},{7,1},{8,14},{9,15},{10,... | collective-permute-start | bytes 294920 | tf_op jit(solution)/shard_map/ppermute | solution.py:382
  11.4 0.9 %constant_dynamic-update-slice_fusion.3 = bf16[1536,128]{1,0:T(8,128)(2,1)S(1)} fusion(bf16[384,128]{1,0:T(8,128)(2,1)} %get-tuple-element.14), kind=kLoop, calls=%fused_computation.12 | loop fusion | bytes 196608
  12.3 2.6 %collective-permute-start.8 = (bf16[384,128]{1,0:T(8,128)(2,1)}, bf16[384,128]{1,0:T(8,128)(2,1)S(1)}, u32[]{:S(2)}, u32[]{:S(2)}) collective-permute-start(bf16[384,128]{1,0:T(8,128)(2,1)} %get-tuple-element.15), channel_id=1, source_target_pairs={{0,4},{1,5},{2,6},{3,7},{4,0},{5,1},{6,2},{7,3},{8,12},{9,13},{10,... | collective-permute-start | bytes 294920 | tf_op jit(solution)/shard_map/ppermute | solution.py:382
  15.0 1.4 %constant_dynamic-update-slice_fusion.8 = (bf16[496,128]{1,0:T(8,128)(2,1)}, bf16[112,128]{1,0:T(8,128)(2,1)S(1)}) fusion(bf16[496,128]{1,0:T(8,128)(2,1)} %get-tuple-element.13, bf16[496,128]{1,0:T(8,128)(2,1)S(1)} %collective-permute-done.2, bf16[496,128]{1,0:T(8,128)(2,1)S(1)} %collective-permute-done.1, pred[]{:T(512)S(6)} %select_n.135, ...), kind=kLoop, calls=%fused_computation.17 | loop fusion | flops 43008 | bytes 172035 | tf_op jit(solution)/shard_map/dynamic_update_slice | solution.py:395
  16.4 0.9 %select_select_fusion.2 = (bf16[384,128]{1,0:T(8,128)(2,1)S(1)}, bf16[384,128]{1,0:T(8,128)(2,1)S(1)}) fusion(pred[]{:T(512)S(6)} %select_n.160, pred[]{:T(512)S(6)} %select_n.157, pred[]{:T(512)S(6)} %select_n.155, bf16[496,128]{1,0:T(8,128)(2,1)S(1)} %collective-permute-done.2, bf16[496,128]{1,0:T(8,128)(2,1)S(1)} %collective-permute-done.1, ...), kind=kLoop, calls=%fused_computation.4 | loop fusion | flops 294912 | bytes 589830 | tf_op jit(solution)/shard_map/select_n | solution.py:408
  17.3 0.6 %constant_dynamic-update-slice_fusion.7 = bf16[496,128]{1,0:T(8,128)(2,1)} fusion(bf16[496,128]{1,0:T(8,128)(2,1)} %get-tuple-element.12, bf16[112,128]{1,0:T(8,128)(2,1)S(1)} %get-tuple-element.23), kind=kLoop, calls=%fused_computation.16 | loop fusion | bytes 57344 | tf_op jit(solution)/shard_map/dynamic_update_slice | solution.py:396
  17.9 2.0 %collective-permute-start.5 = (bf16[496,128]{1,0:T(8,128)(2,1)}, bf16[496,128]{1,0:T(8,128)(2,1)S(1)}, u32[]{:S(2)}, u32[]{:S(2)}) collective-permute-start(bf16[496,128]{1,0:T(8,128)(2,1)} %constant_dynamic-update-slice_fusion.7), channel_id=1, source_target_pairs={{0,6},{1,7},{2,4},{3,5},{4,2},{5,3},{6,0},{7,1},{8,14},{9,15},{10,... | collective-permute-start | bytes 380936 | tf_op jit(solution)/shard_map/ppermute | solution.py:382
  19.9 1.9 %collective-permute-start.4 = (bf16[496,128]{1,0:T(8,128)(2,1)}, bf16[496,128]{1,0:T(8,128)(2,1)S(1)}, u32[]{:S(2)}, u32[]{:S(2)}) collective-permute-start(bf16[496,128]{1,0:T(8,128)(2,1)} %constant_dynamic-update-slice_fusion.7), channel_id=1, source_target_pairs={{0,4},{1,5},{2,6},{3,7},{4,0},{5,1},{6,2},{7,3},{8,12},{9,13},{10,... | collective-permute-start | bytes 380936 | tf_op jit(solution)/shard_map/ppermute | solution.py:382
  21.9 0.4 collective-permute-start.3
  22.4 2.5 %collective-permute-start.14 = (bf16[1152,128]{1,0:T(8,128)(2,1)S(1)}, bf16[1152,128]{1,0:T(8,128)(2,1)S(1)}, u32[]{:S(2)}, u32[]{:S(2)}) collective-permute-start(bf16[1152,128]{1,0:T(8,128)(2,1)S(1)} %get-tuple-element.16), channel_id=1, source_target_pairs={{0,24},{8,16},{16,8},{24,0},{1,25},{9,17},{17,9},{25,1},{2,26},{10... | collective-permute-start | bytes 884744 | tf_op jit(solution)/shard_map/ppermute | solution.py:379
  24.9 0.5 %collective-permute-start.13 = (bf16[1152,128]{1,0:T(8,128)(2,1)S(1)}, bf16[1152,128]{1,0:T(8,128)(2,1)S(1)}, u32[]{:S(2)}, u32[]{:S(2)}) collective-permute-start(bf16[1152,128]{1,0:T(8,128)(2,1)S(1)} %get-tuple-element.16), channel_id=1, source_target_pairs={{0,16},{8,24},{16,0},{24,8},{1,17},{9,25},{17,1},{25,9},{2,18},{10... | collective-permute-start | bytes 884744 | tf_op jit(solution)/shard_map/ppermute | solution.py:379
  25.8 1.5 %collective-permute-start.12 = (bf16[1152,128]{1,0:T(8,128)(2,1)S(1)}, bf16[1152,128]{1,0:T(8,128)(2,1)S(1)}, u32[]{:S(2)}, u32[]{:S(2)}) collective-permute-start(bf16[1152,128]{1,0:T(8,128)(2,1)S(1)} %get-tuple-element.16), channel_id=1, source_target_pairs={{0,8},{8,0},{16,24},{24,16},{1,9},{9,1},{17,25},{25,17},{2,10},{10... | collective-permute-start | bytes 884744 | tf_op jit(solution)/shard_map/ppermute | solution.py:379
  27.3 3.4 %collective-permute-done.4 = bf16[496,128]{1,0:T(8,128)(2,1)S(1)} collective-permute-done((bf16[496,128]{1,0:T(8,128)(2,1)}, bf16[496,128]{1,0:T(8,128)(2,1)S(1)}, u32[]{:S(2)}, u32[]{:S(2)}) %collective-permute-start.4) | collective-permute-done | bytes 127008 | tf_op jit(solution)/shard_map/ppermute | solution.py:382
  30.7 0.6 %collective-permute-start.6 = (bf16[448,128]{1,0:T(8,128)(2,1)S(1)}, bf16[448,128]{1,0:T(8,128)(2,1)S(1)}, u32[]{:S(2)}, u32[]{:S(2)}) collective-permute-start(bf16[448,128]{1,0:T(8,128)(2,1)S(1)} %pad_maximum_fusion.1.mine_ref), channel_id=1, source_target_pairs={{0,1},{1,0},{2,3},{3,2},{4,5},{5,4},{6,7},{7,6},{8,9},{9,8},{10,11... | collective-permute-start | bytes 344072 | tf_op jit(solution)/shard_map/ppermute | solution.py:382
  31.4 1.2 %collective-permute-done.6.sib_ref = bf16[448,128]{1,0:T(8,128)(2,1)S(1)} collective-permute-done((bf16[448,128]{1,0:T(8,128)(2,1)S(1)}, bf16[448,128]{1,0:T(8,128)(2,1)S(1)}, u32[]{:S(2)}, u32[]{:S(2)}) %collective-permute-start.6) | collective-permute-done | bytes 114720 | tf_op jit(solution)/shard_map/ppermute | solution.py:382
  32.7 0.5 %copy-done.4 = bf16[448,128]{1,0:T(8,128)(2,1)} copy-done((bf16[448,128]{1,0:T(8,128)(2,1)}, bf16[448,128]{1,0:T(8,128)(2,1)S(1)}, u32[]{:S(2)}) %copy-start.4) | copy-done | bytes 114712
  33.2 6.7 %first_tile.1.first_hbm = bf16[912,256]{1,0:T(8,128)(2,1)} custom-call(f32[6,128]{1,0:T(8,128)} %bitcast.3, bf16[448,128]{1,0:T(8,128)(2,1)} %copy-done.3, bf16[448,128]{1,0:T(8,128)(2,1)} %copy-done.4), custom_call_target="tpu_custom_call" | custom-call | tf_op jit(solution)/shard_map/first_tile/pallas_call | solution.py:202
  40.2 0.4 collective-permute-start.15
  40.6 1.2 %collective-permute-done.15.refs_6_ = bf16[384,128]{1,0:T(8,128)(2,1)S(1)} collective-permute-done((bf16[384,128]{1,0:T(8,128)(2,1)S(1)}, bf16[384,128]{1,0:T(8,128)(2,1)S(1)}, u32[]{:S(2)}, u32[]{:S(2)}) %collective-permute-start.15) | collective-permute-done | bytes 98336 | tf_op jit(solution)/shard_map/ppermute | solution.py:382
  41.8 6.3 %rest.1 = (f32[8,128,128]{2,1,0:T(8,128)}, f32[4096,128]{1,0:T(8,128)}) custom-call(f32[6,128]{1,0:T(8,128)S(1)} %bitcast.4, f32[8,128]{1,0:T(8,128)S(1)} %copy-done.2, bf16[912,256]{1,0:T(8,128)(2,1)S(1)} %copy-done, bf16[1536,128]{1,0:T(8,128)(2,1)S(1)} %get-tuple-element.29.refs_0_, bf16[1536,128]{1,0:T(8,128)(2,1)S(1)} %collective-permute-done.10.refs_1_, ...), custom_call_target="tpu_custom_call" | custom-call | tf_op jit(solution)/shard_map/rest/pallas_call | solution.py:351
  (41 shorter events, 1.1 us)
Async XLA Ops:
  2.4 28.9 %copy-start.5 = (bf16[384,128]{1,0:T(8,128)(2,1)S(1)}, bf16[384,128]{1,0:T(8,128)(2,1)}, u32[]{:S(2)}) copy-start(bf16[384,128]{1,0:T(8,128)(2,1)} %get-tuple-element.15) | copy-start | bytes 294916
  2.4 12.5 %collective-permute-start.2 = (bf16[496,128]{1,0:T(8,128)(2,1)}, bf16[496,128]{1,0:T(8,128)(2,1)S(1)}, u32[]{:S(2)}, u32[]{:S(2)}) collective-permute-start(bf16[496,128]{1,0:T(8,128)(2,1)} %get-tuple-element.12), channel_id=1, source_target_pairs={{0,24},{8,16},{16,8},{24,0},{1,25},{9,17},{17,9},{25,1},{2,26},{10... | collective-permute-start | bytes 380936 | tf_op jit(solution)/shard_map/ppermute | solution.py:379
  6.3 8.6 %collective-permute-start.1 = (bf16[496,128]{1,0:T(8,128)(2,1)}, bf16[496,128]{1,0:T(8,128)(2,1)S(1)}, u32[]{:S(2)}, u32[]{:S(2)}) collective-permute-start(bf16[496,128]{1,0:T(8,128)(2,1)} %get-tuple-element.12), channel_id=1, source_target_pairs={{0,16},{8,24},{16,0},{24,8},{1,17},{9,25},{17,1},{25,9},{2,18},{10... | collective-permute-start | bytes 380936 | tf_op jit(solution)/shard_map/ppermute | solution.py:379
  6.8 8.2 %collective-permute-start = (bf16[496,128]{1,0:T(8,128)(2,1)}, bf16[496,128]{1,0:T(8,128)(2,1)S(1)}, u32[]{:S(2)}, u32[]{:S(2)}) collective-permute-start(bf16[496,128]{1,0:T(8,128)(2,1)} %get-tuple-element.12), channel_id=1, source_target_pairs={{0,8},{8,0},{16,24},{24,16},{1,9},{9,1},{17,25},{25,17},{2,10},{10... | collective-permute-start | bytes 380936 | tf_op jit(solution)/shard_map/ppermute | solution.py:379
  6.9 5.4 %collective-permute-start.7 = (bf16[384,128]{1,0:T(8,128)(2,1)}, bf16[384,128]{1,0:T(8,128)(2,1)S(1)}, u32[]{:S(2)}, u32[]{:S(2)}) collective-permute-start(bf16[384,128]{1,0:T(8,128)(2,1)} %get-tuple-element.14), channel_id=1, source_target_pairs={{0,2},{1,3},{2,0},{3,1},{4,6},{5,7},{6,4},{7,5},{8,10},{9,11},{10,... | collective-permute-start | bytes 294920 | tf_op jit(solution)/shard_map/ppermute | solution.py:382
  8.9 13.4 %collective-permute-start.9 = (bf16[384,128]{1,0:T(8,128)(2,1)}, bf16[384,128]{1,0:T(8,128)(2,1)S(1)}, u32[]{:S(2)}, u32[]{:S(2)}) collective-permute-start(bf16[384,128]{1,0:T(8,128)(2,1)} %get-tuple-element.15), channel_id=1, source_target_pairs={{0,6},{1,7},{2,4},{3,5},{4,2},{5,3},{6,0},{7,1},{8,14},{9,15},{10,... | collective-permute-start | bytes 294920 | tf_op jit(solution)/shard_map/ppermute | solution.py:382
  12.3 10.0 %collective-permute-start.8 = (bf16[384,128]{1,0:T(8,128)(2,1)}, bf16[384,128]{1,0:T(8,128)(2,1)S(1)}, u32[]{:S(2)}, u32[]{:S(2)}) collective-permute-start(bf16[384,128]{1,0:T(8,128)(2,1)} %get-tuple-element.15), channel_id=1, source_target_pairs={{0,4},{1,5},{2,6},{3,7},{4,0},{5,1},{6,2},{7,3},{8,12},{9,13},{10,... | collective-permute-start | bytes 294920 | tf_op jit(solution)/shard_map/ppermute | solution.py:382
  17.9 7.9 %collective-permute-start.5 = (bf16[496,128]{1,0:T(8,128)(2,1)}, bf16[496,128]{1,0:T(8,128)(2,1)S(1)}, u32[]{:S(2)}, u32[]{:S(2)}) collective-permute-start(bf16[496,128]{1,0:T(8,128)(2,1)} %constant_dynamic-update-slice_fusion.7), channel_id=1, source_target_pairs={{0,6},{1,7},{2,4},{3,5},{4,2},{5,3},{6,0},{7,1},{8,14},{9,15},{10,... | collective-permute-start | bytes 380936 | tf_op jit(solution)/shard_map/ppermute | solution.py:382
  19.9 10.7 %collective-permute-start.4 = (bf16[496,128]{1,0:T(8,128)(2,1)}, bf16[496,128]{1,0:T(8,128)(2,1)S(1)}, u32[]{:S(2)}, u32[]{:S(2)}) collective-permute-start(bf16[496,128]{1,0:T(8,128)(2,1)} %constant_dynamic-update-slice_fusion.7), channel_id=1, source_target_pairs={{0,4},{1,5},{2,6},{3,7},{4,0},{5,1},{6,2},{7,3},{8,12},{9,13},{10,... | collective-permute-start | bytes 380936 | tf_op jit(solution)/shard_map/ppermute | solution.py:382
  21.9 8.8 %collective-permute-start.3 = (bf16[496,128]{1,0:T(8,128)(2,1)}, bf16[496,128]{1,0:T(8,128)(2,1)S(1)}, u32[]{:S(2)}, u32[]{:S(2)}) collective-permute-start(bf16[496,128]{1,0:T(8,128)(2,1)} %get-tuple-element.22), channel_id=1, source_target_pairs={{0,2},{1,3},{2,0},{3,1},{4,6},{5,7},{6,4},{7,5},{8,10},{9,11},{10,... | collective-permute-start | bytes 380936 | tf_op jit(solution)/shard_map/ppermute | solution.py:382
  22.4 17.5 %collective-permute-start.14 = (bf16[1152,128]{1,0:T(8,128)(2,1)S(1)}, bf16[1152,128]{1,0:T(8,128)(2,1)S(1)}, u32[]{:S(2)}, u32[]{:S(2)}) collective-permute-start(bf16[1152,128]{1,0:T(8,128)(2,1)S(1)} %get-tuple-element.16), channel_id=1, source_target_pairs={{0,24},{8,16},{16,8},{24,0},{1,25},{9,17},{17,9},{25,1},{2,26},{10... | collective-permute-start | bytes 884744 | tf_op jit(solution)/shard_map/ppermute | solution.py:379
  24.9 15.0 %collective-permute-start.13 = (bf16[1152,128]{1,0:T(8,128)(2,1)S(1)}, bf16[1152,128]{1,0:T(8,128)(2,1)S(1)}, u32[]{:S(2)}, u32[]{:S(2)}) collective-permute-start(bf16[1152,128]{1,0:T(8,128)(2,1)S(1)} %get-tuple-element.16), channel_id=1, source_target_pairs={{0,16},{8,24},{16,0},{24,8},{1,17},{9,25},{17,1},{25,9},{2,18},{10... | collective-permute-start | bytes 884744 | tf_op jit(solution)/shard_map/ppermute | solution.py:379
  25.8 14.1 %collective-permute-start.12 = (bf16[1152,128]{1,0:T(8,128)(2,1)S(1)}, bf16[1152,128]{1,0:T(8,128)(2,1)S(1)}, u32[]{:S(2)}, u32[]{:S(2)}) collective-permute-start(bf16[1152,128]{1,0:T(8,128)(2,1)S(1)} %get-tuple-element.16), channel_id=1, source_target_pairs={{0,8},{8,0},{16,24},{24,16},{1,9},{9,1},{17,25},{25,17},{2,10},{10... | collective-permute-start | bytes 884744 | tf_op jit(solution)/shard_map/ppermute | solution.py:379
  30.7 11.1 %copy-start.1 = (f32[768]{0:T(1024)S(1)}, f32[768]{0:T(1024)}, u32[]{:S(2)}) copy-start(f32[768]{0:T(1024)} %param.4) | copy-start | bytes 9220
  30.7 11.2 %copy-start.2 = (f32[8,128]{1,0:T(8,128)S(1)}, f32[8,128]{1,0:T(8,128)}, u32[]{:S(2)}) copy-start(f32[8,128]{1,0:T(8,128)} %noise_ref.3) | copy-start | bytes 12292
  30.7 11.1 %collective-permute-start.10 = (bf16[1536,128]{1,0:T(8,128)(2,1)S(1)}, bf16[1536,128]{1,0:T(8,128)(2,1)S(1)}, u32[]{:S(2)}, u32[]{:S(2)}) collective-permute-start(bf16[1536,128]{1,0:T(8,128)(2,1)S(1)} %get-tuple-element.29.refs_0_), channel_id=1, source_target_pairs={{0,1},{1,0},{2,3},{3,2},{4,5},{5,4},{6,7},{7,6},{8,9},{9,8},{10,11... | collective-permute-start | bytes 1179656 | tf_op jit(solution)/shard_map/ppermute | solution.py:382
  30.7 2.0 %copy-start.3 = (bf16[448,128]{1,0:T(8,128)(2,1)}, bf16[448,128]{1,0:T(8,128)(2,1)S(1)}, u32[]{:S(2)}) copy-start(bf16[448,128]{1,0:T(8,128)(2,1)S(1)} %pad_maximum_fusion.1.mine_ref) | copy-start | bytes 344068
  30.7 1.8 %collective-permute-start.6 = (bf16[448,128]{1,0:T(8,128)(2,1)S(1)}, bf16[448,128]{1,0:T(8,128)(2,1)S(1)}, u32[]{:S(2)}, u32[]{:S(2)}) collective-permute-start(bf16[448,128]{1,0:T(8,128)(2,1)S(1)} %pad_maximum_fusion.1.mine_ref), channel_id=1, source_target_pairs={{0,1},{1,0},{2,3},{3,2},{4,5},{5,4},{6,7},{7,6},{8,9},{9,8},{10,11... | collective-permute-start | bytes 344072 | tf_op jit(solution)/shard_map/ppermute | solution.py:382
  32.6 0.6 %copy-start.4 = (bf16[448,128]{1,0:T(8,128)(2,1)}, bf16[448,128]{1,0:T(8,128)(2,1)S(1)}, u32[]{:S(2)}) copy-start(bf16[448,128]{1,0:T(8,128)(2,1)S(1)} %collective-permute-done.6.sib_ref) | copy-start | bytes 344068
  32.6 9.2 %collective-permute-start.11 = (bf16[1536,128]{1,0:T(8,128)(2,1)S(1)}, bf16[1536,128]{1,0:T(8,128)(2,1)S(1)}, u32[]{:S(2)}, u32[]{:S(2)}) collective-permute-start(bf16[1536,128]{1,0:T(8,128)(2,1)S(1)} %pad_maximum_fusion.refs_2_), channel_id=1, source_target_pairs={{0,1},{1,0},{2,3},{3,2},{4,5},{5,4},{6,7},{7,6},{8,9},{9,8},{10,11... | collective-permute-start | bytes 1179656 | tf_op jit(solution)/shard_map/ppermute | solution.py:382
  39.9 1.9 %copy-start = (bf16[912,256]{1,0:T(8,128)(2,1)S(1)}, bf16[912,256]{1,0:T(8,128)(2,1)}, u32[]{:S(2)}) copy-start(bf16[912,256]{1,0:T(8,128)(2,1)} %first_tile.1.first_hbm) | copy-start | bytes 1400836
  40.0 1.8 %collective-permute-start.16 = (bf16[1152,128]{1,0:T(8,128)(2,1)S(1)}, bf16[1152,128]{1,0:T(8,128)(2,1)S(1)}, u32[]{:S(2)}, u32[]{:S(2)}) collective-permute-start(bf16[1152,128]{1,0:T(8,128)(2,1)S(1)} %get-tuple-element.24), channel_id=1, source_target_pairs={{0,1},{1,0},{2,3},{3,2},{4,5},{5,4},{6,7},{7,6},{8,9},{9,8},{10,11... | collective-permute-start | bytes 884744 | tf_op jit(solution)/shard_map/ppermute | solution.py:382
  40.2 1.6 %collective-permute-start.15 = (bf16[384,128]{1,0:T(8,128)(2,1)S(1)}, bf16[384,128]{1,0:T(8,128)(2,1)S(1)}, u32[]{:S(2)}, u32[]{:S(2)}) collective-permute-start(bf16[384,128]{1,0:T(8,128)(2,1)S(1)} %get-tuple-element.26), channel_id=1, source_target_pairs={{0,1},{1,0},{2,3},{3,2},{4,5},{5,4},{6,7},{7,6},{8,9},{9,8},{10,11... | collective-permute-start | bytes 294920 | tf_op jit(solution)/shard_map/ppermute | solution.py:382

commit v7 on v6

--- a/solution.py
+++ b/solution.py
@@ -162,13 +162,21 @@
     return jnp.concatenate(blocks, axis=0)
 
 
-def first_kernel(length_ref, mine_ref, sib_ref, out_ref, work):
+def first_kernel(length_ref, mine_hbm, sib_hbm, out_ref, work, mine_ref, sib_ref, sems):
+    copies = [
+        pltpu.make_async_copy(mine_hbm, mine_ref, sems.at[0]),
+        pltpu.make_async_copy(sib_hbm, sib_ref, sems.at[1]),
+    ]
+    for copy in copies:
+        copy.start()
     width = work.shape[0]
     each = mine_ref.shape[0] // 4
     depth = each - 16
     starts = range(0, 4 * each, each)
+    w = jnp.concatenate(slice_weights(length_ref, depth), axis=0)
+    for copy in copies:
+        copy.wait()
     x = jnp.concatenate([ref[k : k + depth, :] for ref in (mine_ref, sib_ref) for k in starts], axis=0)
-    w = jnp.concatenate(slice_weights(length_ref, depth), axis=0)
     xf = x.astype(jnp.float32)
     xw = xf * w
     parts = split3(xw)
@@ -202,9 +210,14 @@
     return pl.pallas_call(
         first_kernel,
         out_shape=jax.ShapeDtypeStruct((whole + width + 16, 2 * width), jnp.bfloat16),
-        in_specs=[VM] * 3,
+        in_specs=[VM] + [ANY] * 2,
         out_specs=VM,
-        scratch_shapes=[pltpu.VMEM((width, width), jnp.float32)],
+        scratch_shapes=[
+            pltpu.VMEM((width, width), jnp.float32),
+            pltpu.VMEM(mine.shape, mine.dtype),
+            pltpu.VMEM(sib.shape, sib.dtype),
+            pltpu.SemaphoreType.DMA((2,)),
+        ],
         name="first_tile",
     )(lengths, mine, sib)
 

time: 48.4 us -> 48.4 us (level)
  no operation moved by 1% of the time
where the time goes in v7:
time: 48.4 us; the launch traced here: 48 us
  starting transfers between devices  21.8 us (45%)
  Pallas kernels  14.7 us (30%)
  waiting for transfers between devices  6.18 us (13%)
  other arithmetic  2.44 us (5%)
  local copies, waits for them, and re-layouts  2.17 us (4%)
  between operations  0.83 us (2%)
    ppermute x11, starting transfers between devices, over_col(): return lax.ppermute(x, 'col', [(i, i ^ k) for i in range(n_cols)])  12.7 us
    ppermute x6, starting transfers between devices, over_row(): return lax.ppermute(x, 'row', [(i, i ^ k) for i in range(n_rows)])  9.02 us
    pallas_call x1, Pallas kernels, first_tile(): pl.pallas_call(first_kernel, out_shape=jax.ShapeDtypeStruct((whole + widt...  6.61 us
    pallas_call x1, Pallas kernels, rest(): pl.pallas_call(functools.partial(rest_kernel, depth), out_shape=(jax.Shap...  6.26 us
    ppermute x11, waiting for transfers between devices, over_col(): return lax.ppermute(x, 'col', [(i, i ^ k) for i in range(n_cols)])  6.17 us
    pallas_call x1, Pallas kernels, pack(): pl.pallas_call(pack_kernel, out_shape=(rows(3 * width), rows(3 * width),...  1.79 us
    unnamed x15, local copies, waits for them, and re-layouts  1.49 us
    dynamic_update_slice x1, other arithmetic, body(): q1 = over_col(lax.dynamic_update_slice(oth_long, head, (size, 0)), 2)  1.38 us
  transfers between devices with their start and end apart: 17, of which 4 were waited for; matrix products, arithmetic and copies ran while one was open for 8% of the time, Pallas kernels for 14%

profile of v7, /device:TPU:0, one launch (start us, length us, event | category | flops | bytes accessed | tf_op | source)
XLA Modules:
  0.0 48.0 jit_solution(17589379193287105670)
XLA Ops:
  0.6 1.8 %pack.1 = (bf16[384,128]{1,0:T(8,128)(2,1)}, bf16[384,128]{1,0:T(8,128)(2,1)}, bf16[496,128]{1,0:T(8,128)(2,1)}, bf16[496,128]{1,0:T(8,128)(2,1)}) custom-call(bf16[8,96,128]{2,1,0:T(8,128)(2,1)} %bitcast.5, f32[8,128]{1,0:T(8,128)} %noise_ref.3), custom_call_target="tpu_custom_call" | custom-call | tf_op jit(solution)/shard_map/pack/pallas_call | solution.py:56
  2.4 3.9 %collective-permute-start.2 = (bf16[496,128]{1,0:T(8,128)(2,1)}, bf16[496,128]{1,0:T(8,128)(2,1)S(1)}, u32[]{:S(2)}, u32[]{:S(2)}) collective-permute-start(bf16[496,128]{1,0:T(8,128)(2,1)} %get-tuple-element.12), channel_id=1, source_target_pairs={{0,24},{8,16},{16,8},{24,0},{1,25},{9,17},{17,9},{25,1},{2,26},{10... | collective-permute-start | bytes 380936 | tf_op jit(solution)/shard_map/ppermute | solution.py:392
  6.3 0.5 %collective-permute-start.1 = (bf16[496,128]{1,0:T(8,128)(2,1)}, bf16[496,128]{1,0:T(8,128)(2,1)S(1)}, u32[]{:S(2)}, u32[]{:S(2)}) collective-permute-start(bf16[496,128]{1,0:T(8,128)(2,1)} %get-tuple-element.12), channel_id=1, source_target_pairs={{0,16},{8,24},{16,0},{24,8},{1,17},{9,25},{17,1},{25,9},{2,18},{10... | collective-permute-start | bytes 380936 | tf_op jit(solution)/shard_map/ppermute | solution.py:392
  6.9 2.0 %collective-permute-start.7 = (bf16[384,128]{1,0:T(8,128)(2,1)}, bf16[384,128]{1,0:T(8,128)(2,1)S(1)}, u32[]{:S(2)}, u32[]{:S(2)}) collective-permute-start(bf16[384,128]{1,0:T(8,128)(2,1)} %get-tuple-element.14), channel_id=1, source_target_pairs={{0,2},{1,3},{2,0},{3,1},{4,6},{5,7},{6,4},{7,5},{8,10},{9,11},{10,... | collective-permute-start | bytes 294920 | tf_op jit(solution)/shard_map/ppermute | solution.py:395
  8.9 2.5 %collective-permute-start.9 = (bf16[384,128]{1,0:T(8,128)(2,1)}, bf16[384,128]{1,0:T(8,128)(2,1)S(1)}, u32[]{:S(2)}, u32[]{:S(2)}) collective-permute-start(bf16[384,128]{1,0:T(8,128)(2,1)} %get-tuple-element.15), channel_id=1, source_target_pairs={{0,6},{1,7},{2,4},{3,5},{4,2},{5,3},{6,0},{7,1},{8,14},{9,15},{10,... | collective-permute-start | bytes 294920 | tf_op jit(solution)/shard_map/ppermute | solution.py:395
  11.4 0.9 %constant_dynamic-update-slice_fusion.3 = bf16[1536,128]{1,0:T(8,128)(2,1)S(1)} fusion(bf16[384,128]{1,0:T(8,128)(2,1)} %get-tuple-element.14), kind=kLoop, calls=%fused_computation.12 | loop fusion | bytes 196608
  12.3 2.6 %collective-permute-start.8 = (bf16[384,128]{1,0:T(8,128)(2,1)}, bf16[384,128]{1,0:T(8,128)(2,1)S(1)}, u32[]{:S(2)}, u32[]{:S(2)}) collective-permute-start(bf16[384,128]{1,0:T(8,128)(2,1)} %get-tuple-element.15), channel_id=1, source_target_pairs={{0,4},{1,5},{2,6},{3,7},{4,0},{5,1},{6,2},{7,3},{8,12},{9,13},{10,... | collective-permute-start | bytes 294920 | tf_op jit(solution)/shard_map/ppermute | solution.py:395
  15.0 1.4 %constant_dynamic-update-slice_fusion.8 = (bf16[496,128]{1,0:T(8,128)(2,1)}, bf16[112,128]{1,0:T(8,128)(2,1)S(1)}) fusion(bf16[496,128]{1,0:T(8,128)(2,1)} %get-tuple-element.13, bf16[496,128]{1,0:T(8,128)(2,1)S(1)} %collective-permute-done.2, bf16[496,128]{1,0:T(8,128)(2,1)S(1)} %collective-permute-done.1, pred[]{:T(512)S(6)} %select_n.135, ...), kind=kLoop, calls=%fused_computation.17 | loop fusion | flops 43008 | bytes 172035 | tf_op jit(solution)/shard_map/dynamic_update_slice | solution.py:408
  16.4 0.9 %select_select_fusion.2 = (bf16[384,128]{1,0:T(8,128)(2,1)S(1)}, bf16[384,128]{1,0:T(8,128)(2,1)S(1)}) fusion(pred[]{:T(512)S(6)} %select_n.160, pred[]{:T(512)S(6)} %select_n.157, pred[]{:T(512)S(6)} %select_n.155, bf16[496,128]{1,0:T(8,128)(2,1)S(1)} %collective-permute-done.2, bf16[496,128]{1,0:T(8,128)(2,1)S(1)} %collective-permute-done.1, ...), kind=kLoop, calls=%fused_computation.4 | loop fusion | flops 294912 | bytes 589830 | tf_op jit(solution)/shard_map/select_n | solution.py:421
  17.3 0.6 %constant_dynamic-update-slice_fusion.7 = bf16[496,128]{1,0:T(8,128)(2,1)} fusion(bf16[496,128]{1,0:T(8,128)(2,1)} %get-tuple-element.12, bf16[112,128]{1,0:T(8,128)(2,1)S(1)} %get-tuple-element.23), kind=kLoop, calls=%fused_computation.16 | loop fusion | bytes 57344 | tf_op jit(solution)/shard_map/dynamic_update_slice | solution.py:409
  17.9 2.0 %collective-permute-start.5 = (bf16[496,128]{1,0:T(8,128)(2,1)}, bf16[496,128]{1,0:T(8,128)(2,1)S(1)}, u32[]{:S(2)}, u32[]{:S(2)}) collective-permute-start(bf16[496,128]{1,0:T(8,128)(2,1)} %constant_dynamic-update-slice_fusion.7), channel_id=1, source_target_pairs={{0,6},{1,7},{2,4},{3,5},{4,2},{5,3},{6,0},{7,1},{8,14},{9,15},{10,... | collective-permute-start | bytes 380936 | tf_op jit(solution)/shard_map/ppermute | solution.py:395
  19.9 1.9 %collective-permute-start.4 = (bf16[496,128]{1,0:T(8,128)(2,1)}, bf16[496,128]{1,0:T(8,128)(2,1)S(1)}, u32[]{:S(2)}, u32[]{:S(2)}) collective-permute-start(bf16[496,128]{1,0:T(8,128)(2,1)} %constant_dynamic-update-slice_fusion.7), channel_id=1, source_target_pairs={{0,4},{1,5},{2,6},{3,7},{4,0},{5,1},{6,2},{7,3},{8,12},{9,13},{10,... | collective-permute-start | bytes 380936 | tf_op jit(solution)/shard_map/ppermute | solution.py:395
  21.9 0.4 collective-permute-start.3
  22.4 2.5 %collective-permute-start.14 = (bf16[1152,128]{1,0:T(8,128)(2,1)S(1)}, bf16[1152,128]{1,0:T(8,128)(2,1)S(1)}, u32[]{:S(2)}, u32[]{:S(2)}) collective-permute-start(bf16[1152,128]{1,0:T(8,128)(2,1)S(1)} %get-tuple-element.16), channel_id=1, source_target_pairs={{0,24},{8,16},{16,8},{24,0},{1,25},{9,17},{17,9},{25,1},{2,26},{10... | collective-permute-start | bytes 884744 | tf_op jit(solution)/shard_map/ppermute | solution.py:392
  24.9 0.5 %collective-permute-start.13 = (bf16[1152,128]{1,0:T(8,128)(2,1)S(1)}, bf16[1152,128]{1,0:T(8,128)(2,1)S(1)}, u32[]{:S(2)}, u32[]{:S(2)}) collective-permute-start(bf16[1152,128]{1,0:T(8,128)(2,1)S(1)} %get-tuple-element.16), channel_id=1, source_target_pairs={{0,16},{8,24},{16,0},{24,8},{1,17},{9,25},{17,1},{25,9},{2,18},{10... | collective-permute-start | bytes 884744 | tf_op jit(solution)/shard_map/ppermute | solution.py:392
  25.8 1.5 %collective-permute-start.12 = (bf16[1152,128]{1,0:T(8,128)(2,1)S(1)}, bf16[1152,128]{1,0:T(8,128)(2,1)S(1)}, u32[]{:S(2)}, u32[]{:S(2)}) collective-permute-start(bf16[1152,128]{1,0:T(8,128)(2,1)S(1)} %get-tuple-element.16), channel_id=1, source_target_pairs={{0,8},{8,0},{16,24},{24,16},{1,9},{9,1},{17,25},{25,17},{2,10},{10... | collective-permute-start | bytes 884744 | tf_op jit(solution)/shard_map/ppermute | solution.py:392
  27.3 3.4 %collective-permute-done.4 = bf16[496,128]{1,0:T(8,128)(2,1)S(1)} collective-permute-done((bf16[496,128]{1,0:T(8,128)(2,1)}, bf16[496,128]{1,0:T(8,128)(2,1)S(1)}, u32[]{:S(2)}, u32[]{:S(2)}) %collective-permute-start.4) | collective-permute-done | bytes 127008 | tf_op jit(solution)/shard_map/ppermute | solution.py:395
  30.7 0.6 %collective-permute-start.6 = (bf16[448,128]{1,0:T(8,128)(2,1)S(1)}, bf16[448,128]{1,0:T(8,128)(2,1)S(1)}, u32[]{:S(2)}, u32[]{:S(2)}) collective-permute-start(bf16[448,128]{1,0:T(8,128)(2,1)S(1)} %pad_maximum_fusion.1.mine_hbm), channel_id=1, source_target_pairs={{0,1},{1,0},{2,3},{3,2},{4,5},{5,4},{6,7},{7,6},{8,9},{9,8},{10,11... | collective-permute-start | bytes 344072 | tf_op jit(solution)/shard_map/ppermute | solution.py:395
  31.4 1.2 %collective-permute-done.6.sib_hbm = bf16[448,128]{1,0:T(8,128)(2,1)S(1)} collective-permute-done((bf16[448,128]{1,0:T(8,128)(2,1)S(1)}, bf16[448,128]{1,0:T(8,128)(2,1)S(1)}, u32[]{:S(2)}, u32[]{:S(2)}) %collective-permute-start.6) | collective-permute-done | bytes 114720 | tf_op jit(solution)/shard_map/ppermute | solution.py:395
  32.7 0.5 %copy-done.4 = bf16[448,128]{1,0:T(8,128)(2,1)} copy-done((bf16[448,128]{1,0:T(8,128)(2,1)}, bf16[448,128]{1,0:T(8,128)(2,1)S(1)}, u32[]{:S(2)}) %copy-start.4) | copy-done | bytes 114712
  33.2 6.6 %first_tile.1.first_hbm = bf16[912,256]{1,0:T(8,128)(2,1)} custom-call(f32[6,128]{1,0:T(8,128)} %bitcast.3, bf16[448,128]{1,0:T(8,128)(2,1)} %copy-done.3, bf16[448,128]{1,0:T(8,128)(2,1)} %copy-done.4), custom_call_target="tpu_custom_call" | custom-call | tf_op jit(solution)/shard_map/first_tile/pallas_call | solution.py:210
  40.2 0.4 collective-permute-start.15
  40.5 1.2 %collective-permute-done.15.refs_6_ = bf16[384,128]{1,0:T(8,128)(2,1)S(1)} collective-permute-done((bf16[384,128]{1,0:T(8,128)(2,1)S(1)}, bf16[384,128]{1,0:T(8,128)(2,1)S(1)}, u32[]{:S(2)}, u32[]{:S(2)}) %collective-permute-start.15) | collective-permute-done | bytes 98336 | tf_op jit(solution)/shard_map/ppermute | solution.py:395
  41.8 6.3 %rest.1 = (f32[8,128,128]{2,1,0:T(8,128)}, f32[4096,128]{1,0:T(8,128)}) custom-call(f32[6,128]{1,0:T(8,128)S(1)} %bitcast.4, f32[8,128]{1,0:T(8,128)S(1)} %copy-done.2, bf16[912,256]{1,0:T(8,128)(2,1)S(1)} %copy-done, bf16[1536,128]{1,0:T(8,128)(2,1)S(1)} %get-tuple-element.29.refs_0_, bf16[1536,128]{1,0:T(8,128)(2,1)S(1)} %collective-permute-done.10.refs_1_, ...), custom_call_target="tpu_custom_call" | custom-call | tf_op jit(solution)/shard_map/rest/pallas_call | solution.py:364
  (41 shorter events, 1.1 us)
Async XLA Ops:
  2.4 28.9 %copy-start.5 = (bf16[384,128]{1,0:T(8,128)(2,1)S(1)}, bf16[384,128]{1,0:T(8,128)(2,1)}, u32[]{:S(2)}) copy-start(bf16[384,128]{1,0:T(8,128)(2,1)} %get-tuple-element.15) | copy-start | bytes 294916
  2.4 12.5 %collective-permute-start.2 = (bf16[496,128]{1,0:T(8,128)(2,1)}, bf16[496,128]{1,0:T(8,128)(2,1)S(1)}, u32[]{:S(2)}, u32[]{:S(2)}) collective-permute-start(bf16[496,128]{1,0:T(8,128)(2,1)} %get-tuple-element.12), channel_id=1, source_target_pairs={{0,24},{8,16},{16,8},{24,0},{1,25},{9,17},{17,9},{25,1},{2,26},{10... | collective-permute-start | bytes 380936 | tf_op jit(solution)/shard_map/ppermute | solution.py:392
  6.3 8.6 %collective-permute-start.1 = (bf16[496,128]{1,0:T(8,128)(2,1)}, bf16[496,128]{1,0:T(8,128)(2,1)S(1)}, u32[]{:S(2)}, u32[]{:S(2)}) collective-permute-start(bf16[496,128]{1,0:T(8,128)(2,1)} %get-tuple-element.12), channel_id=1, source_target_pairs={{0,16},{8,24},{16,0},{24,8},{1,17},{9,25},{17,1},{25,9},{2,18},{10... | collective-permute-start | bytes 380936 | tf_op jit(solution)/shard_map/ppermute | solution.py:392
  6.8 8.2 %collective-permute-start = (bf16[496,128]{1,0:T(8,128)(2,1)}, bf16[496,128]{1,0:T(8,128)(2,1)S(1)}, u32[]{:S(2)}, u32[]{:S(2)}) collective-permute-start(bf16[496,128]{1,0:T(8,128)(2,1)} %get-tuple-element.12), channel_id=1, source_target_pairs={{0,8},{8,0},{16,24},{24,16},{1,9},{9,1},{17,25},{25,17},{2,10},{10... | collective-permute-start | bytes 380936 | tf_op jit(solution)/shard_map/ppermute | solution.py:392
  6.9 5.4 %collective-permute-start.7 = (bf16[384,128]{1,0:T(8,128)(2,1)}, bf16[384,128]{1,0:T(8,128)(2,1)S(1)}, u32[]{:S(2)}, u32[]{:S(2)}) collective-permute-start(bf16[384,128]{1,0:T(8,128)(2,1)} %get-tuple-element.14), channel_id=1, source_target_pairs={{0,2},{1,3},{2,0},{3,1},{4,6},{5,7},{6,4},{7,5},{8,10},{9,11},{10,... | collective-permute-start | bytes 294920 | tf_op jit(solution)/shard_map/ppermute | solution.py:395
  8.9 13.4 %collective-permute-start.9 = (bf16[384,128]{1,0:T(8,128)(2,1)}, bf16[384,128]{1,0:T(8,128)(2,1)S(1)}, u32[]{:S(2)}, u32[]{:S(2)}) collective-permute-start(bf16[384,128]{1,0:T(8,128)(2,1)} %get-tuple-element.15), channel_id=1, source_target_pairs={{0,6},{1,7},{2,4},{3,5},{4,2},{5,3},{6,0},{7,1},{8,14},{9,15},{10,... | collective-permute-start | bytes 294920 | tf_op jit(solution)/shard_map/ppermute | solution.py:395
  12.3 10.0 %collective-permute-start.8 = (bf16[384,128]{1,0:T(8,128)(2,1)}, bf16[384,128]{1,0:T(8,128)(2,1)S(1)}, u32[]{:S(2)}, u32[]{:S(2)}) collective-permute-start(bf16[384,128]{1,0:T(8,128)(2,1)} %get-tuple-element.15), channel_id=1, source_target_pairs={{0,4},{1,5},{2,6},{3,7},{4,0},{5,1},{6,2},{7,3},{8,12},{9,13},{10,... | collective-permute-start | bytes 294920 | tf_op jit(solution)/shard_map/ppermute | solution.py:395
  17.9 7.9 %collective-permute-start.5 = (bf16[496,128]{1,0:T(8,128)(2,1)}, bf16[496,128]{1,0:T(8,128)(2,1)S(1)}, u32[]{:S(2)}, u32[]{:S(2)}) collective-permute-start(bf16[496,128]{1,0:T(8,128)(2,1)} %constant_dynamic-update-slice_fusion.7), channel_id=1, source_target_pairs={{0,6},{1,7},{2,4},{3,5},{4,2},{5,3},{6,0},{7,1},{8,14},{9,15},{10,... | collective-permute-start | bytes 380936 | tf_op jit(solution)/shard_map/ppermute | solution.py:395
  19.9 10.7 %collective-permute-start.4 = (bf16[496,128]{1,0:T(8,128)(2,1)}, bf16[496,128]{1,0:T(8,128)(2,1)S(1)}, u32[]{:S(2)}, u32[]{:S(2)}) collective-permute-start(bf16[496,128]{1,0:T(8,128)(2,1)} %constant_dynamic-update-slice_fusion.7), channel_id=1, source_target_pairs={{0,4},{1,5},{2,6},{3,7},{4,0},{5,1},{6,2},{7,3},{8,12},{9,13},{10,... | collective-permute-start | bytes 380936 | tf_op jit(solution)/shard_map/ppermute | solution.py:395
  21.9 8.8 %collective-permute-start.3 = (bf16[496,128]{1,0:T(8,128)(2,1)}, bf16[496,128]{1,0:T(8,128)(2,1)S(1)}, u32[]{:S(2)}, u32[]{:S(2)}) collective-permute-start(bf16[496,128]{1,0:T(8,128)(2,1)} %get-tuple-element.22), channel_id=1, source_target_pairs={{0,2},{1,3},{2,0},{3,1},{4,6},{5,7},{6,4},{7,5},{8,10},{9,11},{10,... | collective-permute-start | bytes 380936 | tf_op jit(solution)/shard_map/ppermute | solution.py:395
  22.4 17.4 %collective-permute-start.14 = (bf16[1152,128]{1,0:T(8,128)(2,1)S(1)}, bf16[1152,128]{1,0:T(8,128)(2,1)S(1)}, u32[]{:S(2)}, u32[]{:S(2)}) collective-permute-start(bf16[1152,128]{1,0:T(8,128)(2,1)S(1)} %get-tuple-element.16), channel_id=1, source_target_pairs={{0,24},{8,16},{16,8},{24,0},{1,25},{9,17},{17,9},{25,1},{2,26},{10... | collective-permute-start | bytes 884744 | tf_op jit(solution)/shard_map/ppermute | solution.py:392
  24.9 14.9 %collective-permute-start.13 = (bf16[1152,128]{1,0:T(8,128)(2,1)S(1)}, bf16[1152,128]{1,0:T(8,128)(2,1)S(1)}, u32[]{:S(2)}, u32[]{:S(2)}) collective-permute-start(bf16[1152,128]{1,0:T(8,128)(2,1)S(1)} %get-tuple-element.16), channel_id=1, source_target_pairs={{0,16},{8,24},{16,0},{24,8},{1,17},{9,25},{17,1},{25,9},{2,18},{10... | collective-permute-start | bytes 884744 | tf_op jit(solution)/shard_map/ppermute | solution.py:392
  25.8 14.1 %collective-permute-start.12 = (bf16[1152,128]{1,0:T(8,128)(2,1)S(1)}, bf16[1152,128]{1,0:T(8,128)(2,1)S(1)}, u32[]{:S(2)}, u32[]{:S(2)}) collective-permute-start(bf16[1152,128]{1,0:T(8,128)(2,1)S(1)} %get-tuple-element.16), channel_id=1, source_target_pairs={{0,8},{8,0},{16,24},{24,16},{1,9},{9,1},{17,25},{25,17},{2,10},{10... | collective-permute-start | bytes 884744 | tf_op jit(solution)/shard_map/ppermute | solution.py:392
  30.7 11.1 %copy-start.1 = (f32[768]{0:T(1024)S(1)}, f32[768]{0:T(1024)}, u32[]{:S(2)}) copy-start(f32[768]{0:T(1024)} %param.4) | copy-start | bytes 9220
  30.7 11.1 %copy-start.2 = (f32[8,128]{1,0:T(8,128)S(1)}, f32[8,128]{1,0:T(8,128)}, u32[]{:S(2)}) copy-start(f32[8,128]{1,0:T(8,128)} %noise_ref.3) | copy-start | bytes 12292
  30.7 11.1 %collective-permute-start.10 = (bf16[1536,128]{1,0:T(8,128)(2,1)S(1)}, bf16[1536,128]{1,0:T(8,128)(2,1)S(1)}, u32[]{:S(2)}, u32[]{:S(2)}) collective-permute-start(bf16[1536,128]{1,0:T(8,128)(2,1)S(1)} %get-tuple-element.29.refs_0_), channel_id=1, source_target_pairs={{0,1},{1,0},{2,3},{3,2},{4,5},{5,4},{6,7},{7,6},{8,9},{9,8},{10,11... | collective-permute-start | bytes 1179656 | tf_op jit(solution)/shard_map/ppermute | solution.py:395
  30.7 2.0 %copy-start.3 = (bf16[448,128]{1,0:T(8,128)(2,1)}, bf16[448,128]{1,0:T(8,128)(2,1)S(1)}, u32[]{:S(2)}) copy-start(bf16[448,128]{1,0:T(8,128)(2,1)S(1)} %pad_maximum_fusion.1.mine_hbm) | copy-start | bytes 344068
  30.7 1.8 %collective-permute-start.6 = (bf16[448,128]{1,0:T(8,128)(2,1)S(1)}, bf16[448,128]{1,0:T(8,128)(2,1)S(1)}, u32[]{:S(2)}, u32[]{:S(2)}) collective-permute-start(bf16[448,128]{1,0:T(8,128)(2,1)S(1)} %pad_maximum_fusion.1.mine_hbm), channel_id=1, source_target_pairs={{0,1},{1,0},{2,3},{3,2},{4,5},{5,4},{6,7},{7,6},{8,9},{9,8},{10,11... | collective-permute-start | bytes 344072 | tf_op jit(solution)/shard_map/ppermute | solution.py:395
  32.6 0.6 %copy-start.4 = (bf16[448,128]{1,0:T(8,128)(2,1)}, bf16[448,128]{1,0:T(8,128)(2,1)S(1)}, u32[]{:S(2)}) copy-start(bf16[448,128]{1,0:T(8,128)(2,1)S(1)} %collective-permute-done.6.sib_hbm) | copy-start | bytes 344068
  32.6 9.2 %collective-permute-start.11 = (bf16[1536,128]{1,0:T(8,128)(2,1)S(1)}, bf16[1536,128]{1,0:T(8,128)(2,1)S(1)}, u32[]{:S(2)}, u32[]{:S(2)}) collective-permute-start(bf16[1536,128]{1,0:T(8,128)(2,1)S(1)} %pad_maximum_fusion.refs_2_), channel_id=1, source_target_pairs={{0,1},{1,0},{2,3},{3,2},{4,5},{5,4},{6,7},{7,6},{8,9},{9,8},{10,11... | collective-permute-start | bytes 1179656 | tf_op jit(solution)/shard_map/ppermute | solution.py:395
  39.8 2.0 %copy-start = (bf16[912,256]{1,0:T(8,128)(2,1)S(1)}, bf16[912,256]{1,0:T(8,128)(2,1)}, u32[]{:S(2)}) copy-start(bf16[912,256]{1,0:T(8,128)(2,1)} %first_tile.1.first_hbm) | copy-start | bytes 1400836
  40.0 1.8 %collective-permute-start.16 = (bf16[1152,128]{1,0:T(8,128)(2,1)S(1)}, bf16[1152,128]{1,0:T(8,128)(2,1)S(1)}, u32[]{:S(2)}, u32[]{:S(2)}) collective-permute-start(bf16[1152,128]{1,0:T(8,128)(2,1)S(1)} %get-tuple-element.24), channel_id=1, source_target_pairs={{0,1},{1,0},{2,3},{3,2},{4,5},{5,4},{6,7},{7,6},{8,9},{9,8},{10,11... | collective-permute-start | bytes 884744 | tf_op jit(solution)/shard_map/ppermute | solution.py:395
  40.2 1.6 %collective-permute-start.15 = (bf16[384,128]{1,0:T(8,128)(2,1)S(1)}, bf16[384,128]{1,0:T(8,128)(2,1)S(1)}, u32[]{:S(2)}, u32[]{:S(2)}) collective-permute-start(bf16[384,128]{1,0:T(8,128)(2,1)S(1)} %get-tuple-element.26), channel_id=1, source_target_pairs={{0,1},{1,0},{2,3},{3,2},{4,5},{5,4},{6,7},{7,6},{8,9},{9,8},{10,11... | collective-permute-start | bytes 294920 | tf_op jit(solution)/shard_map/ppermute | solution.py:395
